TPU v7x, 32 devices: a whole 2x2x4 slice. The times are simulated.
32 devices in a mesh: stream: 4 (over y, x), span: 8 (over z, core).
Axes of the slice: x: 2, y: 2, z: 4, core: 2. Of those that a mesh axis runs over, the one named last changes fastest.
Arguments:
- tokens: bfloat16 [4, 2048, 1024], P('stream', 'span'), may hold values from -6 to 6
- cotangent: bfloat16 [4, 2048, 1024], P('stream', 'span'), may hold values from -6 to 6
- doc_stretches: int32 [4, 3], P('stream'), may hold values from 1 to 29, 32 in all within a row
- w_qkv: bfloat16 [1024, 3072], P('span'), may hold values from -0.1875 to 0.1875
- conv_weight: bfloat16 [4, 3072], P(None, 'span'), may hold values from -3 to 3
- w_beta: bfloat16 [1024, 8], P('span'), may hold values from -0.1875 to 0.1875
- beta_bias: float32 [8], replicated, as said below
- norm_attn: bfloat16 [1024], P('span'), may hold values from 0.099609375 to 1.8984375
- norm_head: bfloat16 [128], P('span'), may hold values from 0.099609375 to 1.8984375
- w_out: bfloat16 [1024, 1024], P('span'), may hold values from -0.1875 to 0.1875
- norm_ffn: bfloat16 [1024], P('span'), may hold values from 0.099609375 to 1.8984375
- w_gate: bfloat16 [1024, 2816], P('span'), may hold values from -0.1875 to 0.1875
- w_up: bfloat16 [1024, 2816], P('span'), may hold values from -0.1875 to 0.1875
- w_down: bfloat16 [2816, 1024], P('span'), may hold values from -0.109375 to 0.109375
Outputs:
- out: bfloat16 [4, 2048, 1024], P('stream', 'span')
- grad_tokens: float32 [4, 2048, 1024], P('stream', 'span')
- grad_qkv: float32 [1024, 3072], P('span')
- grad_conv: float32 [4, 3072], P(None, 'span')
- grad_w_beta: float32 [1024, 8], P('span')
- grad_beta_bias: float32 [8], replicated
- grad_norm_attn: float32 [1024], P('span')
- grad_norm_head: float32 [128], P('span')
- grad_out: float32 [1024, 1024], P('span')
- grad_norm_ffn: float32 [1024], P('span')
- grad_gate: float32 [1024, 2816], P('span')
- grad_up: float32 [1024, 2816], P('span')
- grad_down: float32 [2816, 1024], P('span')
Inputs may be any that keep to these rules, and one draw needn't show every extreme that they name: `doc_stretches`: each stream's documents in stretches of 64 tokens, in order; they sum to 32 and one of them has 29 stretches. `beta_bias`: one offset per head.
All inputs are finite; a program needn't handle non-finite values.
Results may differ from a plain program's by a relative error of at most 0.019.
Values may be sent and summed in bfloat16 or wider, within the bound.
A program may use at most 320 MiB of HBM per device.

v0:
```python
import jax
import jax.numpy as jnp
from jax import lax
from jax.sharding import PartitionSpec as P

STRETCH = 64


EPSILON = 1e-06
PRECISE = lax.Precision.HIGHEST


def from_behind(block, axis, distance):
    devices = range(lax.axis_size(axis))
    route = [(i - distance, i) for i in devices if i - distance in devices]
    return lax.ppermute(block, axis, route)


def exact_product(pattern, first_op, second_op):
    return jnp.einsum(
        pattern, first_op, second_op, precision=PRECISE, preferred_element_type=jnp.float32
    )


def bf_product(pattern, first_op, second_op):
    return jnp.einsum(pattern, first_op, second_op, preferred_element_type=jnp.float32)


def compose(earlier, later):
    return (
        exact_product("hab,hbc->hac", earlier[0], later[0]),
        exact_product("hab,hbc->hac", earlier[1], later[0]) + later[1],
    )


def silu_slope(pre_act, sig_value):
    return sig_value * (1.0 + pre_act * (1.0 - sig_value))


def norm_back(grad_in, values, inv_rms, gain_vec):
    scaled = grad_in * gain_vec
    return inv_rms * scaled - values * inv_rms**3 * jnp.mean(scaled * values, -1, keepdims=True)


def unit_back(grad_in, values, inv_norm):
    return inv_norm * grad_in - values * inv_norm**3 * jnp.sum(grad_in * values, -1, keepdims=True)


def retract(grad_state, pieces):
    transition, adjoint_term, carried = pieces
    return (
        carried * (exact_product("hab,hcb->hac", grad_state, transition) + adjoint_term),
        grad_state,
    )


def advance(running, pieces):
    transition, contrib, carried = pieces
    begin_state = running * carried
    return (exact_product("hab,hbc->hac", begin_state, transition) + contrib, begin_state)


def fold_maps(carry_map, map_piece):
    return (compose(carry_map, map_piece), None)


def local(
    tokens,
    cotangent,
    doc_stretches,
    w_qkv,
    conv_weight,
    w_beta,
    beta_bias,
    norm_attn,
    norm_head,
    w_out,
    norm_ffn,
    w_gate,
    w_up,
    w_down,
):
    full_weights = (
        lax.all_gather(w_qkv, "span", axis=0, tiled=True),
        lax.all_gather(conv_weight, "span", axis=1, tiled=True),
        lax.all_gather(w_beta, "span", axis=0, tiled=True),
        lax.all_gather(norm_attn, "span", axis=0, tiled=True),
        lax.all_gather(norm_head, "span", axis=0, tiled=True),
        lax.all_gather(w_out, "span", axis=0, tiled=True),
        lax.all_gather(norm_ffn, "span", axis=0, tiled=True),
        lax.all_gather(w_gate, "span", axis=0, tiled=True),
        lax.all_gather(w_up, "span", axis=0, tiled=True),
        lax.all_gather(w_down, "span", axis=0, tiled=True),
    )
    (
        full_qkv,
        full_conv,
        full_beta,
        gain_attn,
        gain_head,
        full_out,
        gain_ffn,
        full_gate,
        full_up,
        full_down,
    ) = full_weights
    tok_rows = tokens.shape[1]
    model_width = tokens.shape[2]
    head_count = beta_bias.shape[0]
    head_size = model_width // head_count
    stretch_count = tok_rows // STRETCH
    span_count = lax.axis_size("span")
    span_place = lax.axis_index("span")
    taps_count = full_conv.shape[0]
    stretch_ids = span_place * stretch_count + jnp.arange(stretch_count, dtype=jnp.int32)
    doc_lengths = doc_stretches[0]
    doc_begins = jnp.cumsum(doc_lengths) - doc_lengths
    stretch_start = jnp.any(stretch_ids[:, None] == doc_begins[None, :], axis=1).astype(jnp.float32)
    stretch_keep = 1.0 - stretch_start
    token_start = jnp.repeat(stretch_start, STRETCH)
    token_offset = jnp.arange(tok_rows, dtype=jnp.int32) % STRETCH
    allowed = [
        (1.0 - token_start * (token_offset < tap_index).astype(jnp.float32))[:, None]
        for tap_index in range(taps_count)
    ]
    inputs_f = tokens[0].astype(jnp.float32)
    attn_gain = gain_attn.astype(jnp.float32)
    inv_first = lax.rsqrt(jnp.mean(inputs_f * inputs_f, -1, keepdims=True) + EPSILON)
    normed = (inputs_f * inv_first * attn_gain).astype(jnp.bfloat16)
    projected = jnp.dot(normed, full_qkv, preferred_element_type=jnp.float32).astype(jnp.bfloat16)
    strength = jax.nn.sigmoid(
        jnp.dot(normed, full_beta, preferred_element_type=jnp.float32) + beta_bias
    )
    halo_rows = from_behind(projected[tok_rows - taps_count + 1 :], "span", 1)
    extended = jnp.concatenate([halo_rows, projected], 0).astype(jnp.float32)
    conv_f = full_conv.astype(jnp.float32)
    earlier_rows = [
        extended[taps_count - 1 - tap_index : taps_count - 1 - tap_index + tok_rows]
        for tap_index in range(taps_count)
    ]
    mixed = sum(
        (
            conv_f[tap_index] * allowed[tap_index] * earlier_rows[tap_index]
            for tap_index in range(taps_count)
        )
    )
    mix_sig = jax.nn.sigmoid(mixed)
    active = mixed * mix_sig
    query_raw = active[:, :model_width].reshape(tok_rows, head_count, head_size)
    key_raw = active[:, model_width : 2 * model_width].reshape(tok_rows, head_count, head_size)
    query_inv = lax.rsqrt(jnp.sum(query_raw * query_raw, -1, keepdims=True) + EPSILON)
    key_inv = lax.rsqrt(jnp.sum(key_raw * key_raw, -1, keepdims=True) + EPSILON)
    queries = (query_raw * query_inv).astype(jnp.bfloat16)
    keys_bf = (key_raw * key_inv).astype(jnp.bfloat16)
    values_bf = (
        active[:, 2 * model_width :].reshape(tok_rows, head_count, head_size).astype(jnp.bfloat16)
    )

    def by_stretch(array_in):
        return jnp.swapaxes(array_in.reshape((stretch_count, STRETCH) + array_in.shape[1:]), 1, 2)

    def by_token(array_in):
        swapped = jnp.swapaxes(array_in, 1, 2)
        return swapped.reshape((tok_rows,) + swapped.shape[2:])

    query_c = by_stretch(queries)
    key_c = by_stretch(keys_bf)
    value_c = by_stretch(values_bf)
    rate_c = by_stretch(strength)
    query_f = query_c.astype(jnp.float32)
    key_f = key_c.astype(jnp.float32)
    value_f = value_c.astype(jnp.float32)
    strict = jnp.tril(jnp.ones((STRETCH, STRETCH), jnp.float32), -1)
    causal = jnp.tril(jnp.ones((STRETCH, STRETCH), jnp.float32))
    key_gram = bf_product("chtd,chsd->chts", key_c, key_c)
    unit_lower = jnp.eye(STRETCH, dtype=jnp.float32) + rate_c[..., None] * key_gram * strict
    weighted_keys = jax.scipy.linalg.solve_triangular(
        unit_lower, rate_c[..., None] * key_f, lower=True, unit_diagonal=True
    )
    weighted_values = jax.scipy.linalg.solve_triangular(
        unit_lower, rate_c[..., None] * value_f, lower=True, unit_diagonal=True
    )
    identity = jnp.broadcast_to(
        jnp.eye(head_size, dtype=jnp.float32), (head_count, head_size, head_size)
    )
    zero_state = jnp.zeros((head_count, head_size, head_size), jnp.float32)
    transitions = identity - exact_product("chtb,chte->chbe", weighted_keys, key_f)
    contribs = exact_product("chta,chtb->chab", weighted_values, key_f)
    keep_wide = stretch_keep[:, None, None, None]
    device_map, _ = lax.scan(fold_maps, (identity, zero_state), (transitions * keep_wide, contribs))
    every_map = (
        lax.all_gather(device_map[0][None].astype(jnp.bfloat16), "span", axis=0, tiled=True).astype(
            jnp.float32
        ),
        lax.all_gather(device_map[1][None].astype(jnp.bfloat16), "span", axis=0, tiled=True).astype(
            jnp.float32
        ),
    )

    def forward_step(step_index, running):
        return (
            exact_product("hab,hbc->hac", running, every_map[0][step_index])
            + every_map[1][step_index]
        )

    state_in = lax.fori_loop(0, span_place, forward_step, zero_state)
    _, stretch_states = lax.scan(advance, state_in, (transitions, contribs, stretch_keep))
    new_values = weighted_values - exact_product("chtb,chab->chta", weighted_keys, stretch_states)
    scores = bf_product("chtd,chsd->chts", query_c, key_c) * causal
    readout_c = exact_product("chtb,chab->chta", query_f, stretch_states) + exact_product(
        "chts,chsa->chta", scores, new_values
    )
    readout = by_token(readout_c)
    head_gain = gain_head.astype(jnp.float32)
    head_inv = lax.rsqrt(jnp.mean(readout * readout, -1, keepdims=True) + EPSILON)
    normal_heads = (
        (readout * head_inv * head_gain).reshape(tok_rows, model_width).astype(jnp.bfloat16)
    )
    middle = inputs_f + jnp.dot(normal_heads, full_out, preferred_element_type=jnp.float32)
    ffn_gain = gain_ffn.astype(jnp.float32)
    inv_second = lax.rsqrt(jnp.mean(middle * middle, -1, keepdims=True) + EPSILON)
    normed_ffn = (middle * inv_second * ffn_gain).astype(jnp.bfloat16)
    gate = jnp.dot(normed_ffn, full_gate, preferred_element_type=jnp.float32)
    up_part = jnp.dot(normed_ffn, full_up, preferred_element_type=jnp.float32)
    gate_sig = jax.nn.sigmoid(gate)
    gate_act = gate * gate_sig
    hidden = (gate_act * up_part).astype(jnp.bfloat16)
    result = middle + jnp.dot(hidden, full_down, preferred_element_type=jnp.float32)
    grad_result = cotangent[0].astype(jnp.float32)
    grad_branch = cotangent[0]
    grad_down = bf_product("tf,td->fd", hidden, grad_branch)
    grad_hidden = bf_product("td,fd->tf", grad_branch, full_down)
    grad_gate_in = (grad_hidden * up_part * silu_slope(gate, gate_sig)).astype(jnp.bfloat16)
    grad_up_in = (grad_hidden * gate_act).astype(jnp.bfloat16)
    grad_gate = bf_product("td,tf->df", normed_ffn, grad_gate_in)
    grad_up = bf_product("td,tf->df", normed_ffn, grad_up_in)
    grad_nffn = bf_product("tf,df->td", grad_gate_in, full_gate) + bf_product(
        "tf,df->td", grad_up_in, full_up
    )
    grad_norm_ffn = jnp.sum(grad_nffn * middle * inv_second, 0)
    grad_middle = grad_result + norm_back(grad_nffn, middle, inv_second, ffn_gain)
    grad_attn_in = grad_middle.astype(jnp.bfloat16)
    grad_out = bf_product("tk,td->kd", normal_heads, grad_attn_in)
    grad_normal = bf_product("td,kd->tk", grad_attn_in, full_out).reshape(
        tok_rows, head_count, head_size
    )
    grad_norm_head = jnp.sum(grad_normal * readout * head_inv, (0, 1))
    grad_readout = norm_back(grad_normal, readout, head_inv, head_gain)
    grad_read_c = by_stretch(grad_readout)
    local_grad_values = exact_product("chts,chta->chsa", scores, grad_read_c)
    adjoint_c = exact_product("chta,chtb->chab", grad_read_c, query_f) - exact_product(
        "chta,chtb->chab", local_grad_values, weighted_keys
    )
    device_adjoint, _ = lax.scan(
        retract, zero_state, (transitions, adjoint_c, stretch_keep), reverse=True
    )
    every_adjoint = lax.all_gather(
        device_adjoint[None].astype(jnp.bfloat16), "span", axis=0, tiled=True
    ).astype(jnp.float32)

    def backward_step(step_index, running):
        source = span_count - 1 - step_index
        return exact_product("hab,hcb->hac", running, every_map[0][source]) + every_adjoint[source]

    grad_out_state = lax.fori_loop(0, span_count - 1 - span_place, backward_step, zero_state)
    _, stretch_end_grads = lax.scan(
        retract, grad_out_state, (transitions, adjoint_c, stretch_keep), reverse=True
    )
    grad_new_values = local_grad_values + exact_product("chtb,chab->chta", key_f, stretch_end_grads)
    grad_scores = exact_product("chta,chsa->chts", grad_read_c, new_values) * causal
    grad_query_c = exact_product("chts,chsb->chtb", grad_scores, key_f) + exact_product(
        "chta,chab->chtb", grad_read_c, stretch_states
    )
    grad_key_c = exact_product("chts,chtb->chsb", grad_scores, query_f) + exact_product(
        "chta,chab->chtb", new_values, stretch_end_grads
    )
    grad_weighted_keys = -exact_product("chta,chab->chtb", grad_new_values, stretch_states)
    grad_bv = jax.scipy.linalg.solve_triangular(
        unit_lower, grad_new_values, trans=1, lower=True, unit_diagonal=True
    )
    grad_bk = jax.scipy.linalg.solve_triangular(
        unit_lower, grad_weighted_keys, trans=1, lower=True, unit_diagonal=True
    )
    grad_lower = (
        -(
            exact_product("chta,chsa->chts", grad_bv, weighted_values)
            + exact_product("chtb,chsb->chts", grad_bk, weighted_keys)
        )
        * strict
    )
    grad_rate_c = (
        jnp.sum(grad_lower * key_gram, -1)
        + jnp.sum(grad_bv * value_f, -1)
        + jnp.sum(grad_bk * key_f, -1)
    )
    grad_gram = rate_c[..., None] * grad_lower
    grad_key_c = (
        grad_key_c
        + exact_product("chts,chsb->chtb", grad_gram + jnp.swapaxes(grad_gram, -1, -2), key_f)
        + rate_c[..., None] * grad_bk
    )
    grad_value_c = rate_c[..., None] * grad_bv
    grad_strength = by_token(grad_rate_c)
    grad_logit = grad_strength * strength * (1.0 - strength)
    grad_logit_low = grad_logit.astype(jnp.bfloat16)
    grad_w_beta = bf_product("td,th->dh", normed, grad_logit_low)
    bias_term = jnp.sum(grad_logit, 0)
    grad_query_raw = unit_back(by_token(grad_query_c), query_raw, query_inv)
    grad_key_raw = unit_back(by_token(grad_key_c), key_raw, key_inv)
    grad_active = jnp.concatenate(
        [
            grad_query_raw.reshape(tok_rows, model_width),
            grad_key_raw.reshape(tok_rows, model_width),
            by_token(grad_value_c).reshape(tok_rows, model_width),
        ],
        1,
    )
    grad_mixed = grad_active * silu_slope(mixed, mix_sig)
    grad_conv = jnp.stack(
        [
            jnp.sum(grad_mixed * allowed[tap_index] * earlier_rows[tap_index], 0)
            for tap_index in range(taps_count)
        ]
    )
    grad_extended = sum(
        (
            jnp.pad(
                conv_f[tap_index] * allowed[tap_index] * grad_mixed,
                ((taps_count - 1 - tap_index, tap_index), (0, 0)),
            )
            for tap_index in range(taps_count)
        )
    )
    halo_grad = from_behind(
        grad_extended[: taps_count - 1].astype(jnp.bfloat16), "span", -1
    ).astype(jnp.float32)
    grad_proj = (
        grad_extended[taps_count - 1 :]
        + jnp.pad(halo_grad, ((tok_rows - taps_count + 1, 0), (0, 0)))
    ).astype(jnp.bfloat16)
    grad_qkv = bf_product("td,te->de", normed, grad_proj)
    grad_normed = bf_product("te,de->td", grad_proj, full_qkv) + bf_product(
        "th,dh->td", grad_logit_low, full_beta
    )
    grad_norm_attn = jnp.sum(grad_normed * inputs_f * inv_first, 0)
    grad_tokens = grad_middle + norm_back(grad_normed, inputs_f, inv_first, attn_gain)
    bias_spread = jnp.broadcast_to(bias_term[None], (span_count, head_count))
    shared = (
        lax.psum_scatter(grad_qkv, "span", scatter_dimension=0, tiled=True),
        lax.psum_scatter(grad_conv, "span", scatter_dimension=1, tiled=True),
        lax.psum_scatter(grad_w_beta, "span", scatter_dimension=0, tiled=True),
        lax.psum_scatter(grad_norm_attn, "span", scatter_dimension=0, tiled=True),
        lax.psum_scatter(grad_norm_head, "span", scatter_dimension=0, tiled=True),
        lax.psum_scatter(grad_out, "span", scatter_dimension=0, tiled=True),
        lax.psum_scatter(grad_norm_ffn, "span", scatter_dimension=0, tiled=True),
        lax.psum_scatter(grad_gate, "span", scatter_dimension=0, tiled=True),
        lax.psum_scatter(grad_up, "span", scatter_dimension=0, tiled=True),
        lax.psum_scatter(grad_down, "span", scatter_dimension=0, tiled=True),
        lax.psum_scatter(bias_spread, "span", scatter_dimension=0, tiled=True),
    )
    (
        part_qkv,
        part_conv,
        part_beta,
        part_attn,
        part_head,
        part_out,
        part_ffn,
        part_gate,
        part_up,
        part_down,
        part_bias,
    ) = shared
    summed = (
        lax.psum(part_qkv.astype(jnp.bfloat16), "stream").astype(jnp.float32),
        lax.psum(part_conv.astype(jnp.bfloat16), "stream").astype(jnp.float32),
        lax.psum(part_beta.astype(jnp.bfloat16), "stream").astype(jnp.float32),
        lax.psum(part_attn.astype(jnp.bfloat16), "stream").astype(jnp.float32),
        lax.psum(part_head.astype(jnp.bfloat16), "stream").astype(jnp.float32),
        lax.psum(part_out.astype(jnp.bfloat16), "stream").astype(jnp.float32),
        lax.psum(part_ffn.astype(jnp.bfloat16), "stream").astype(jnp.float32),
        lax.psum(part_gate.astype(jnp.bfloat16), "stream").astype(jnp.float32),
        lax.psum(part_up.astype(jnp.bfloat16), "stream").astype(jnp.float32),
        lax.psum(part_down.astype(jnp.bfloat16), "stream").astype(jnp.float32),
        lax.psum(part_bias.astype(jnp.bfloat16), "stream").astype(jnp.float32),
    )
    return (
        result.astype(jnp.bfloat16)[None],
        grad_tokens[None],
        summed[0],
        summed[1],
        summed[2],
        summed[10][0],
        summed[3],
        summed[4],
        summed[5],
        summed[6],
        summed[7],
        summed[8],
        summed[9],
    )


def solution(mesh):
    in_specs = (
        P("stream", "span", None),
        P("stream", "span", None),
        P("stream", None),
        P("span", None),
        P(None, "span"),
        P("span", None),
        P(),
        P("span"),
        P("span"),
        P("span", None),
        P("span"),
        P("span", None),
        P("span", None),
        P("span", None),
    )
    out_specs = (
        P("stream", "span", None),
        P("stream", "span", None),
        P("span", None),
        P(None, "span"),
        P("span", None),
        P(),
        P("span"),
        P("span"),
        P("span", None),
        P("span"),
        P("span", None),
        P("span", None),
        P("span", None),
    )
    return jax.shard_map(local, mesh=mesh, in_specs=in_specs, out_specs=out_specs, check_vma=False)
```

profile of v0, /device:TPU:0, one launch (start us, length us, event | category | flops | bytes accessed | tf_op | source)
XLA Modules:
  0.0 1406.5 jit_solution(12403364871915935832)
XLA Ops:
  8.0 13.5 all-gather.3
  23.4 13.1 all_gather.42
  36.5 14.2 %all_gather.39 = bf16[4,3072]{1,0:T(4,128)(2,1)S(1)} all-gather(bf16[4,384]{1,0:T(4,128)(2,1)} %param.34), channel_id=1, replica_groups=mesh['stream'=4,'span'=8] {'span'}, dimensions={1}, use_global_device_ids=true | all-gather | bytes 27648 | tf_op jit(solution)/shard_map/all_gather | solution.py:85
  55.8 21.6 %all-gather.14.cloned.1.call-done = bf16[1024,3072]{1,0:T(8,128)(2,1)} async-done(((bf16[128,3072]{1,0:T(8,128)(2,1)}), bf16[1024,3072]{1,0:T(8,128)(2,1)}) %all-gather.14.cloned.1.call-update) | async-done | bytes 6291472 | tf_op jit(solution)/shard_map/all_gather | solution.py:84
  77.4 4.8 convolution_convert_fusion
  87.2 3.8 fusion.42
  114.5 159.1 %custom-call.10 = f32[4,8,1,64,64]{3,4,2,1,0:T(8,128)} custom-call(f32[4,8,1,64,64]{4,3,2,1,0:T(8,128)} %add_bitcast_fusion), custom_call_target="InvertDiagBlocksLowerTriangular" | custom-call | tf_op jit(solution)/shard_map/jit(_solve_triangular)/vmap(vmap())/triangular_solve | solution.py:177
  275.2 3.8 fusion.55
  282.2 3.2 fusion.134
  285.4 4.0 broadcast_multiply_fusion
  290.2 43.7 %while.82 = (s32[]{:T(128)}, f32[8,128,128]{1,2,0:T(8,128)}, f32[8,128,128]{1,2,0:T(8,128)}, f32[4,8,128,128]{3,2,1,0:T(8,128)}, f32[4,8,128,128]{3,2,1,0:T(8,128)}, /*index=5*/s32[]{:T(128)}, s32[]{:T(128)}) while((s32[]{:T(128)}, f32[8,128,128]{1,2,0:T(8,128)}, f32[8,128,128]{1,2,0:T(8,128)}, f32[4,8,128,128]{3,2,1,0:T(8,128)}, ...), condition=%wide.region_6.8_spmd.clone, body=%wide.region_5.7_spmd.clone.sunk | while | flops 402915328 | bytes 9962615 | solution.py:190
  342.0 14.6 %all-reduce.5 = bf16[128]{0:T(256)(128)(2,1)S(1)} all-reduce(bf16[128]{0:T(256)(128)(2,1)S(1)} %dynamic-update-slice), channel_id=1, replica_groups=mesh['stream'=4,'span'=8] {'span'}, use_global_device_ids=true, to_apply=%add.5 | all-reduce | flops 128 | bytes 512
  356.6 8.5 all-gather.4
  367.7 4.2 convert.19
  371.9 25.1 %all-gather.26.cloned.1.call-done = bf16[64,128,128]{2,1,0:T(8,128)(2,1)} async-done(((bf16[8,128,128]{2,1,0:T(8,128)(2,1)}), bf16[64,128,128]{2,1,0:T(8,128)(2,1)}) %all-gather.26.cloned.1.call-update) | async-done | bytes 2097168 | tf_op jit(solution)/shard_map/all_gather | solution.py:195
  397.0 4.1 convert.20
  404.0 25.8 %while.79 = (s32[]{:T(128)}, f32[8,128,128]{2,1,0:T(8,128)}, f32[4,8,128,128]{3,2,1,0:T(8,128)}, f32[4]{0:T(128)S(1)}, f32[4,8,128,128]{3,2,1,0:T(8,128)}, /*index=5*/f32[4,8,128,128]{3,2,1,0:T(8,128)}, s32[]{:T(128)}) while((s32[]{:T(128)}, f32[8,128,128]{2,1,0:T(8,128)}, f32[4,8,128,128]{3,2,1,0:T(8,128)}, f32[4]{0:T(128)S(1)}, ...), condition=%wide.region_10.12_spmd, body=%wide.region_9.11_spmd.sunk | while | flops 201719808 | bytes 4196953 | solution.py:207
  407.1 3.3 convolution_add_fusion.12
  413.5 3.3 convolution_add_fusion.12
  420.0 3.3 convolution_add_fusion.12
  426.4 3.3 convolution_add_fusion.12
  429.9 4.1 fusion.135
  434.0 5.6 convolution_subtract_fusion.2
  451.9 36.6 %all-gather.18.cloned.1.call-done = bf16[1024,2816]{1,0:T(8,128)(2,1)} async-done(((bf16[128,2816]{1,0:T(8,128)(2,1)}), bf16[1024,2816]{1,0:T(8,128)(2,1)}) %all-gather.18.cloned.1.call-update) | async-done | bytes 5767184 | tf_op jit(solution)/shard_map/all_gather | solution.py:91
  488.5 6.0 fusion.136
  494.6 54.6 %all-gather.20.cloned.1.call-done = bf16[1024,2816]{1,0:T(8,128)(2,1)} async-done(((bf16[128,2816]{1,0:T(8,128)(2,1)}), bf16[1024,2816]{1,0:T(8,128)(2,1)}) %all-gather.20.cloned.1.call-update) | async-done | bytes 5767184 | tf_op jit(solution)/shard_map/all_gather | solution.py:92
  549.2 6.1 fusion.137
  555.3 54.7 %all-gather.22.cloned.1.call-done = bf16[2816,1024]{1,0:T(8,128)(2,1)} async-done(((bf16[352,1024]{1,0:T(8,128)(2,1)}), bf16[2816,1024]{1,0:T(8,128)(2,1)}) %all-gather.22.cloned.1.call-update) | async-done | bytes 5767184 | tf_op jit(solution)/shard_map/all_gather | solution.py:93
  610.0 8.6 multiply_convert_fusion
  618.5 5.4 fusion.138
  635.4 4.9 convolution_subtract_fusion
  643.2 19.8 %while.83 = (s32[]{:T(128)}, f32[8,128,128]{1,2,0:T(8,128)}, f32[4]{0:T(128)S(1)}, f32[4,8,128,128]{3,2,1,0:T(8,128)}, f32[4,8,128,128]{2,3,1,0:T(8,128)}, /*index=5*/s32[]{:T(128)}, s32[]{:T(128)}, s32[]{:T(128)}) while((s32[]{:T(128)}, f32[8,128,128]{1,2,0:T(8,128)}, f32[4]{0:T(128)S(1)}, f32[4,8,128,128]{3,2,1,0:T(8,128)}, ...), condition=%wide.region_17.19_spmd.clone, body=%wide.region_16.18_spmd.clone.sunk | while | flops 201719808 | bytes 3147894 | solution.py:254
  644.8 3.3 fusion.249
  649.8 3.3 fusion.249
  654.7 3.3 fusion.249
  659.6 3.3 fusion.249
  664.9 4.1 fusion.104
  669.1 7.5 fusion.143
  676.9 7.4 fusion.144
  684.4 7.4 fusion.94
  695.0 3.5 convolution_multiply_fusion
  700.1 3.2 multiply_reduce_fusion.7
  706.9 3.3 fusion.140
  710.3 4.2 convert.21
  715.2 53.5 %while.80 = (s32[]{:T(128)}, f32[8,128,128]{1,2,0:T(8,128)}, s32[]{:T(128)}, f32[8,8,128,128]{3,2,1,0:T(8,128)}, f32[8,8,128,128]{3,2,1,0:T(8,128)}, /*index=5*/s32[]{:T(128)}, s32[]{:T(128)}, s32[]{:T(128)}, s32[]{:T(128)}) while((s32[]{:T(128)}, f32[8,128,128]{1,2,0:T(8,128)}, s32[]{:T(128)}, f32[8,8,128,128]{3,2,1,0:T(8,128)}, ...), condition=%wide.region_19.21_spmd, body=%wide.region_18.20_spmd.sunk | while | flops 201457664 | bytes 5243027 | solution.py:265
  770.3 23.2 %while.81 = (s32[]{:T(128)}, f32[8,128,128]{1,2,0:T(8,128)}, f32[4,8,128,128]{2,3,1,0:T(8,128)}, f32[4]{0:T(128)S(1)}, f32[4,8,128,128]{3,2,1,0:T(8,128)}, /*index=5*/f32[4,8,128,128]{2,3,1,0:T(8,128)}, s32[]{:T(128)}, s32[]{:T(128)}) while((s32[]{:T(128)}, f32[8,128,128]{1,2,0:T(8,128)}, f32[4,8,128,128]{2,3,1,0:T(8,128)}, ...), condition=%wide.region_21.23_spmd, body=%wide.region_20.22_spmd.sunk | while | flops 201588736 | bytes 4195953 | solution.py:266
  772.7 3.3 fusion.241
  778.5 3.3 fusion.241
  784.2 3.3 fusion.241
  790.0 3.3 fusion.241
  793.5 3.4 convolution_add_fusion.6
  810.9 6.9 convolution_add_fusion.3
  830.9 3.8 multiply_reduce_fusion.3
  841.3 6.5 fusion.108
  854.5 10.0 reduce-scatter.16.cloned.1.call-done
  866.8 117.5 %reduce-scatter.18.cloned.1.call-done = f32[128,2816]{1,0:T(8,128)} async-done(((f32[1024,2816]{1,0:T(8,128)}), f32[128,2816]{1,0:T(8,128)}) %reduce-scatter.18.cloned.1.call-update) | async-done | bytes 1441808 | tf_op jit(solution)/shard_map/reduce_scatter | solution.py:357
  986.8 117.5 %reduce-scatter.20.cloned.1.call-done = f32[352,1024]{1,0:T(8,128)} async-done(((f32[2816,1024]{1,0:T(8,128)}), f32[352,1024]{1,0:T(8,128)}) %reduce-scatter.20.cloned.1.call-update) | async-done | bytes 1441808 | tf_op jit(solution)/shard_map/reduce_scatter | solution.py:358
  1106.6 127.5 %reduce-scatter.10.cloned.1.call-done = f32[128,3072]{1,0:T(8,128)} async-done(((f32[1024,3072]{1,0:T(8,128)}), f32[128,3072]{1,0:T(8,128)}) %reduce-scatter.10.cloned.1.call-update) | async-done | bytes 1572880 | tf_op jit(solution)/shard_map/reduce_scatter | solution.py:349
  1238.0 5.7 fusion.50
  1244.0 5.1 fusion.66
  1249.1 26.0 %all-reduce.10 = (bf16[8,8]{1,0:T(8,128)(2,1)S(1)}, bf16[1024]{0:T(1024)(128)(2,1)S(1)}, bf16[128]{0:T(256)(128)(2,1)S(1)}, bf16[1024]{0:T(1024)(128)(2,1)S(1)}) all-reduce(f32[8,8]{1,0:T(8,128)S(1)} %broadcast_in_dim.37, f32[1024]{0:T(1024)S(1)} %get-tuple-element.627, ...), channel_id=8, replica_groups=mesh['stream'=4,'span'=8] {'span'}, use_global_device_ids=true, to_apply=%region_38.41.clone | all-reduce | flops 2240 | bytes 13440
  1278.1 21.8 %reduce-scatter.22.cloned.1.call-done = f32[384,4]{1,0:T(8,128)} async-done(((f32[3072,4]{1,0:T(8,128)}), f32[384,4]{1,0:T(8,128)}) %reduce-scatter.22.cloned.1.call-update) | async-done | bytes 6160
  1300.9 9.9 all-reduce.11
  1314.1 77.5 %all-reduce.15.cloned.1.call-done = (bf16[128,3072]{1,0:T(8,128)(2,1)}, bf16[128,1024]{1,0:T(8,128)(2,1)}, bf16[128,2816]{1,0:T(8,128)(2,1)}, bf16[128,2816]{1,0:T(8,128)(2,1)}, bf16[352,1024]{1,0:T(8,128)(2,1)}) async-done(((bf16[128,3072]{1,0:T(8,128)(2,1)}, bf16[128,1024]{1,0:T(8,128)(2,1)}, bf16[128,2816]{1,0:T(8,128)(2,1)}, bf16[128,2816]{1,0:T(8,128)(2,1)}, bf16[352,1024]{1,0:T(8,128)(2,1)}), ...) | async-done | bytes 3211280 | tf_op jit(solution)/shard_map/psum | solution.py:375
  (502 shorter events, 284.5 us)
Async XLA Ops:
  7.2 70.2 %all-gather.14.cloned.1.call-start = ((), (), s32[]{:S(2)}) async-start(), calls=%async_computation.7 | async-start | bytes 7077888 | tf_op jit(solution)/shard_map/all_gather | solution.py:84
  7.9 359.8 %all-gather.24.cloned.1.call-start = ((), (), s32[]{:S(2)}) async-start(), calls=%async_computation.18 | async-start | bytes 2359296 | tf_op jit(solution)/shard_map/all_gather | solution.py:192
  21.5 60.7 %copy-start.69 = (f32[8,1,128]{2,1,0:T(1,128)}, f32[8,1,128]{2,1,0:T(1,128)S(1)}, u32[]{:S(2)}) copy-start(f32[8,1,128]{2,1,0:T(1,128)S(1)} %convert_element_type.271) | copy-start | bytes 12292
  36.5 19.2 %copy-start.86 = (bf16[1024,8]{0,1:T(8,128)(2,1)}, bf16[1024,8]{0,1:T(8,128)(2,1)S(1)}, u32[]{:S(2)}) copy-start(bf16[1024,8]{0,1:T(8,128)(2,1)S(1)} %all_gather.42) | copy-start | bytes 49156
  52.9 29.3 %copy-start.94 = (f32[256]{0:T(256)}, f32[256]{0:T(256)S(1)}, u32[]{:S(2)}) copy-start(f32[256]{0:T(256)S(1)} %get-tuple-element.739) | copy-start | bytes 3076
  52.9 34.2 %copy-start.96 = (f32[256]{0:T(256)}, f32[256]{0:T(256)S(1)}, u32[]{:S(2)}) copy-start(f32[256]{0:T(256)S(1)} %get-tuple-element.742) | copy-start | bytes 3076
  53.0 34.2 %copy-start.98 = (f32[256]{0:T(256)}, f32[256]{0:T(256)S(1)}, u32[]{:S(2)}) copy-start(f32[256]{0:T(256)S(1)} %get-tuple-element.743) | copy-start | bytes 3076
  53.0 34.2 %copy-start.100 = (f32[256]{0:T(256)}, f32[256]{0:T(256)S(1)}, u32[]{:S(2)}) copy-start(f32[256]{0:T(256)S(1)} %get-tuple-element.744) | copy-start | bytes 3076
  53.0 34.2 %copy-start.102 = (f32[256]{0:T(256)}, f32[256]{0:T(256)S(1)}, u32[]{:S(2)}) copy-start(f32[256]{0:T(256)S(1)} %get-tuple-element.745) | copy-start | bytes 3076
  55.7 29.4 %copy-start.92 = (f32[256,8]{0,1:T(8,128)}, f32[256,8]{0,1:T(8,128)S(1)}, u32[]{:S(2)}) copy-start(f32[256,8]{0,1:T(8,128)S(1)} %fusion.54) | copy-start | bytes 24580
  55.7 31.5 %copy-start.74 = (f32[1,3072]{1,0:T(1,128)}, f32[1,3072]{1,0:T(1,128)S(1)}, u32[]{:S(2)}) copy-start(f32[1,3072]{1,0:T(1,128)S(1)} %get-tuple-element.726) | copy-start | bytes 36868
  55.7 31.5 %copy-start.76 = (f32[1,3072]{1,0:T(1,128)}, f32[1,3072]{1,0:T(1,128)S(1)}, u32[]{:S(2)}) copy-start(f32[1,3072]{1,0:T(1,128)S(1)} %get-tuple-element.727) | copy-start | bytes 36868
  55.7 31.5 %copy-start.78 = (f32[1,3072]{1,0:T(1,128)}, f32[1,3072]{1,0:T(1,128)S(1)}, u32[]{:S(2)}) copy-start(f32[1,3072]{1,0:T(1,128)S(1)} %get-tuple-element.728) | copy-start | bytes 36868
  55.8 31.5 %copy-start.80 = (f32[1,3072]{1,0:T(1,128)}, f32[1,3072]{1,0:T(1,128)S(1)}, u32[]{:S(2)}) copy-start(f32[1,3072]{1,0:T(1,128)S(1)} %get-tuple-element.729) | copy-start | bytes 36868
  82.3 3.0 collective-permute-start
  104.8 4.7 copy-start.88
  273.6 5.4 copy-start.19
  275.2 10.2 copy-start.30
  275.2 7.0 copy-start.1
  279.0 6.4 copy-start.10
  279.1 6.4 copy-start.106
  333.9 6.5 copy-start.105
  333.9 7.8 copy-start.110
  333.9 22.7 %copy-start.108 = (bf16[128]{0:T(256)(128)(2,1)S(1)}, bf16[128]{0:T(256)(128)(2,1)}, u32[]{:S(2)}) copy-start(bf16[128]{0:T(256)(128)(2,1)} %param.40) | copy-start | bytes 772
  335.8 61.2 %all-gather.26.cloned.1.call-start = ((), (), s32[]{:S(2)}) async-start(), calls=%async_computation.19 | async-start | bytes 2359296 | tf_op jit(solution)/shard_map/all_gather | solution.py:195
  337.8 109.5 %all-gather.16.cloned.1.call-start = ((), (), s32[]{:S(2)}) async-start(), calls=%async_computation.8 | async-start | bytes 2359296 | tf_op jit(solution)/shard_map/all_gather | solution.py:89
  338.4 150.2 %all-gather.18.cloned.1.call-start = ((), (), s32[]{:S(2)}) async-start(), calls=%async_computation.9 | async-start | bytes 6488064 | tf_op jit(solution)/shard_map/all_gather | solution.py:91
  339.0 210.2 %all-gather.20.cloned.1.call-start = ((), (), s32[]{:S(2)}) async-start(), calls=%async_computation.10 | async-start | bytes 6488064 | tf_op jit(solution)/shard_map/all_gather | solution.py:92
  339.5 270.4 %all-gather.22.cloned.1.call-start = ((), (), s32[]{:S(2)}) async-start(), calls=%async_computation.11 | async-start | bytes 6488064 | tf_op jit(solution)/shard_map/all_gather | solution.py:93
  340.3 370.0 %all-gather.28.cloned.1.call-start = ((), (), s32[]{:S(2)}) async-start(), calls=%async_computation.20 | async-start | bytes 2359296 | tf_op jit(solution)/shard_map/all_gather | solution.py:257
  434.0 6.6 copy-start.41
  618.5 5.4 copy-start.60
  618.5 5.4 copy-start.59
  618.5 5.4 copy-start.32
  618.5 5.7 copy-start.109
  630.7 4.7 copy-start.12
  664.9 187.9 %reduce-scatter.14.cloned.1.call-start = ((), (), s32[]{:S(2)}) async-start(), calls=%async_computation.14 | async-start | bytes 4718592 | tf_op jit(solution)/shard_map/reduce_scatter | solution.py:354
  669.1 195.5 %reduce-scatter.16.cloned.1.call-start = ((), (), s32[]{:S(2)}) async-start(), calls=%async_computation.15 | async-start | bytes 12976128 | tf_op jit(solution)/shard_map/reduce_scatter | solution.py:356
  676.7 307.7 %reduce-scatter.18.cloned.1.call-start = ((), (), s32[]{:S(2)}) async-start(), calls=%async_computation.16 | async-start | bytes 12976128 | tf_op jit(solution)/shard_map/reduce_scatter | solution.py:357
  684.3 419.9 %reduce-scatter.20.cloned.1.call-start = ((), (), s32[]{:S(2)}) async-start(), calls=%async_computation.17 | async-start | bytes 12976128 | tf_op jit(solution)/shard_map/reduce_scatter | solution.py:358
  691.8 542.3 %reduce-scatter.10.cloned.1.call-start = ((), (), s32[]{:S(2)}) async-start(), calls=%async_computation.12 | async-start | bytes 14155776 | tf_op jit(solution)/shard_map/reduce_scatter | solution.py:349
  695.0 5.1 copy-start.6
  695.0 5.1 copy-start.9
  695.0 5.1 copy-start.40
  793.5 5.6 copy-start.18
  810.9 6.9 copy-start.4
  810.9 6.9 copy-start.38
  810.9 6.9 copy-start.48
  810.9 6.9 copy-start.51
  810.9 6.9 copy-start.52
  810.9 6.9 copy-start.71
  838.1 9.7 copy-start.26
  838.2 3.1 collective-permute-start.1
  847.9 429.5 %reduce-scatter.12.cloned.1.call-start = ((), (), s32[]{:S(2)}) async-start(), calls=%async_computation.13 | async-start | bytes 36864 | tf_op jit(solution)/shard_map/reduce_scatter | solution.py:351
  850.9 449.1 %reduce-scatter.22.cloned.1.call-start = ((), (), s32[]{:S(2)}) async-start(), calls=%async_computation.21 | async-start | bytes 1769472
  852.7 538.9 %all-reduce.15.cloned.1.call-start = ((), (), s32[]{:S(2)}) async-start(), calls=%async_computation.22 | async-start | bytes 6422528 | tf_op jit(solution)/shard_map/psum | solution.py:375
  1106.6 131.4 %copy-start.33 = (f32[256,1024]{1,0:T(8,128)S(1)}, f32[256,1024]{1,0:T(8,128)}, u32[]{:S(2)}) copy-start(f32[256,1024]{1,0:T(8,128)} %copy-done.31) | copy-start | bytes 3145732
  1237.9 5.7 copy-start.87
  1238.0 6.0 copy-start.27
  1244.0 32.1 %copy-start.23 = (f32[256,1024]{1,0:T(8,128)S(1)}, f32[256,1024]{1,0:T(8,128)}, u32[]{:S(2)}) copy-start(f32[256,1024]{1,0:T(8,128)} %copy-done.22) | copy-start | bytes 3145732
  1244.0 32.1 %copy-start.104 = (f32[256]{0:T(256)S(1)}, f32[256]{0:T(256)}, u32[]{:S(2)}) copy-start(f32[256]{0:T(256)} %get-tuple-element.738) | copy-start | bytes 3076
  1391.6 4.9 copy-start.62
  1391.6 6.1 copy-start.61
  1394.1 4.8 copy-start.68
  (68 other events, 169.2 us)
Sparse Core Ops, SparseCore 0:
  9.7 67.7 all-gather.13
  336.0 30.2 all-gather.23
  368.4 28.5 all-gather.25
  398.5 28.5 all-gather.15
  428.6 59.9 all-gather.17
  490.0 59.0 all-gather.19
  550.8 59.0 all-gather.21
  665.0 27.7 all-gather.27
  695.1 49.4 reduce-scatter.13
  746.8 117.6 reduce-scatter.15
  866.9 117.4 reduce-scatter.17
  986.5 117.6 reduce-scatter.19
  1106.5 127.5 reduce-scatter.9
  1236.2 28.3 reduce-scatter.11
  1267.5 32.4 reduce-scatter.21
  1304.5 87.0 all-reduce.14
where the time goes:
time: 1420 us; the launch traced here: 1410 us
  waiting for transfers between devices  669 us (47%)
  other arithmetic  241 us (17%)
  matrix products  234 us (16%)
  local copies, waits for them, and re-layouts  139 us (10%)
  blocking collectives  99.9 us (7%)
  between operations  17.8 us (1%)
    another operation x5, other arithmetic, local(): jax.scipy.linalg.solve_triangular(unit_lower, rate_c[..., None] * key_f,...  162 us
    dot_general x45, matrix products, exact_product(): jnp.einsum(pattern, first_op, second_op, precision=PRECISE, preferred_ele...  139 us
    reduce_scatter x1, waiting for transfers between devices, local(): lax.psum_scatter(grad_qkv, 'span', scatter_dimension=0, tiled=True)  128 us
    reduce_scatter x1, waiting for transfers between devices, local(): lax.psum_scatter(grad_up, 'span', scatter_dimension=0, tiled=True)  118 us
    reduce_scatter x1, waiting for transfers between devices, local(): lax.psum_scatter(grad_down, 'span', scatter_dimension=0, tiled=True)  117 us
    psum x1, waiting for transfers between devices, local(): lax.psum(part_qkv.astype(jnp.bfloat16), 'stream').astype(jnp.float32)  77.5 us
    dot_general x14, matrix products, bf_product(): jnp.einsum(pattern, first_op, second_op, preferred_element_type=jnp.float32)  59.2 us
    all_gather x1, waiting for transfers between devices, local(): lax.all_gather(w_down, 'span', axis=0, tiled=True)  54.7 us
  transfers between devices with their start and end apart: 18, of which 12 were waited for; matrix products, arithmetic and copies ran while one was open for 20% of the time, Pallas kernels for 0%

commit v1 on v0

v1 whole, which is shorter than its diff:
```python
import functools

import jax
import jax.numpy as jnp
from jax import lax
from jax.experimental import pallas as pl
from jax.experimental.pallas import tpu as pltpu
from jax.sharding import PartitionSpec as P

STRETCH = 64
HALO = 16
EPSILON = 1e-06
F32 = jnp.float32
BF16 = jnp.bfloat16
AXES = ("stream", "span")
VMEM_LIMIT = 56 * 2**20


def nn(a, b):
    return lax.dot_general(a, b, (((1,), (0,)), ((), ())), preferred_element_type=F32)


def nt(a, b):
    return lax.dot_general(a, b, (((1,), (1,)), ((), ())), preferred_element_type=F32)


def tn(a, b):
    return lax.dot_general(a, b, (((0,), (0,)), ((), ())), preferred_element_type=F32)


def fine(a, b):
    a_hi = a.astype(BF16)
    a_lo = (a - a_hi.astype(F32)).astype(BF16)
    b_hi = b.astype(BF16)
    b_lo = (b - b_hi.astype(F32)).astype(BF16)
    return nn(jnp.concatenate([a_hi, a_hi, a_lo], 1), jnp.concatenate([b_hi, b_lo, b_hi], 0))


def grid_ids(size):
    return (
        lax.broadcasted_iota(jnp.int32, (size, size), 0),
        lax.broadcasted_iota(jnp.int32, (size, size), 1),
    )


def unit_inverse(lower_list):
    rows, cols = grid_ids(STRETCH)
    eye = (rows == cols).astype(F32)
    out = [eye - jnp.where((rows // 2) == (cols // 2), low, 0.0) for low in lower_list]
    half = 2
    while half < STRETCH:
        cross = ((rows // (2 * half)) == (cols // (2 * half))) & ((rows // half) != (cols // half))
        inner = [fine(jnp.where(cross, low, 0.0), inv) for low, inv in zip(lower_list, out)]
        out = [inv - fine(inv, mid) for inv, mid in zip(out, inner)]
        half *= 2
    return out


def column_of(table, index):
    lanes = lax.broadcasted_iota(jnp.int32, table.shape, 1)
    return jnp.sum(jnp.where(lanes == index, table, 0.0), -1, keepdims=True)


def mix_rows(ext_ref, conv_ref, allow):
    ext = ext_ref[...].astype(F32)
    conv = conv_ref[...].astype(F32)
    shifted = [
        (ext if tap == 0 else pltpu.roll(ext, tap, 0))[HALO:] * allow[tap]
        for tap in range(conv.shape[0])
    ]
    mixed = sum(conv[tap : tap + 1] * shifted[tap] for tap in range(conv.shape[0]))
    return shifted, mixed, conv


def local_kernel(
    keep_ref, eq_ref, ek_ref, ev_ref, cq_ref, ck_ref, cv_ref, rate_ref, allow_ref,
    q_ref, k_ref, v_ref, inv_ref, wk_ref, pre_ref, end_ref, read_ref, rmap_ref, nv_ref, np_ref,
):
    head = pl.program_id(0)
    allow_all = allow_ref[...]
    allow = [allow_all[:, tap : tap + 1] for tap in range(cq_ref.shape[0])]
    rate = column_of(rate_ref[...], head)

    def unit(ref, conv):
        _, mixed, _ = mix_rows(ref, conv, allow)
        act = mixed * jax.nn.sigmoid(mixed)
        return act

    act_q = unit(eq_ref, cq_ref)
    act_k = unit(ek_ref, ck_ref)
    act_v = unit(ev_ref, cv_ref)
    queries = (act_q * lax.rsqrt(jnp.sum(act_q * act_q, -1, keepdims=True) + EPSILON)).astype(BF16)
    keys = (act_k * lax.rsqrt(jnp.sum(act_k * act_k, -1, keepdims=True) + EPSILON)).astype(BF16)
    values = act_v.astype(BF16)
    q_ref[...] = queries
    k_ref[...] = keys
    v_ref[...] = values
    count = queries.shape[0] // STRETCH
    rows, cols = grid_ids(STRETCH)
    parts = [slice(n * STRETCH, (n + 1) * STRETCH) for n in range(count)]
    lows = []
    for part in parts:
        gram = nt(keys[part], keys[part])
        lows.append(jnp.where(rows > cols, gram * rate[part], 0.0))
    invs = unit_inverse(lows)
    size = keys.shape[1]
    drows, dcols = grid_ids(size)
    running = jnp.concatenate(
        [jnp.zeros((size, size), F32), (drows == dcols).astype(F32)], 0
    )
    for n, part in enumerate(parts):
        key, query = keys[part], queries[part]
        inv = invs[n].astype(BF16)
        inv_ref[0, part, :] = inv
        scaled = jnp.concatenate(
            [key.astype(F32) * rate[part], values[part].astype(F32) * rate[part]], 1
        ).astype(BF16)
        weighted = nn(inv, scaled)
        wkey = weighted[:, :size].astype(BF16)
        wk_ref[part, :] = wkey
        running = running * keep_ref[n]
        low_state = running.astype(BF16)
        pre_ref[0, n] = low_state
        back = nt(jnp.concatenate([wkey, query], 0), low_state)
        new = jnp.concatenate(
            [weighted[:, size:] - back[:STRETCH, :size], -back[:STRETCH, size:]], 1
        ).astype(BF16)
        nv_ref[part, :] = new[:, :size]
        np_ref[part, :] = new[:, size:]
        scores = jnp.where(rows >= cols, nt(query, key), 0.0).astype(BF16)
        out = back[STRETCH:] + nn(scores, new)
        read_ref[part, :] = out[:, :size]
        rmap_ref[part, :] = out[:, size:].astype(BF16)
        running = running + tn(new, key)
    end_ref[0] = running.astype(BF16)


def local_call(keep, ext, conv, rate, allow, heads):
    tok = rate.shape[0]
    width = ext.shape[1] // 3
    size = width // heads
    count = tok // STRETCH
    taps = conv.shape[0]
    rows = ext.shape[0]

    def third(i, r):
        return pl.BlockSpec((r, size), lambda h: (0, h + i * heads))

    def token_block():
        return pl.BlockSpec((tok, size), lambda h: (0, h))

    return pl.pallas_call(
        local_kernel,
        grid=(heads,),
        in_specs=[
            pl.BlockSpec(memory_space=pltpu.SMEM),
            third(0, rows), third(1, rows), third(2, rows),
            third(0, taps), third(1, taps), third(2, taps),
            pl.BlockSpec((tok, heads), lambda h: (0, 0)),
            pl.BlockSpec((tok, taps), lambda h: (0, 0)),
        ],
        out_specs=[
            token_block(), token_block(), token_block(),
            pl.BlockSpec((1, tok, STRETCH), lambda h: (h, 0, 0)),
            token_block(),
            pl.BlockSpec((1, count, 2 * size, size), lambda h: (h, 0, 0, 0)),
            pl.BlockSpec((1, 2 * size, size), lambda h: (h, 0, 0)),
            token_block(), token_block(), token_block(), token_block(),
        ],
        out_shape=[
            jax.ShapeDtypeStruct((tok, width), BF16),
            jax.ShapeDtypeStruct((tok, width), BF16),
            jax.ShapeDtypeStruct((tok, width), BF16),
            jax.ShapeDtypeStruct((heads, tok, STRETCH), BF16),
            jax.ShapeDtypeStruct((tok, width), BF16),
            jax.ShapeDtypeStruct((heads, count, 2 * size, size), BF16),
            jax.ShapeDtypeStruct((heads, 2 * size, size), BF16),
            jax.ShapeDtypeStruct((tok, width), F32),
            jax.ShapeDtypeStruct((tok, width), BF16),
            jax.ShapeDtypeStruct((tok, width), BF16),
            jax.ShapeDtypeStruct((tok, width), BF16),
        ],
        compiler_params=pltpu.CompilerParams(vmem_limit_bytes=VMEM_LIMIT),
        cost_estimate=pl.CostEstimate(flops=2 * 10**9, bytes_accessed=10**7, transcendentals=10**6),
        name="delta_local",
    )(keep, ext, ext, ext, conv, conv, conv, rate, allow)


def readout_kernel(state_ref, read_ref, rmap_ref, gain_ref, out_ref, normal_ref):
    readout = read_ref[...] + nt(rmap_ref[...], state_ref[0])
    inv = lax.rsqrt(jnp.mean(readout * readout, -1, keepdims=True) + EPSILON)
    out_ref[...] = readout
    normal_ref[...] = (readout * inv * gain_ref[...]).astype(BF16)


def readout_call(state, read, rmap, gain):
    heads, size, _ = state.shape
    tok, width = read.shape
    block = pl.BlockSpec((tok, size), lambda h: (0, h))
    return pl.pallas_call(
        readout_kernel,
        grid=(heads,),
        in_specs=[
            pl.BlockSpec((1, size, size), lambda h: (h, 0, 0)),
            block, block,
            pl.BlockSpec((1, size), lambda h: (0, 0)),
        ],
        out_specs=[block, block],
        out_shape=[
            jax.ShapeDtypeStruct((tok, width), F32),
            jax.ShapeDtypeStruct((tok, width), BF16),
        ],
        compiler_params=pltpu.CompilerParams(vmem_limit_bytes=VMEM_LIMIT),
        cost_estimate=pl.CostEstimate(flops=10**8, bytes_accessed=4 * 10**6, transcendentals=2000),
        name="delta_readout",
    )(state, read, rmap, gain)


def adjoint_kernel(
    keep_ref, gn_ref, read_ref, gain_ref, q_ref, k_ref, wk_ref, go_ref, adj_ref, gain_grad_ref
):
    grad, readout = gn_ref[...], read_ref[...]
    inv = lax.rsqrt(jnp.mean(readout * readout, -1, keepdims=True) + EPSILON)
    scaled = grad * gain_ref[...]
    grad_read = inv * scaled - readout * (inv * inv * inv) * jnp.mean(
        scaled * readout, -1, keepdims=True
    )
    gain_grad_ref[0] = jnp.sum(grad * readout * inv, 0, keepdims=True)
    grad_read = grad_read.astype(BF16)
    go_ref[...] = grad_read
    count = grad.shape[0] // STRETCH
    rows, cols = grid_ids(STRETCH)
    size = grad.shape[1]
    adj = jnp.zeros((size, size), F32)
    for n in range(count - 1, -1, -1):
        part = slice(n * STRETCH, (n + 1) * STRETCH)
        key, query, out = k_ref[part, :], q_ref[part, :], grad_read[part]
        scores = jnp.where(rows >= cols, nt(query, key), 0.0).astype(BF16)
        new_grad = tn(scores, out) + nt(key, adj.astype(BF16))
        adj = (
            adj
            + tn(
                jnp.concatenate([out, (-new_grad).astype(BF16)], 0),
                jnp.concatenate([query, wk_ref[part, :]], 0),
            )
        ) * keep_ref[n]
    adj_ref[0] = adj.astype(BF16)


def adjoint_call(keep, grad_normal, readout, gain, queries, keys, wkeys, heads):
    tok, width = readout.shape
    size = width // heads
    block = pl.BlockSpec((tok, size), lambda h: (0, h))
    return pl.pallas_call(
        adjoint_kernel,
        grid=(heads,),
        in_specs=[
            pl.BlockSpec(memory_space=pltpu.SMEM),
            block, block,
            pl.BlockSpec((1, size), lambda h: (0, 0)),
            block, block, block,
        ],
        out_specs=[
            block,
            pl.BlockSpec((1, size, size), lambda h: (h, 0, 0)),
            pl.BlockSpec((1, 1, size), lambda h: (h, 0, 0)),
        ],
        out_shape=[
            jax.ShapeDtypeStruct((tok, width), BF16),
            jax.ShapeDtypeStruct((heads, size, size), BF16),
            jax.ShapeDtypeStruct((heads, 1, size), F32),
        ],
        compiler_params=pltpu.CompilerParams(vmem_limit_bytes=VMEM_LIMIT),
        cost_estimate=pl.CostEstimate(flops=5 * 10**8, bytes_accessed=6 * 10**6, transcendentals=0),
        name="delta_adjoint",
    )(keep, grad_normal, readout, gain, queries, keys, wkeys)


def backward_kernel(
    keep_ref, din_ref, min_ref, pre_ref, go_ref, q_ref, k_ref, v_ref, inv_ref, wk_ref,
    nv_ref, np_ref, rate_ref, allow_ref,
    eq_ref, ek_ref, ev_ref, cq_ref, ck_ref, cv_ref,
    gext_ref, gconv_ref, grate_ref,
    gq_buf, gk_buf, gv_buf,
):
    head = pl.program_id(0)
    size = q_ref.shape[1]
    tok = q_ref.shape[0]
    count = tok // STRETCH
    rows, cols = grid_ids(STRETCH)
    rate = column_of(rate_ref[...], head)
    low_in = min_ref[0]
    adj = din_ref[0].astype(F32)
    grate_parts = [None] * count
    for n in range(count - 1, -1, -1):
        part = slice(n * STRETCH, (n + 1) * STRETCH)
        key, query, value, out = k_ref[part, :], q_ref[part, :], v_ref[part, :], go_ref[part, :]
        beta = rate[part]
        pre = pre_ref[0, n]
        state = (nn(low_in, pre[size:]) + pre[:size].astype(F32)).astype(BF16)
        new = (nt(np_ref[part, :], low_in) + nv_ref[part, :].astype(F32)).astype(BF16)
        low_adj = adj.astype(BF16)
        gram_both = nt(jnp.concatenate([key, query], 0), key)
        gram = gram_both[:STRETCH]
        scores = jnp.where(rows >= cols, gram_both[STRETCH:], 0.0).astype(BF16)
        new_grad = tn(scores, out) + nt(key, low_adj)
        low_new_grad = new_grad.astype(BF16)
        adj = (
            adj
            + tn(
                jnp.concatenate([out, -low_new_grad], 0),
                jnp.concatenate([query, wk_ref[part, :]], 0),
            )
        ) * keep_ref[n]
        grad_b = tn(inv_ref[0, part, :], low_new_grad)
        both = nt(jnp.concatenate([out, grad_b.astype(BF16)], 0), new)
        grad_scores = jnp.where(rows >= cols, both[:STRETCH], 0.0).astype(BF16)
        grad_low = jnp.where(rows > cols, -both[STRETCH:], 0.0)
        left = value.astype(F32) - nt(key, state)
        grate_parts[n] = jnp.sum(grad_low * gram, -1, keepdims=True) + jnp.sum(
            grad_b * left, -1, keepdims=True
        )
        grad_v = beta * grad_b
        grad_gram = beta * grad_low
        symmetric = (grad_gram + grad_gram.T).astype(BF16)
        by_state = nn(jnp.concatenate([out, -grad_v.astype(BF16)], 0), state)
        gq_buf[part, :] = by_state[:STRETCH] + nn(grad_scores, key)
        gk_buf[part, :] = (
            by_state[STRETCH:]
            + tn(grad_scores, query)
            + nn(jnp.concatenate([new, symmetric], 1), jnp.concatenate([low_adj, key], 0))
        )
        gv_buf[part, :] = grad_v
    grate = jnp.concatenate(grate_parts, 0)
    lanes = lax.broadcasted_iota(jnp.int32, grate_ref.shape, 1)
    before = jnp.where(head == 0, jnp.zeros(grate_ref.shape, F32), grate_ref[...])
    grate_ref[...] = jnp.where(lanes == head, grate, before)
    allow_all = allow_ref[...]
    allow = [allow_all[:, tap : tap + 1] for tap in range(cq_ref.shape[0])]
    zeros = jnp.zeros((HALO, size), F32)
    for i, (ext, conv_ref, buf) in enumerate(
        ((eq_ref, cq_ref, gq_buf), (ek_ref, ck_ref, gk_buf), (ev_ref, cv_ref, gv_buf))
    ):
        shifted, mixed, conv = mix_rows(ext, conv_ref, allow)
        sig = jax.nn.sigmoid(mixed)
        grad = buf[...]
        if i < 2:
            raw = mixed * sig
            inv = lax.rsqrt(jnp.sum(raw * raw, -1, keepdims=True) + EPSILON)
            grad = inv * grad - raw * (inv * inv * inv) * jnp.sum(grad * raw, -1, keepdims=True)
        grad = grad * (sig * (1.0 + mixed * (1.0 - sig)))
        total = None
        for tap in range(conv.shape[0]):
            gconv_ref[i, tap : tap + 1, :] = jnp.sum(grad * shifted[tap], 0, keepdims=True)
            term = jnp.concatenate([zeros, grad * (conv[tap : tap + 1] * allow[tap])], 0)
            if tap:
                term = pltpu.roll(term, tok + HALO - tap, 0)
            total = term if total is None else total + term
        gext_ref[i] = total.astype(BF16)


def backward_call(
    keep, state_grad, state, prefix, grad_read, queries, keys, values, invs, wkeys,
    new_v, new_p, rate, allow, ext, conv, heads,
):
    tok, width = queries.shape
    size = width // heads
    count = tok // STRETCH
    taps = conv.shape[0]
    rows = ext.shape[0]
    block = pl.BlockSpec((tok, size), lambda h: (0, h))
    square = pl.BlockSpec((1, size, size), lambda h: (h, 0, 0))

    def third(i, r):
        return pl.BlockSpec((r, size), lambda h: (0, h + i * heads))

    return pl.pallas_call(
        backward_kernel,
        grid=(heads,),
        in_specs=[
            pl.BlockSpec(memory_space=pltpu.SMEM),
            square, square,
            pl.BlockSpec((1, count, 2 * size, size), lambda h: (h, 0, 0, 0)),
            block, block, block, block,
            pl.BlockSpec((1, tok, STRETCH), lambda h: (h, 0, 0)),
            block, block, block,
            pl.BlockSpec((tok, heads), lambda h: (0, 0)),
            pl.BlockSpec((tok, taps), lambda h: (0, 0)),
            third(0, rows), third(1, rows), third(2, rows),
            third(0, taps), third(1, taps), third(2, taps),
        ],
        out_specs=[
            pl.BlockSpec((3, rows, size), lambda h: (0, 0, h)),
            pl.BlockSpec((3, taps, size), lambda h: (0, 0, h)),
            pl.BlockSpec((tok, heads), lambda h: (0, 0)),
        ],
        out_shape=[
            jax.ShapeDtypeStruct((3, rows, width), BF16),
            jax.ShapeDtypeStruct((3, taps, width), F32),
            jax.ShapeDtypeStruct((tok, heads), F32),
        ],
        scratch_shapes=[pltpu.VMEM((tok, size), F32)] * 3,
        compiler_params=pltpu.CompilerParams(vmem_limit_bytes=VMEM_LIMIT),
        cost_estimate=pl.CostEstimate(flops=2 * 10**9, bytes_accessed=12 * 10**6, transcendentals=10**6),
        name="delta_backward",
    )(
        keep, state_grad, state, prefix, grad_read, queries, keys, values, invs, wkeys,
        new_v, new_p, rate, allow, ext, ext, ext, conv, conv, conv,
    )


def silu_slope(pre_act, sig_value):
    return sig_value * (1.0 + pre_act * (1.0 - sig_value))


def norm_back(grad_in, values, inv_rms, gain_vec):
    scaled = grad_in * gain_vec
    return inv_rms * scaled - values * inv_rms**3 * jnp.mean(scaled * values, -1, keepdims=True)


def product(pattern, first, second, kind=F32):
    return jnp.einsum(pattern, first, second, preferred_element_type=F32).astype(kind)


def swap_core(block):
    streams, spans = lax.axis_size("stream"), lax.axis_size("span")
    pairs = [
        (s * spans + p, s * spans + (p ^ 1)) for s in range(streams) for p in range(spans)
    ]
    return lax.ppermute(block, AXES, pairs)


def pair_tokens(block):
    return jnp.concatenate([block, swap_core(block)], 0)


def pair_columns(block, spans):
    core = lax.axis_index("span") % 2
    rows, width = block.shape
    split = block.reshape(rows, spans // 2, 2, width // spans)
    mine = lax.dynamic_index_in_dim(split, core, 2, keepdims=False).reshape(rows, -1)
    theirs = lax.dynamic_index_in_dim(split, 1 - core, 2, keepdims=False).reshape(rows, -1)
    return jnp.concatenate([mine, swap_core(theirs)], 0)


def weight_grad(left, right, spans):
    grad = product("td,te->de", left, right, BF16)
    return grad.reshape(spans // 2, -1, grad.shape[1])


MESH = pl.DeviceIdType.MESH


class Place:
    def __init__(self, streams, spans):
        self.streams, self.spans, self.chips = streams, spans, spans // 2
        self.stream = lax.axis_index("stream")
        self.span = lax.axis_index("span")
        self.chip = lax.div(self.span, 2)
        self.core = lax.rem(self.span, 2)

    def beside(self, step):
        return (self.stream ^ step, self.span)

    def along(self, step):
        return (self.stream, 2 * self.shifted(step) + self.core)

    def shifted(self, step):
        return lax.rem(self.chip + step + self.chips, self.chips)

    def other(self):
        return (self.stream, 2 * self.chip + 1 - self.core)


def greet(places):
    barrier = pltpu.get_barrier_semaphore()
    for target in places:
        pl.semaphore_signal(barrier, inc=1, device_id=target, device_id_type=MESH)
    pl.semaphore_wait(barrier, len(places))


def quarter_of(rows, width, streams):
    if (width // 128) % streams == 0:
        return 1, streams
    return 2, streams // 2


def quarter_index(rows, width, streams, at, piece=0, pieces=1):
    down, across = quarter_of(rows, width, streams)
    r, c = rows // down, width // across
    row = pl.ds(0, rows) if down == 1 else pl.ds(pl.multiple_of(lax.div(at, across) * r, r), r)
    start = lax.rem(at, across) * c + piece * (c // pieces)
    return row, pl.ds(pl.multiple_of(start, 128), c // pieces)


def copy_to(source, target, send_sem, recv_sem, device):
    return pltpu.make_async_remote_copy(
        src_ref=source, dst_ref=target, send_sem=send_sem, recv_sem=recv_sem,
        device_id=device, device_id_type=MESH,
    )


class Gather:
    def __init__(self, place, shards, fulls, sems):
        self.place, self.shards, self.fulls = place, shards, fulls
        self.sems = sems
        self.units = []
        for w, shard in enumerate(shards):
            rows, width = shard.shape
            _, across = quarter_of(rows, width, place.streams)
            pieces = 2 if (width // across) % 256 == 0 else 1
            for piece in range(pieces):
                self.units.append((w, piece, pieces))

    @staticmethod
    def sem_shapes(shapes, streams, spans):
        units = 0
        for rows, width in shapes:
            _, across = quarter_of(rows, width, streams)
            units += 2 if (width // across) % 256 == 0 else 1
        slots = spans // 2
        dma = pltpu.SemaphoreType.DMA
        return [dma((units, slots, 4, 2)), dma((len(shapes), slots, 2)), dma((len(shapes),))]

    def part(self, unit, at, span=None):
        w, piece, pieces = self.units[unit]
        rows, width = self.shards[w].shape
        index = quarter_index(rows, width, self.place.streams, at, piece, pieces)
        if span is None:
            return self.shards[w].at[index]
        return self.fulls[w].at[(span,) + index]

    def source_span(self, k):
        return 2 * self.place.shifted(-k) + self.place.core

    def wire(self, unit, k, kind, span, at, device, source=None):
        region = self.part(unit, at, span)
        return copy_to(
            region if source is None else source, region,
            self.sems[0].at[unit, k, kind, 0], self.sems[0].at[unit, k, kind, 1], device,
        )

    def along(self, unit, k):
        p = self.place
        return self.wire(
            unit, k, 0, p.span, p.stream, p.along(k), self.part(unit, p.stream)
        )

    def along_wait(self, unit, k):
        p = self.place
        self.wire(unit, k, 0, self.source_span(k), p.stream, p.along(k)).wait_recv()

    def sideways(self, unit, k, step):
        p = self.place
        return self.wire(unit, k, step, self.source_span(k), p.stream, p.beside(step))

    def sideways_wait(self, unit, k, step):
        p = self.place
        self.wire(
            unit, k, step, self.source_span(k), p.stream ^ step, p.beside(step)
        ).wait_recv()

    def corner(self, unit, k):
        p = self.place
        first, second = (1, 2) if unit % 2 == 0 else (2, 1)
        return self.wire(
            unit, k, 3, self.source_span(k), p.stream ^ first, p.beside(second)
        )

    def corner_wait(self, unit, k):
        p = self.place
        self.wire(unit, k, 3, self.source_span(k), p.stream ^ 3, p.beside(1)).wait_recv()

    def across(self, w, k):
        p = self.place
        span = p.span if k == 0 else self.source_span(k)
        region = self.fulls[w].at[span]
        return copy_to(
            self.shards[w] if k == 0 else region, region,
            self.sems[1].at[w, k, 0], self.sems[1].at[w, k, 1], p.other(),
        )

    def across_wait(self, w, k):
        p = self.place
        span = 2 * p.shifted(-k) + 1 - p.core
        region = self.fulls[w].at[span]
        copy_to(
            region, region, self.sems[1].at[w, k, 0], self.sems[1].at[w, k, 1], p.other()
        ).wait_recv()

    def own(self, w):
        return pltpu.make_async_copy(
            self.shards[w], self.fulls[w].at[self.place.span], self.sems[2].at[w]
        )

    def neighbours(self):
        p = self.place
        return (
            [p.along(k) for k in range(1, p.chips)] + [p.beside(1), p.beside(2), p.other()]
        )

    def steps(self):
        p = self.place
        slots = range(1, p.chips)
        count = len(self.units)
        ends = {}
        for unit, (w, piece, pieces) in enumerate(self.units):
            if piece == pieces - 1:
                ends[unit] = w
        steps = []

        def begin(unit):
            w, piece, pieces = self.units[unit]
            for k in slots:
                self.along(unit, k).start()
            if piece == 0:
                self.across(w, 0).start()
                self.own(w).start()

        def beside(unit, k):
            self.along_wait(unit, k)
            self.sideways(unit, k, 1).start()
            self.sideways(unit, k, 2).start()

        def turn(unit, k):
            self.sideways_wait(unit, k, 1 if unit % 2 == 0 else 2)
            self.corner(unit, k).start()

        def close(w, k):
            for unit, (owner, _, _) in enumerate(self.units):
                if owner == w:
                    self.sideways_wait(unit, k, 2 if unit % 2 == 0 else 1)
                    self.corner_wait(unit, k)
            self.across(w, k).start()

        def finish(w):
            for k in range(p.chips):
                self.across_wait(w, k)
                self.across(w, k).wait_send()
            self.own(w).wait()
            for unit, (owner, _, _) in enumerate(self.units):
                if owner == w:
                    for k in slots:
                        self.along(unit, k).wait_send()
                        self.sideways(unit, k, 1).wait_send()
                        self.sideways(unit, k, 2).wait_send()
                        self.corner(unit, k).wait_send()

        for unit in range(min(2, count)):
            steps.append(functools.partial(begin, unit))
        for turn_at in range(count + 2):
            if turn_at + 2 < count:
                steps.append(functools.partial(begin, turn_at + 2))
            if turn_at < count:
                steps += [functools.partial(beside, turn_at, k) for k in slots]
            if 0 <= turn_at - 1 < count:
                steps += [functools.partial(turn, turn_at - 1, k) for k in slots]
            if turn_at - 2 in ends:
                steps += [functools.partial(close, ends[turn_at - 2], k) for k in slots]
        steps += [functools.partial(finish, w) for w in range(len(self.shards))]
        return steps


def gather_kernel(streams, spans, count, *refs):
    shards, fulls, sems = refs[:count], refs[count : 2 * count], refs[2 * count :]
    place = Place(streams, spans)
    work = Gather(place, shards, fulls, sems)
    greet(work.neighbours())
    for step in work.steps():
        step()


def gather_call(shards, collective_id):
    streams, spans = lax.axis_size("stream"), lax.axis_size("span")
    shapes = [shard.shape for shard in shards]
    outs = pl.pallas_call(
        functools.partial(gather_kernel, streams, spans, len(shards)),
        in_specs=[pl.BlockSpec(memory_space=pl.ANY)] * len(shards),
        out_specs=[pl.BlockSpec(memory_space=pl.ANY)] * len(shards),
        out_shape=[jax.ShapeDtypeStruct((spans,) + s.shape, s.dtype) for s in shards],
        scratch_shapes=Gather.sem_shapes(shapes, streams, spans),
        compiler_params=pltpu.CompilerParams(
            collective_id=collective_id, has_side_effects=True, vmem_limit_bytes=VMEM_LIMIT
        ),
        name="gather_weights",
    )(*shards)
    return outs


class Reduce:
    def __init__(self, place, grads, outs, bufs, sems):
        self.place, self.grads, self.outs, self.bufs, self.sems = place, grads, outs, bufs, sems

    @staticmethod
    def block(shape, streams):
        _, rows, width = shape
        down, across = quarter_of(rows, width, streams)
        return rows // down, width // across

    @staticmethod
    def scratch(shapes, streams):
        out = []
        dma = pltpu.SemaphoreType.DMA
        for shape in shapes:
            chips = shape[0]
            r, c = Reduce.block(shape, streams)
            out += [
                pltpu.VMEM((2, chips, r, c), BF16),
                pltpu.VMEM((2, chips, r, c), BF16),
                pltpu.VMEM((chips, r, c), BF16),
                pltpu.VMEM((chips, r, c), BF16),
                pltpu.VMEM((chips, r, c), BF16),
                pltpu.VMEM((streams, r, c), BF16),
            ]
        n = len(shapes)
        chips = shapes[0][0]
        out += [dma((n, 2, 3, 2)), dma((n, chips, 2)), dma((n, streams, 2))]
        return out

    def turn(self, w, half):
        return (1, 2) if (w + half) % 2 == 0 else (2, 1)

    def chips_of(self, half):
        n = self.place.chips // 2
        return half * n, n

    def region(self, w, half, at):
        _, rows, width = self.grads[w].shape
        start, n = self.chips_of(half)
        return (pl.ds(start, n),) + quarter_index(rows, width, self.place.streams, at)

    def first(self, w, half, slot):
        p = self.place
        a, b = self.turn(w, half)
        start, n = self.chips_of(half)
        at = p.stream ^ a if slot == 0 else p.stream ^ a ^ b
        return copy_to(
            self.grads[w].at[self.region(w, half, at)],
            self.bufs[w][0].at[slot, pl.ds(start, n)],
            self.sems[0].at[w, half, slot, 0], self.sems[0].at[w, half, slot, 1], p.beside(a),
        )

    def second(self, w, half):
        p = self.place
        _, b = self.turn(w, half)
        start, n = self.chips_of(half)
        return copy_to(
            self.bufs[w][1].at[1, pl.ds(start, n)], self.bufs[w][2].at[pl.ds(start, n)],
            self.sems[0].at[w, half, 2, 0], self.sems[0].at[w, half, 2, 1], p.beside(b),
        )

    def third(self, w, k):
        p = self.place
        return copy_to(
            self.bufs[w][3].at[p.shifted(k)], self.bufs[w][4].at[k],
            self.sems[1].at[w, k, 0], self.sems[1].at[w, k, 1], p.along(k),
        )

    def fourth(self, w, step):
        p = self.place
        return copy_to(
            self.bufs[w][5].at[0], self.bufs[w][5].at[step],
            self.sems[2].at[w, step, 0], self.sems[2].at[w, step, 1], p.beside(step),
        )

    def neighbours(self):
        p = self.place
        return [p.along(k) for k in range(1, p.chips)] + [
            p.beside(s) for s in range(1, p.streams)
        ]

    def begin(self, w):
        for half in range(2):
            for slot in (1, 0):
                self.first(w, half, slot).start()

    def add_first(self, w, half):
        p = self.place
        _, b = self.turn(w, half)
        start, n = self.chips_of(half)
        for slot in (1, 0):
            self.first(w, half, slot).wait_recv()
            at = p.stream ^ b if slot else p.stream
            _, row, col = self.region(w, half, at)
            for chip in range(start, start + n):
                self.bufs[w][1][slot, chip] = (
                    self.grads[w][chip, row, col].astype(F32)
                    + self.bufs[w][0][slot, chip].astype(F32)
                ).astype(BF16)
            if slot:
                self.second(w, half).start()

    def add_second(self, w, half):
        start, n = self.chips_of(half)
        self.second(w, half).wait_recv()
        for chip in range(start, start + n):
            self.bufs[w][3][chip] = (
                self.bufs[w][1][0, chip].astype(F32) + self.bufs[w][2][chip].astype(F32)
            ).astype(BF16)

    def spread(self, w):
        for k in range(1, self.place.chips):
            self.third(w, k).start()

    def add_third(self, w):
        p = self.place
        total = self.bufs[w][3][p.chip].astype(F32)
        for k in range(1, p.chips):
            self.third(w, k).wait_recv()
            total = total + self.bufs[w][4][k].astype(F32)
        self.bufs[w][5][0] = total.astype(BF16)
        for step in range(1, p.streams):
            self.fourth(w, step).start()

    def finish(self, w):
        p = self.place
        _, rows, width = self.grads[w].shape
        for step in range(p.streams):
            if step:
                self.fourth(w, step).wait_recv()
            row, col = quarter_index(rows, width, p.streams, p.stream ^ step)
            self.outs[w][row, col] = self.bufs[w][5][step]
        for half in range(2):
            for slot in range(2):
                self.first(w, half, slot).wait_send()
            self.second(w, half).wait_send()
        for k in range(1, p.chips):
            self.third(w, k).wait_send()
        for step in range(1, p.streams):
            self.fourth(w, step).wait_send()

    def steps(self):
        count = len(self.grads)
        steps = [functools.partial(self.begin, w) for w in range(count)]
        for t in range(count + 3):
            if t < count:
                steps += [functools.partial(self.add_first, t, half) for half in range(2)]
            if 0 <= t - 1 < count:
                steps += [functools.partial(self.add_second, t - 1, half) for half in range(2)]
                steps.append(functools.partial(self.spread, t - 1))
            if 0 <= t - 2 < count:
                steps.append(functools.partial(self.add_third, t - 2))
            if 0 <= t - 3 < count:
                steps.append(functools.partial(self.finish, t - 3))
        return steps


def reduce_kernel(streams, spans, count, *refs):
    grads, outs, rest = refs[:count], refs[count : 2 * count], refs[2 * count :]
    bufs = [rest[6 * w : 6 * w + 6] for w in range(count)]
    work = Reduce(Place(streams, spans), grads, outs, bufs, rest[6 * count :])
    greet(work.neighbours())
    for step in work.steps():
        step()


def reduce_call(grads, collective_id):
    streams, spans = lax.axis_size("stream"), lax.axis_size("span")
    shapes = [grad.shape for grad in grads]
    vmem = pl.BlockSpec(memory_space=pltpu.VMEM)
    return pl.pallas_call(
        functools.partial(reduce_kernel, streams, spans, len(grads)),
        in_specs=[vmem] * len(grads),
        out_specs=[vmem] * len(grads),
        out_shape=[jax.ShapeDtypeStruct(s[1:], BF16) for s in shapes],
        scratch_shapes=Reduce.scratch(shapes, streams),
        compiler_params=pltpu.CompilerParams(
            collective_id=collective_id, has_side_effects=True, vmem_limit_bytes=VMEM_LIMIT
        ),
        name="reduce_grads",
    )(*grads)


def chain_kernel(streams, spans, backward, *refs):
    p = Place(streams, spans)
    if backward:
        (adj_ref, p_low, p_high, p_chip, state_ref,
         swap, carry, outgo, sent, swap_sem, hop_sem, back_sem) = refs
    else:
        (map_ref, state_ref, p_low, p_high, p_chip,
         swap, carry, outgo, sent, s_chip, swap_sem, hop_sem, back_sem) = refs
    source = adj_ref if backward else map_ref
    heads, size = source.shape[0], source.shape[2]
    half = heads // 2
    mine = p.core * half
    theirs = (1 - p.core) * half
    ahead, behind = (-1, 1) if backward else (1, -1)
    edge_in = p.chips - 1 if backward else 0
    edge_out = 0 if backward else p.chips - 1
    greet([p.other(), p.along(1), p.along(-1)])
    swap_copy = copy_to(
        source.at[pl.ds(theirs, half)], swap, swap_sem.at[0], swap_sem.at[1], p.other()
    )
    swap_copy.start()
    swap_copy.wait_recv()
    low_core = p.core == 0
    for h in range(half):
        own, got = source[mine + h], swap[h]
        low = jnp.where(low_core, own, got)
        high = jnp.where(low_core, got, own)
        if backward:
            outgo[h] = low.astype(F32) + nt(high, p_low[h])
        else:
            joined = nn(low, high[size:])
            s_chip[h] = joined[:size] + high[:size].astype(F32)
            p_chip[h] = joined[size:].astype(BF16)
            p_low[h] = low[size:]
            p_high[h] = high[size:]
            outgo[h] = low[:size].astype(F32)

    def hop(h):
        return copy_to(
            sent.at[h], carry.at[h], hop_sem.at[h, 0], hop_sem.at[h, 1], p.along(ahead)
        )

    @pl.when(p.chip == edge_in)
    def _():
        carry[...] = jnp.zeros(carry.shape, BF16)

    for h in range(half):

        @pl.when(p.chip != edge_in)
        def _():
            hop(h).wait_recv()

        moved = nt(carry[h], p_chip[h]) + outgo[h] if backward else nn(carry[h], p_chip[h]) + s_chip[h]
        sent[h] = moved.astype(BF16)

        @pl.when(p.chip != edge_out)
        def _():
            hop(h).start()

    for h in range(half):
        state = carry[h]
        if backward:
            low_state = (nt(state, p_high[h]) + jnp.where(low_core, swap[h], source[mine + h]).astype(F32)).astype(BF16)
            keep = jnp.where(low_core, low_state, state)
            give = jnp.where(low_core, state, low_state)
        else:
            high_state = (nn(state, p_low[h]) + outgo[h]).astype(BF16)
            keep = jnp.where(low_core, state, high_state)
            give = jnp.where(low_core, high_state, state)
        state_ref[mine + h] = keep
        sent[half + h] = give
    back = copy_to(
        sent.at[pl.ds(half, half)], state_ref.at[pl.ds(mine, half)],
        back_sem.at[0], back_sem.at[1], p.other(),
    )
    back.start()
    copy_to(
        sent.at[pl.ds(half, half)], state_ref.at[pl.ds(theirs, half)],
        back_sem.at[0], back_sem.at[1], p.other(),
    ).wait_recv()
    back.wait_send()
    swap_copy.wait_send()

    @pl.when(p.chip != edge_out)
    def _():
        for h in range(half):
            hop(h).wait_send()


def chain_call(maps, carried, collective_id):
    streams, spans = lax.axis_size("stream"), lax.axis_size("span")
    backward = carried is not None
    heads, size = maps.shape[0], maps.shape[2]
    half = heads // 2
    vmem = pl.BlockSpec(memory_space=pltpu.VMEM)
    dma = pltpu.SemaphoreType.DMA
    square = jax.ShapeDtypeStruct((half, size, size), BF16)
    state = jax.ShapeDtypeStruct((heads, size, size), BF16)
    scratch = [
        pltpu.VMEM((half,) + maps.shape[1:], BF16),
        pltpu.VMEM((half, size, size), BF16),
        pltpu.VMEM((half, size, size), F32),
        pltpu.VMEM((heads, size, size), BF16),
    ]
    if not backward:
        scratch.append(pltpu.VMEM((half, size, size), F32))
    scratch += [dma((2,)), dma((half, 2)), dma((2,))]
    operands = [maps] + (list(carried) if backward else [])
    return pl.pallas_call(
        functools.partial(chain_kernel, streams, spans, backward),
        in_specs=[vmem] * len(operands),
        out_specs=[vmem] * (1 if backward else 4),
        out_shape=[state] if backward else [state, square, square, square],
        scratch_shapes=scratch,
        compiler_params=pltpu.CompilerParams(
            collective_id=collective_id, has_side_effects=True, vmem_limit_bytes=VMEM_LIMIT
        ),
        name="span_chain",
    )(*operands)


def local(
    tokens, cotangent, doc_stretches, w_qkv, conv_weight, w_beta, beta_bias, norm_attn, norm_head,
    w_out, norm_ffn, w_gate, w_up, w_down,
):
    tok_rows, model_width = tokens.shape[1:]
    heads = beta_bias.shape[0]
    size = model_width // heads
    count = tok_rows // STRETCH
    span_count = lax.axis_size("span")
    place = lax.axis_index("span")
    taps = conv_weight.shape[0]

    small = jnp.concatenate(
        [x.reshape(-1) for x in (conv_weight, w_beta, norm_attn, norm_ffn, norm_head)]
    )
    small_len = small.shape[0]
    small = jnp.pad(small, (0, 16 * 512 - small_len)).reshape(16, 512)
    full_qkv, smalls = gather_call([w_qkv, small], 1)
    full_out, full_gate, full_up, full_down = gather_call([w_out, w_gate, w_up, w_down], 2)
    full_qkv, full_out, full_gate, full_up, full_down = (
        w.reshape(-1, w.shape[2]) for w in (full_qkv, full_out, full_gate, full_up, full_down)
    )
    smalls = smalls.reshape(span_count, -1)

    def small_part(shape, start):
        length = 1
        for dim in shape:
            length *= dim
        return smalls[:, start : start + length].reshape((span_count,) + shape), start + length

    at = 0
    full_conv, at = small_part(conv_weight.shape, at)
    full_beta, at = small_part(w_beta.shape, at)
    gain_attn, at = small_part(norm_attn.shape, at)
    gain_ffn, at = small_part(norm_ffn.shape, at)
    gain_head, at = small_part(norm_head.shape, at)
    full_conv = jnp.swapaxes(full_conv, 0, 1).reshape(taps, -1)
    full_beta = full_beta.reshape(-1, heads)
    attn_gain = gain_attn.reshape(-1).astype(F32)
    ffn_gain = gain_ffn.reshape(-1).astype(F32)
    head_gain = gain_head.reshape(1, -1).astype(F32)

    stretch_ids = place * count + jnp.arange(count, dtype=jnp.int32)
    doc_lengths = doc_stretches[0]
    doc_begins = jnp.cumsum(doc_lengths) - doc_lengths
    stretch_start = jnp.any(stretch_ids[:, None] == doc_begins[None, :], axis=1).astype(F32)
    stretch_keep = 1.0 - stretch_start
    token_start = jnp.repeat(stretch_start, STRETCH)
    token_offset = jnp.arange(tok_rows, dtype=jnp.int32) % STRETCH
    allow = jnp.stack(
        [1.0 - token_start * (token_offset < tap).astype(F32) for tap in range(taps)], 1
    )

    ends = tokens[0, tok_rows - HALO :]
    before = lax.ppermute(
        ends, "span", [(i, i + 1) for i in range(span_count - 1)]
    )
    inputs_ext = jnp.concatenate([before, tokens[0]], 0).astype(F32)
    inv_ext = lax.rsqrt(jnp.mean(inputs_ext * inputs_ext, -1, keepdims=True) + EPSILON)
    normed_ext = (inputs_ext * inv_ext * attn_gain).astype(BF16)
    inputs_f, inv_first, normed = inputs_ext[HALO:], inv_ext[HALO:], normed_ext[HALO:]
    projected = jnp.dot(normed_ext, full_qkv, preferred_element_type=F32).astype(BF16)
    strength = jax.nn.sigmoid(
        jnp.dot(normed, full_beta, preferred_element_type=F32) + beta_bias
    )
    (
        queries, keys, values, invs, wkeys, prefix, device_map, read_local, read_map, new_v, new_p
    ) = local_call(stretch_keep, projected, full_conv, strength, allow, heads)
    state_in, p_low, p_high, p_chip = chain_call(device_map, None, 3)
    readout, normal_heads = readout_call(state_in, read_local, read_map, head_gain)

    middle = inputs_f + jnp.dot(normal_heads, full_out, preferred_element_type=F32)
    inv_second = lax.rsqrt(jnp.mean(middle * middle, -1, keepdims=True) + EPSILON)
    normed_ffn = (middle * inv_second * ffn_gain).astype(BF16)
    gate = jnp.dot(normed_ffn, full_gate, preferred_element_type=F32)
    up_part = jnp.dot(normed_ffn, full_up, preferred_element_type=F32)
    gate_sig = jax.nn.sigmoid(gate)
    gate_act = gate * gate_sig
    hidden = (gate_act * up_part).astype(BF16)
    grad_branch = cotangent[0]
    pair_cot = pair_tokens(grad_branch)
    half_down = weight_grad(pair_columns(hidden, span_count), pair_cot, span_count)
    grad_hidden = product("td,fd->tf", grad_branch, full_down)
    grad_gate_in = (grad_hidden * up_part * silu_slope(gate, gate_sig)).astype(BF16)
    grad_up_in = (grad_hidden * gate_act).astype(BF16)
    grad_nffn = product("tf,df->td", grad_gate_in, full_gate) + product(
        "tf,df->td", grad_up_in, full_up
    )
    pair_ffn = pair_columns(normed_ffn, span_count)
    half_gate = weight_grad(pair_ffn, pair_tokens(grad_gate_in), span_count)
    half_up = weight_grad(pair_ffn, pair_tokens(grad_up_in), span_count)
    result = middle + jnp.dot(hidden, full_down, preferred_element_type=F32)

    grad_norm_ffn = jnp.sum(grad_nffn * middle * inv_second, 0)
    grad_middle = grad_branch.astype(F32) + norm_back(grad_nffn, middle, inv_second, ffn_gain)
    grad_attn_in = grad_middle.astype(BF16)
    grad_normal = product("td,kd->tk", grad_attn_in, full_out)
    grad_read, device_adjoint, head_grads = adjoint_call(
        stretch_keep, grad_normal, readout, head_gain, queries, keys, wkeys, heads
    )
    pair_heads = pair_columns(normal_heads, span_count)
    half_out = weight_grad(pair_heads, pair_tokens(grad_attn_in), span_count)
    (state_grad,) = chain_call(device_adjoint, (p_low, p_high, p_chip), 4)
    grad_ext, grad_conv, grad_strength = backward_call(
        stretch_keep, state_grad, state_in, prefix, grad_read, queries, keys, values, invs, wkeys,
        new_v, new_p, strength, allow, projected, full_conv, heads,
    )
    pair_normed = pair_columns(normed_ext, span_count)
    half_q, half_k, half_v = (
        weight_grad(pair_normed, pair_tokens(grad_ext[i]), span_count) for i in range(3)
    )

    grad_logit = grad_strength * strength * (1.0 - strength)
    grad_logit_low = grad_logit.astype(BF16)
    grad_w_beta = product("td,th->dh", normed, grad_logit_low)
    grad_normed_ext = sum(
        product("te,de->td", grad_ext[i], full_qkv[:, i * model_width : (i + 1) * model_width])
        for i in range(3)
    )
    halo_back = lax.ppermute(
        grad_normed_ext[:HALO].astype(BF16), "span", [(i, i - 1) for i in range(1, span_count)]
    )
    grad_normed = (
        grad_normed_ext[HALO:]
        + product("th,dh->td", grad_logit_low, full_beta)
        + jnp.pad(halo_back.astype(F32), ((tok_rows - HALO, 0), (0, 0)))
    )
    grad_norm_attn = jnp.sum(grad_normed * inputs_f * inv_first, 0)
    grad_tokens = grad_middle + norm_back(grad_normed, inputs_f, inv_first, attn_gain)

    def by_span(array):
        return array.reshape(span_count, -1)

    grad_conv = jnp.swapaxes(grad_conv, 0, 1).reshape(taps, span_count, -1)
    packed = jnp.concatenate(
        [
            by_span(jnp.swapaxes(grad_conv, 0, 1)),
            by_span(grad_w_beta),
            by_span(grad_norm_attn),
            by_span(grad_norm_ffn),
            by_span(jnp.sum(head_grads, (0, 1))),
            jnp.broadcast_to(jnp.sum(grad_logit, 0)[None], (span_count, heads)),
        ],
        1,
    )
    packed = jnp.pad(packed, ((0, 0), (0, 16 * 512 - packed.shape[1])))
    packed = packed.astype(BF16).reshape(span_count // 2, 2, 16, 512)
    core = place % 2
    half_small = (
        lax.dynamic_index_in_dim(packed, core, 1, keepdims=False).astype(F32)
        + swap_core(lax.dynamic_index_in_dim(packed, 1 - core, 1, keepdims=False)).astype(F32)
    ).astype(BF16)
    parts = reduce_call(
        [half_down, half_gate, half_up, half_out, half_q, half_k, half_v, half_small], 5
    )
    part_down, part_gate, part_up, part_out = (x.astype(F32) for x in parts[:4])
    part_qkv = jnp.concatenate([x.astype(F32) for x in parts[4:7]], 1)
    part_small = parts[7].reshape(-1).astype(F32)
    sums = []
    at = 0
    for like in (conv_weight, w_beta, norm_attn, norm_ffn, norm_head, beta_bias):
        sums.append(part_small[at : at + like.size].reshape(like.shape))
        at += like.size

    return (
        result.astype(BF16)[None],
        grad_tokens[None],
        part_qkv,
        sums[0],
        sums[1],
        sums[5],
        sums[2],
        sums[4],
        part_out,
        sums[3],
        part_gate,
        part_up,
        part_down,
    )


def solution(mesh):
    in_specs = (
        P("stream", "span", None),
        P("stream", "span", None),
        P("stream", None),
        P("span", None),
        P(None, "span"),
        P("span", None),
        P(),
        P("span"),
        P("span"),
        P("span", None),
        P("span"),
        P("span", None),
        P("span", None),
        P("span", None),
    )
    out_specs = (
        P("stream", "span", None),
        P("stream", "span", None),
        P("span", None),
        P(None, "span"),
        P("span", None),
        P(),
        P("span"),
        P("span"),
        P("span", None),
        P("span"),
        P("span", None),
        P("span", None),
        P("span", None),
    )
    return jax.shard_map(local, mesh=mesh, in_specs=in_specs, out_specs=out_specs, check_vma=False)
```

time: 1420 us -> 562 us (0.40)
  waiting for transfers between devices: 669 us -> 0.04 us
  Pallas kernels: 0 us -> 418 us
  other arithmetic: 241 us -> 19.5 us
  matrix products: 234 us -> 64.2 us
  blocking collectives: 99.9 us -> 0 us
  local copies, waits for them, and re-layouts: 139 us -> 42.2 us
  between operations: 17.8 us -> 1.84 us
    pallas_call x0 -> x9, Pallas kernels: none -> 418 us  [the longest x1 170 us: reduce_call(): pl.pallas_call(functools.partial(reduce_kernel, streams, spans, len(grads...]
    reduce_scatter x6 -> x0, waiting for transfers between devices: 373 us -> none  [the longest x1 128 us: local(): lax.psum_scatter(grad_qkv, 'span', scatter_dimension=0, tiled=True)]
    all_gather x8 -> x0, waiting for transfers between devices: 193 us -> none  [the longest x1 54.7 us: local(): lax.all_gather(w_down, 'span', axis=0, tiled=True)]
    another operation x8 -> x2, other arithmetic: 163 us -> 0.84 us  [the longest x5 162 us: local(): jax.scipy.linalg.solve_triangular(unit_lower, rate_c[..., None] * key_f,...]
    dot_general x65 -> x22, matrix products: 225 us -> 64.2 us  [the longest x16 43.4 us: product(): jnp.einsum(pattern, first, second, preferred_element_type=F32).astype(kind)]
    psum x1 -> x0, waiting for transfers between devices: 77.5 us -> none  [local(): lax.psum(part_qkv.astype(jnp.bfloat16), 'stream').astype(jnp.float32)]
    all_gather x4 -> x0, blocking collectives: 49.3 us -> none  [the longest x1 14.2 us: local(): lax.all_gather(conv_weight, 'span', axis=1, tiled=True)]
    dynamic_slice x34 -> x4, local copies, waits for them, and re-layouts: 50 us -> 6.77 us  [the longest x3 6.57 us: pair_columns(): lax.dynamic_index_in_dim(split, core, 2, keepdims=False).reshape(rows, -1)]
  transfers between devices with their start and end apart: 18 -> 14, of which waited for: 12 -> 0; matrix products, arithmetic and copies ran while one was open for 20% -> 13% of each run, Pallas kernels for 0% -> 23%
where the time goes in v1:
time: 562 us; the launch traced here: 554 us
  Pallas kernels  418 us (74%)
  matrix products  64.2 us (11%)
  local copies, waits for them, and re-layouts  42.2 us (8%)
  other arithmetic  19.5 us (3%)
  starting transfers between devices  7.82 us (1%)
    pallas_call x1, Pallas kernels, reduce_call(): pl.pallas_call(functools.partial(reduce_kernel, streams, spans, len(grads...  170 us
    pallas_call x2, Pallas kernels, gather_call(): pl.pallas_call(functools.partial(gather_kernel, streams, spans, len(shard...  129 us
    dot_general x16, matrix products, product(): jnp.einsum(pattern, first, second, preferred_element_type=F32).astype(kind)  43.4 us
    pallas_call x2, Pallas kernels, chain_call(): pl.pallas_call(functools.partial(chain_kernel, streams, spans, backward),...  38.4 us
    pallas_call x1, Pallas kernels, local_call(): pl.pallas_call(local_kernel, grid=(heads,), in_specs=[pl.BlockSpec(memory...  32.7 us
    pallas_call x1, Pallas kernels, backward_call(): pl.pallas_call(backward_kernel, grid=(heads,), in_specs=[pl.BlockSpec(mem...  27.2 us
    unnamed x112, local copies, waits for them, and re-layouts  14.4 us
    pallas_call x1, Pallas kernels, adjoint_call(): pl.pallas_call(adjoint_kernel, grid=(heads,), in_specs=[pl.BlockSpec(memo...  14.2 us
  transfers between devices with their start and end apart: 14, of which 0 were waited for; matrix products, arithmetic and copies ran while one was open for 13% of the time, Pallas kernels for 23%

profile of v1, /device:TPU:0, one launch (start us, length us, event | category | flops | bytes accessed | tf_op | source)
XLA Modules:
  0.0 553.6 jit_solution(17632085390477192513)
XLA Ops:
  1.4 2.3 collective-permute-start
  3.8 0.8 reduce-window_clone.1
  6.0 0.8 copy.63
  8.0 0.8 dynamic-update-slice.4
  8.8 0.8 dynamic-update-slice.5
  9.6 0.8 dynamic-update-slice.6
  11.1 39.1 %gather_weights.2 = (bf16[8,128,3072]{2,1,0:T(8,128)(2,1)}, bf16[8,16,512]{2,1,0:T(8,128)(2,1)}) custom-call(bf16[128,3072]{1,0:T(8,128)(2,1)} %refs_0_.2, bf16[16,512]{1,0:T(8,128)(2,1)} %reshape.362.refs_1_), custom_call_target="tpu_custom_call" | custom-call | tf_op jit(solution)/shard_map/gather_weights/pallas_call | solution.py:676
  50.2 1.0 copy.85
  51.5 1.4 concatenate.66
  53.2 0.8 copy.65.allow_ref
  55.2 0.9 copy.73
  56.1 89.5 %gather_weights.3 = (bf16[8,128,1024]{2,1,0:T(8,128)(2,1)}, bf16[8,128,2816]{2,1,0:T(8,128)(2,1)}, bf16[8,128,2816]{2,1,0:T(8,128)(2,1)}, bf16[8,352,1024]{2,1,0:T(8,128)(2,1)}) custom-call(bf16[128,1024]{1,0:T(8,128)(2,1)} %refs_0_.3, bf16[128,2816]{1,0:T(8,128)(2,1)} %refs_1_.1, bf16[128,2816]{1,0:T(8,128)(2,1)} %refs_2_.1, bf16[352,1024]{1,0:T(8,128)(2,1)} %refs_3_.1), custom_call_target="tpu_custom_call" | custom-call | tf_op jit(solution)/shard_map/gather_weights/pallas_call | solution.py:676
  146.2 6.2 %convolution_convert_fusion.2.eq_ref.ek_ref.ev_ref = bf16[272,3072]{1,0:T(8,128)(2,1)} fusion(bf16[272,1024]{1,0:T(8,128)(2,1)S(1)} %multiply_convert_fusion.4, bf16[1024,3072]{1,0:T(8,128)(2,1)} %bitcast.139), kind=kOutput, calls=%fused_computation.3 | convolution fusion | flops 1712111616 | bytes 8519680 | tf_op jit(solution)/shard_map/dot_general | solution.py:1056
  152.3 1.0 fusion.27.rate_ref
  153.3 32.7 %delta_local.1 = (bf16[256,1024]{1,0:T(8,128)(2,1)}, bf16[256,1024]{1,0:T(8,128)(2,1)}, bf16[256,1024]{1,0:T(8,128)(2,1)}, bf16[8,256,64]{2,1,0:T(8,128)(2,1)}, ...) custom-call(f32[4]{0:T(128)} %broadcast_subtract_fusion.keep_ref, ...), custom_call_target="tpu_custom_call" | custom-call | flops 2000000000 | bytes 10000000 | tf_op jit(solution)/shard_map/delta_local/pallas_call | solution.py:152
  186.0 13.3 %span_chain.2 = (bf16[8,128,128]{2,1,0:T(8,128)(2,1)}, bf16[4,128,128]{2,1,0:T(8,128)(2,1)}, bf16[4,128,128]{2,1,0:T(8,128)(2,1)}, bf16[4,128,128]{2,1,0:T(8,128)(2,1)}) custom-call(bf16[8,256,128]{2,1,0:T(8,128)(2,1)} %get-tuple-element.52.refs_0_), custom_call_target="tpu_custom_call" | custom-call | tf_op jit(solution)/shard_map/span_chain/pallas_call | solution.py:982
  199.3 6.3 %delta_readout.1 = (f32[256,1024]{1,0:T(8,128)}, bf16[256,1024]{1,0:T(8,128)(2,1)}) custom-call(bf16[8,128,128]{2,1,0:T(8,128)(2,1)} %get-tuple-element.53.state_ref.min_ref, f32[256,1024]{1,0:T(8,128)} %get-tuple-element.54.read_ref, bf16[256,1024]{1,0:T(8,128)(2,1)} %get-tuple-element.55.rmap_ref, f32[1,128]{1,0:T(1,128)} %reshape.399.gain_ref), custom_call_target="tpu_custom_call" | custom-call | flops 100000000 | bytes 4000000 | tf_op jit(solution)/shard_map/delta_readout/pallas_call | solution.py:200
  205.6 1.8 multiply_reduce_fusion.5
  207.7 4.6 fusion.68
  212.3 1.7 fusion.67
  214.1 3.9 multiply_convert_fusion
  218.0 1.7 fusion.69
  219.7 2.4 multiply_reduce_fusion.1
  222.1 1.5 fusion.65
  223.6 2.8 fusion.70.gn_ref
  226.4 14.2 %delta_adjoint.1 = (bf16[256,1024]{1,0:T(8,128)(2,1)}, bf16[8,128,128]{2,1,0:T(8,128)(2,1)}, f32[8,1,128]{2,1,0:T(1,128)}) custom-call(f32[4]{0:T(128)} %broadcast_subtract_fusion.keep_ref, f32[256,1024]{1,0:T(8,128)} %fusion.70.gn_ref, f32[256,1024]{1,0:T(8,128)} %get-tuple-element.61.read_ref, f32[1,128]{1,0:T(1,128)} %reshape.399.gain_ref, ...), custom_call_target="tpu_custom_call" | custom-call | flops 500000000 | bytes 6000000 | tf_op jit(solution)/shard_map/delta_adjoint/pallas_call | solution.py:254
  240.6 25.1 %span_chain.3.din_ref = bf16[8,128,128]{2,1,0:T(8,128)(2,1)} custom-call(bf16[8,128,128]{2,1,0:T(8,128)(2,1)} %get-tuple-element.65.refs_0_, bf16[4,128,128]{2,1,0:T(8,128)(2,1)} %get-tuple-element.66.refs_1_, bf16[4,128,128]{2,1,0:T(8,128)(2,1)} %get-tuple-element.67.refs_2_, bf16[4,128,128]{2,1,0:T(8,128)(2,1)} %get-tuple-element.68.refs_3_), custom_call_target="tpu_custom_call" | custom-call | tf_op jit(solution)/shard_map/span_chain/pallas_call | solution.py:982
  265.8 27.2 %delta_backward.1 = (bf16[3,272,1024]{2,1,0:T(8,128)(2,1)}, f32[3,4,1024]{2,1,0:T(4,128)}, f32[256,8]{1,0:T(8,128)}) custom-call(f32[4]{0:T(128)} %broadcast_subtract_fusion.keep_ref, bf16[8,128,128]{2,1,0:T(8,128)(2,1)} %span_chain.3.din_ref, bf16[8,128,128]{2,1,0:T(8,128)(2,1)} %get-tuple-element.53.state_ref.min_ref, ...), custom_call_target="tpu_custom_call" | custom-call | flops 2000000000 | bytes 12000000 | tf_op jit(solution)/shard_map/delta_backward/pallas_call | solution.py:377
  293.0 3.7 fusion.9
  296.7 3.4 fusion.7
  300.1 1.3 slice_bitcast_fusion
  301.8 1.2 reshape.381
  302.9 1.4 reshape.376
  304.3 2.5 copy.67
  306.9 5.7 %fusion.23 = bf16[1,256,1024]{2,1,0:T(8,128)(2,1)} fusion(f32[256,1024]{1,0:T(8,128)S(1)} %get-tuple-element.173, bf16[256,2816]{1,0:T(8,128)(2,1)} %get-tuple-element.147, bf16[2816,1024]{1,0:T(8,128)(2,1)} %bitcast.174), kind=kOutput, calls=%fused_computation.36 | convolution fusion | flops 1476919296 | bytes 8781824 | tf_op jit(solution)/shard_map/dot_general | solution.py:1086
  314.0 2.6 fusion.19
  317.3 1.3 collective-permute-start.1
  319.2 1.1 collective-permute-start.12
  320.4 1.4 multiply_convert_fusion.3
  323.6 3.3 constant_dynamic-slice_fusion.3
  326.9 1.9 copy.83
  329.3 1.2 constant_dynamic-slice_fusion.7
  331.0 2.1 constant_dynamic-slice_fusion.5
  333.3 0.9 reshape.392
  334.3 1.9 copy.82
  336.2 1.9 copy.81
  338.0 1.3 copy.80
  339.4 2.9 multiply_reduce_fusion.2
  342.3 0.8 concatenate.72
  344.1 2.6 add_bitcast_fusion
  348.4 1.0 constant_dynamic-update-slice_fusion
  349.5 3.1 convolution_convert_fusion.7
  353.0 3.0 convolution_convert_fusion.4
  356.3 2.0 convolution_convert_fusion.5
  358.7 2.0 convolution_convert_fusion.6
  360.7 3.2 convolution_convert_fusion.3
  363.9 3.3 convolution_convert_fusion
  367.2 3.3 convolution_convert_fusion.1
  370.5 170.5 %reduce_grads.1 = (bf16[352,1024]{1,0:T(8,128)(2,1)}, bf16[128,2816]{1,0:T(8,128)(2,1)}, bf16[128,2816]{1,0:T(8,128)(2,1)}, bf16[128,1024]{1,0:T(8,128)(2,1)}, b...) custom-call(bf16[4,352,1024]{2,1,0:T(8,128)(2,1)} %bitcast.128, ...), custom_call_target="tpu_custom_call" | custom-call | tf_op jit(solution)/shard_map/reduce_grads/pallas_call | solution.py:861
  544.8 2.4 convert_element_type.178
  547.2 1.2 convert_element_type.179
  548.4 1.3 convert_element_type.180
  549.7 0.8 convert_element_type.177
  551.9 1.3 maximum_convert_fusion
  (188 shorter events, 21.7 us)
Async XLA Ops:
  1.4 144.3 %collective-permute-start = (bf16[16,1024]{1,0:T(8,128)(2,1)S(1)}, bf16[16,1024]{1,0:T(8,128)(2,1)S(1)}, u32[]{:S(2)}, u32[]{:S(2)}) collective-permute-start(bf16[16,1024]{1,0:T(8,128)(2,1)S(1)} %slice_bitcast_fusion.3), channel_id=1, source_target_pairs={{0,1},{1,2},{2,3},{3,4},{4,5},{5,6},{6,7},{8,9},{9,10},{10,11},{11... | collective-permute-start | bytes 98312 | tf_op jit(solution)/shard_map/ppermute | solution.py:1049
  52.9 92.8 %copy-start = (bf16[1,256,1024]{2,1,0:T(8,128)(2,1)S(1)}, bf16[1,256,1024]{2,1,0:T(8,128)(2,1)}, u32[]{:S(2)}) copy-start(bf16[1,256,1024]{2,1,0:T(8,128)(2,1)} %param.14) | copy-start | bytes 1572868
  146.1 6.2 %copy-start.19 = (bf16[272,1024]{1,0:T(8,128)(2,1)}, bf16[272,1024]{1,0:T(8,128)(2,1)S(1)}, u32[]{:S(2)}) copy-start(bf16[272,1024]{1,0:T(8,128)(2,1)S(1)} %multiply_convert_fusion.4) | copy-start | bytes 1671172
  146.2 6.2 %copy-start.41 = (f32[8]{0:T(128)S(1)}, f32[8]{0:T(128)}, u32[]{:S(2)}) copy-start(f32[8]{0:T(128)} %param.20) | copy-start | bytes 100
  186.0 19.7 %copy-start.1 = (bf16[8,128,1024]{2,1,0:T(8,128)(2,1)S(1)}, bf16[8,128,1024]{2,1,0:T(8,128)(2,1)}, u32[]{:S(2)}) copy-start(bf16[8,128,1024]{2,1,0:T(8,128)(2,1)} %get-tuple-element.57) | copy-start | bytes 6291460
  207.5 4.8 slice-start.4
  207.7 4.6 copy-start.8
  207.7 4.6 slice-start.5
  207.7 6.4 %slice-start = ((s8[5767168]{0:T(1024)(128)(4,1)}), s8[4194304]{0:T(1024)(128)(4,1)S(1)}, s32[]{:S(2)}) async-start(s8[5767168]{0:T(1024)(128)(4,1)} %bitcast.175), calls=%async_computation | async-start | bytes 8388608
  212.3 1.7 copy-start.22
  212.3 1.8 slice-start.1
  212.3 7.4 %slice-start.2 = ((s8[5767168]{0:T(1024)(128)(4,1)}), s8[4194304]{0:T(1024)(128)(4,1)S(1)}, s32[]{:S(2)}) async-start(s8[5767168]{0:T(1024)(128)(4,1)} %bitcast.179), calls=%async_computation.2 | async-start | bytes 8388608
  214.1 5.6 %slice-start.3 = ((s8[5767168]{0:T(1024)(128)(4,1)}), s8[1572864]{0:T(1024)(128)(4,1)S(1)}, s32[]{:S(2)}) async-start(s8[5767168]{0:T(1024)(128)(4,1)} %bitcast.179), calls=%async_computation.3 | async-start | bytes 3145728
  218.0 1.7 copy-start.37
  218.0 1.7 copy-start.39
  293.0 3.7 copy-start.6
  300.1 1.7 copy-start.7
  301.4 47.9 %collective-permute-start.8 = (bf16[256,1024]{1,0:T(8,128)(2,1)}, bf16[256,1024]{1,0:T(8,128)(2,1)}, u32[]{:S(2)}, u32[]{:S(2)}) collective-permute-start(bf16[256,1024]{1,0:T(8,128)(2,1)} %get-tuple-element.143), channel_id=1, source_target_pairs={{0,1},{1,0},{2,3},{3,2},{4,5},{5,4},{6,7},{7,6},{8,9},{9,8},{10,11... | collective-permute-start | bytes 1572872 | tf_op jit(solution)/shard_map/ppermute | solution.py:430
  306.9 5.7 %copy-start.21 = (f32[256,8]{1,0:T(8,128)S(1)}, f32[256,8]{1,0:T(8,128)}, u32[]{:S(2)}) copy-start(f32[256,8]{1,0:T(8,128)} %fusion.27.rate_ref) | copy-start | bytes 24580
  306.9 5.7 %copy-start.33 = (f32[256,8]{1,0:T(8,128)S(1)}, f32[256,8]{1,0:T(8,128)}, u32[]{:S(2)}) copy-start(f32[256,8]{1,0:T(8,128)} %get-tuple-element.76) | copy-start | bytes 24580
  306.9 6.9 %copy-start.20 = (bf16[272,1024]{1,0:T(8,128)(2,1)S(1)}, bf16[272,1024]{1,0:T(8,128)(2,1)}, u32[]{:S(2)}) copy-start(bf16[272,1024]{1,0:T(8,128)(2,1)} %copy-done.19) | copy-start | bytes 1671172
  306.9 7.1 %copy-start.10 = (f32[272,1024]{1,0:T(8,128)S(1)}, f32[272,1024]{1,0:T(8,128)}, u32[]{:S(2)}) copy-start(f32[272,1024]{1,0:T(8,128)} %fusion.9) | copy-start | bytes 3342340
  306.9 7.1 %copy-start.11 = (f32[272,1024]{1,0:T(8,128)S(1)}, f32[272,1024]{1,0:T(8,128)}, u32[]{:S(2)}) copy-start(f32[272,1024]{1,0:T(8,128)} %fusion.7) | copy-start | bytes 3342340
  313.1 0.6 copy-start.31
  314.0 4.6 copy-start.34
  316.6 5.3 copy-start.3
  317.3 22.1 %collective-permute-start.1 = (bf16[16,1024]{1,0:T(8,128)(2,1)}, bf16[16,1024]{1,0:T(8,128)(2,1)}, u32[]{:S(2)}, u32[]{:S(2)}) collective-permute-start(bf16[16,1024]{1,0:T(8,128)(2,1)} %slice.164), channel_id=1, source_target_pairs={{1,0},{2,1},{3,2},{4,3},{5,4},{6,5},{7,6},{9,8},{10,9},{11,10},{12... | collective-permute-start | bytes 98312 | tf_op jit(solution)/shard_map/ppermute | solution.py:1114
  319.2 33.4 %collective-permute-start.12 = (bf16[272,1024]{1,0:T(8,128)(2,1)}, bf16[272,1024]{1,0:T(8,128)(2,1)}, u32[]{:S(2)}, u32[]{:S(2)}) collective-permute-start(bf16[272,1024]{1,0:T(8,128)(2,1)} %get-tuple-element.148), channel_id=1, source_target_pairs={{0,1},{1,0},{2,3},{3,2},{4,5},{5,4},{6,7},{7,6},{8,9},{9,8},{10,11... | collective-permute-start | bytes 1671176 | tf_op jit(solution)/shard_map/ppermute | solution.py:430
  322.1 7.2 %copy-start.2 = (bf16[256,2816]{0,1:T(8,128)(2,1)S(1)}, bf16[256,2816]{0,1:T(8,128)(2,1)}, u32[]{:S(2)}) copy-start(bf16[256,2816]{0,1:T(8,128)(2,1)} %copy.67) | copy-start | bytes 4325380
  322.8 25.1 %collective-permute-start.9 = (bf16[272,512]{1,0:T(8,128)(2,1)}, bf16[272,512]{1,0:T(8,128)(2,1)}, u32[]{:S(2)}, u32[]{:S(2)}) collective-permute-start(bf16[272,512]{1,0:T(8,128)(2,1)} %bitcast.121), channel_id=1, source_target_pairs={{0,1},{1,0},{2,3},{3,2},{4,5},{5,4},{6,7},{7,6},{8,9},{9,8},{10,11... | collective-permute-start | bytes 835592 | tf_op jit(solution)/shard_map/ppermute | solution.py:430
  328.8 18.4 %collective-permute-start.7 = (bf16[256,512]{0,1:T(8,128)(2,1)}, bf16[256,512]{0,1:T(8,128)(2,1)}, u32[]{:S(2)}, u32[]{:S(2)}) collective-permute-start(bf16[256,512]{0,1:T(8,128)(2,1)} %bitcast.158), channel_id=1, source_target_pairs={{0,1},{1,0},{2,3},{3,2},{4,5},{5,4},{6,7},{7,6},{8,9},{9,8},{10,11... | collective-permute-start | bytes 786440 | tf_op jit(solution)/shard_map/ppermute | solution.py:430
  329.3 4.9 copy-start.35
  331.0 8.4 %copy-start.4 = (f32[272,1024]{1,0:T(8,128)S(1)}, f32[272,1024]{1,0:T(8,128)}, u32[]{:S(2)}) copy-start(f32[272,1024]{1,0:T(8,128)} %copy-done.3) | copy-start | bytes 3342340
  333.1 4.9 copy-start.9
  339.4 2.9 copy-start.36
  339.4 4.7 copy-start.5
  343.2 3.6 copy-start.40
  343.3 3.5 collective-permute-start.13
  344.1 3.1 copy-start.17
  344.1 3.8 copy-start.38
  344.1 4.2 copy-start.32
  344.1 5.3 copy-start.16
  344.1 5.4 copy-start.26
  346.8 17.1 %collective-permute-start.6 = (bf16[256,2816]{1,0:T(8,128)(2,1)S(1)}, bf16[256,2816]{1,0:T(8,128)(2,1)S(1)}, u32[]{:S(2)}, u32[]{:S(2)}) collective-permute-start(bf16[256,2816]{1,0:T(8,128)(2,1)S(1)} %copy-done.40), channel_id=1, source_target_pairs={{0,1},{1,0},{2,3},{3,2},{4,5},{5,4},{6,7},{7,6},{8,9},{9,8},{10,11... | collective-permute-start | bytes 4325384 | tf_op jit(solution)/shard_map/ppermute | solution.py:430
  347.2 8.9 %collective-permute-start.11 = (bf16[272,1024]{1,0:T(8,128)(2,1)S(1)}, bf16[272,1024]{1,0:T(8,128)(2,1)S(1)}, u32[]{:S(2)}, u32[]{:S(2)}) collective-permute-start(bf16[272,1024]{1,0:T(8,128)(2,1)S(1)} %copy-done.17), channel_id=1, source_target_pairs={{0,1},{1,0},{2,3},{3,2},{4,5},{5,4},{6,7},{7,6},{8,9},{9,8},{10,11... | collective-permute-start | bytes 1671176 | tf_op jit(solution)/shard_map/ppermute | solution.py:430
  347.9 19.3 %collective-permute-start.5 = (bf16[256,2816]{1,0:T(8,128)(2,1)S(1)}, bf16[256,2816]{1,0:T(8,128)(2,1)S(1)}, u32[]{:S(2)}, u32[]{:S(2)}) collective-permute-start(bf16[256,2816]{1,0:T(8,128)(2,1)S(1)} %copy-done.38), channel_id=1, source_target_pairs={{0,1},{1,0},{2,3},{3,2},{4,5},{5,4},{6,7},{7,6},{8,9},{9,8},{10,11... | collective-permute-start | bytes 4325384 | tf_op jit(solution)/shard_map/ppermute | solution.py:430
  349.3 3.3 copy-start.15
  349.3 3.7 copy-start.18
  349.4 8.9 %collective-permute-start.10 = (bf16[272,1024]{1,0:T(8,128)(2,1)S(1)}, bf16[272,1024]{1,0:T(8,128)(2,1)S(1)}, u32[]{:S(2)}, u32[]{:S(2)}) collective-permute-start(bf16[272,1024]{1,0:T(8,128)(2,1)S(1)} %copy-done.16), channel_id=1, source_target_pairs={{0,1},{1,0},{2,3},{3,2},{4,5},{5,4},{6,7},{7,6},{8,9},{9,8},{10,11... | collective-permute-start | bytes 1671176 | tf_op jit(solution)/shard_map/ppermute | solution.py:430
  352.6 3.4 copy-start.23
  352.6 8.0 %collective-permute-start.2 = (bf16[256,1408]{0,1:T(8,128)(2,1)S(1)}, bf16[256,1408]{0,1:T(8,128)(2,1)S(1)}, u32[]{:S(2)}, u32[]{:S(2)}) collective-permute-start(bf16[256,1408]{0,1:T(8,128)(2,1)S(1)} %bitcast.138), channel_id=1, source_target_pairs={{0,1},{1,0},{2,3},{3,2},{4,5},{5,4},{6,7},{7,6},{8,9},{9,8},{10,11... | collective-permute-start | bytes 2162696 | tf_op jit(solution)/shard_map/ppermute | solution.py:430
  356.1 2.2 copy-start.25
  356.1 4.6 collective-permute-start.3
  358.3 2.4 copy-start.14
  358.3 5.6 %collective-permute-start.4 = (bf16[256,512]{0,1:T(8,128)(2,1)S(1)}, bf16[256,512]{0,1:T(8,128)(2,1)S(1)}, u32[]{:S(2)}, u32[]{:S(2)}) collective-permute-start(bf16[256,512]{0,1:T(8,128)(2,1)S(1)} %bitcast.156), channel_id=1, source_target_pairs={{0,1},{1,0},{2,3},{3,2},{4,5},{5,4},{6,7},{7,6},{8,9},{9,8},{10,11... | collective-permute-start | bytes 786440 | tf_op jit(solution)/shard_map/ppermute | solution.py:430
  360.6 3.3 copy-start.24
  541.0 6.2 %copy-start.13 = (bf16[128,2816]{1,0:T(8,128)(2,1)S(1)}, bf16[128,2816]{1,0:T(8,128)(2,1)}, u32[]{:S(2)}) copy-start(bf16[128,2816]{1,0:T(8,128)(2,1)} %get-tuple-element.85) | copy-start | bytes 2162692
  544.8 3.6 copy-start.12
  547.2 2.5 copy-start.30
  547.2 4.7 copy-start.27
  547.2 4.7 copy-start.28
  547.2 4.7 copy-start.29

commit v2 on v1

--- a/solution.py
+++ b/solution.py
@@ -133,87 +133,6 @@
         rmap_ref[part, :] = out[:, size:].astype(BF16)
         running = running + tn(new, key)
     end_ref[0] = running.astype(BF16)
-
-
-def local_call(keep, ext, conv, rate, allow, heads):
-    tok = rate.shape[0]
-    width = ext.shape[1] // 3
-    size = width // heads
-    count = tok // STRETCH
-    taps = conv.shape[0]
-    rows = ext.shape[0]
-
-    def third(i, r):
-        return pl.BlockSpec((r, size), lambda h: (0, h + i * heads))
-
-    def token_block():
-        return pl.BlockSpec((tok, size), lambda h: (0, h))
-
-    return pl.pallas_call(
-        local_kernel,
-        grid=(heads,),
-        in_specs=[
-            pl.BlockSpec(memory_space=pltpu.SMEM),
-            third(0, rows), third(1, rows), third(2, rows),
-            third(0, taps), third(1, taps), third(2, taps),
-            pl.BlockSpec((tok, heads), lambda h: (0, 0)),
-            pl.BlockSpec((tok, taps), lambda h: (0, 0)),
-        ],
-        out_specs=[
-            token_block(), token_block(), token_block(),
-            pl.BlockSpec((1, tok, STRETCH), lambda h: (h, 0, 0)),
-            token_block(),
-            pl.BlockSpec((1, count, 2 * size, size), lambda h: (h, 0, 0, 0)),
-            pl.BlockSpec((1, 2 * size, size), lambda h: (h, 0, 0)),
-            token_block(), token_block(), token_block(), token_block(),
-        ],
-        out_shape=[
-            jax.ShapeDtypeStruct((tok, width), BF16),
-            jax.ShapeDtypeStruct((tok, width), BF16),
-            jax.ShapeDtypeStruct((tok, width), BF16),
-            jax.ShapeDtypeStruct((heads, tok, STRETCH), BF16),
-            jax.ShapeDtypeStruct((tok, width), BF16),
-            jax.ShapeDtypeStruct((heads, count, 2 * size, size), BF16),
-            jax.ShapeDtypeStruct((heads, 2 * size, size), BF16),
-            jax.ShapeDtypeStruct((tok, width), F32),
-            jax.ShapeDtypeStruct((tok, width), BF16),
-            jax.ShapeDtypeStruct((tok, width), BF16),
-            jax.ShapeDtypeStruct((tok, width), BF16),
-        ],
-        compiler_params=pltpu.CompilerParams(vmem_limit_bytes=VMEM_LIMIT),
-        cost_estimate=pl.CostEstimate(flops=2 * 10**9, bytes_accessed=10**7, transcendentals=10**6),
-        name="delta_local",
-    )(keep, ext, ext, ext, conv, conv, conv, rate, allow)
-
-
-def readout_kernel(state_ref, read_ref, rmap_ref, gain_ref, out_ref, normal_ref):
-    readout = read_ref[...] + nt(rmap_ref[...], state_ref[0])
-    inv = lax.rsqrt(jnp.mean(readout * readout, -1, keepdims=True) + EPSILON)
-    out_ref[...] = readout
-    normal_ref[...] = (readout * inv * gain_ref[...]).astype(BF16)
-
-
-def readout_call(state, read, rmap, gain):
-    heads, size, _ = state.shape
-    tok, width = read.shape
-    block = pl.BlockSpec((tok, size), lambda h: (0, h))
-    return pl.pallas_call(
-        readout_kernel,
-        grid=(heads,),
-        in_specs=[
-            pl.BlockSpec((1, size, size), lambda h: (h, 0, 0)),
-            block, block,
-            pl.BlockSpec((1, size), lambda h: (0, 0)),
-        ],
-        out_specs=[block, block],
-        out_shape=[
-            jax.ShapeDtypeStruct((tok, width), F32),
-            jax.ShapeDtypeStruct((tok, width), BF16),
-        ],
-        compiler_params=pltpu.CompilerParams(vmem_limit_bytes=VMEM_LIMIT),
-        cost_estimate=pl.CostEstimate(flops=10**8, bytes_accessed=4 * 10**6, transcendentals=2000),
-        name="delta_readout",
-    )(state, read, rmap, gain)
 
 
 def adjoint_kernel(
@@ -560,9 +479,13 @@
             unit, k, step, self.source_span(k), p.stream ^ step, p.beside(step)
         ).wait_recv()
 
+    @staticmethod
+    def turns(unit, k):
+        return (1, 2) if (unit + k) % 2 == 0 else (2, 1)
+
     def corner(self, unit, k):
         p = self.place
-        first, second = (1, 2) if unit % 2 == 0 else (2, 1)
+        first, second = self.turns(unit, k)
         return self.wire(
             unit, k, 3, self.source_span(k), p.stream ^ first, p.beside(second)
         )
@@ -623,13 +546,13 @@
             self.sideways(unit, k, 2).start()
 
         def turn(unit, k):
-            self.sideways_wait(unit, k, 1 if unit % 2 == 0 else 2)
+            self.sideways_wait(unit, k, self.turns(unit, k)[0])
             self.corner(unit, k).start()
 
         def close(w, k):
             for unit, (owner, _, _) in enumerate(self.units):
                 if owner == w:
-                    self.sideways_wait(unit, k, 2 if unit % 2 == 0 else 1)
+                    self.sideways_wait(unit, k, self.turns(unit, k)[1])
                     self.corner_wait(unit, k)
             self.across(w, k).start()
 
@@ -698,19 +621,19 @@
         return rows // down, width // across
 
     @staticmethod
-    def scratch(shapes, streams):
+    def scratch(shapes, kinds, streams):
         out = []
         dma = pltpu.SemaphoreType.DMA
-        for shape in shapes:
+        for shape, kind in zip(shapes, kinds):
             chips = shape[0]
             r, c = Reduce.block(shape, streams)
             out += [
-                pltpu.VMEM((2, chips, r, c), BF16),
-                pltpu.VMEM((2, chips, r, c), BF16),
-                pltpu.VMEM((chips, r, c), BF16),
-                pltpu.VMEM((chips, r, c), BF16),
-                pltpu.VMEM((chips, r, c), BF16),
-                pltpu.VMEM((streams, r, c), BF16),
+                pltpu.VMEM((2, chips, r, c), kind),
+                pltpu.VMEM((2, chips, r, c), kind),
+                pltpu.VMEM((chips, r, c), kind),
+                pltpu.VMEM((chips, r, c), kind),
+                pltpu.VMEM((chips, r, c), kind),
+                pltpu.VMEM((streams, r, c), kind),
             ]
         n = len(shapes)
         chips = shapes[0][0]
@@ -786,7 +709,7 @@
                 self.bufs[w][1][slot, chip] = (
                     self.grads[w][chip, row, col].astype(F32)
                     + self.bufs[w][0][slot, chip].astype(F32)
-                ).astype(BF16)
+                ).astype(self.grads[w].dtype)
             if slot:
                 self.second(w, half).start()
 
@@ -796,7 +719,7 @@
         for chip in range(start, start + n):
             self.bufs[w][3][chip] = (
                 self.bufs[w][1][0, chip].astype(F32) + self.bufs[w][2][chip].astype(F32)
-            ).astype(BF16)
+            ).astype(self.grads[w].dtype)
 
     def spread(self, w):
         for k in range(1, self.place.chips):
@@ -808,7 +731,7 @@
         for k in range(1, p.chips):
             self.third(w, k).wait_recv()
             total = total + self.bufs[w][4][k].astype(F32)
-        self.bufs[w][5][0] = total.astype(BF16)
+        self.bufs[w][5][0] = total.astype(self.grads[w].dtype)
         for step in range(1, p.streams):
             self.fourth(w, step).start()
 
@@ -862,8 +785,8 @@
         functools.partial(reduce_kernel, streams, spans, len(grads)),
         in_specs=[vmem] * len(grads),
         out_specs=[vmem] * len(grads),
-        out_shape=[jax.ShapeDtypeStruct(s[1:], BF16) for s in shapes],
-        scratch_shapes=Reduce.scratch(shapes, streams),
+        out_shape=[jax.ShapeDtypeStruct(g.shape[1:], g.dtype) for g in grads],
+        scratch_shapes=Reduce.scratch(shapes, [g.dtype for g in grads], streams),
         compiler_params=pltpu.CompilerParams(
             collective_id=collective_id, has_side_effects=True, vmem_limit_bytes=VMEM_LIMIT
         ),
@@ -871,15 +794,11 @@
     )(*grads)
 
 
-def chain_kernel(streams, spans, backward, *refs):
-    p = Place(streams, spans)
-    if backward:
-        (adj_ref, p_low, p_high, p_chip, state_ref,
-         swap, carry, outgo, sent, swap_sem, hop_sem, back_sem) = refs
-    else:
-        (map_ref, state_ref, p_low, p_high, p_chip,
-         swap, carry, outgo, sent, s_chip, swap_sem, hop_sem, back_sem) = refs
-    source = adj_ref if backward else map_ref
+def chain_body(p, backward, source, maps, state_ref, scratch):
+    p_low, p_high, p_chip = maps
+    swap, carry, outgo, sent = scratch[:4]
+    swap_sem, hop_sem, back_sem = scratch[-3:]
+    s_chip = None if backward else scratch[4]
     heads, size = source.shape[0], source.shape[2]
     half = heads // 2
     mine = p.core * half
@@ -887,7 +806,6 @@
     ahead, behind = (-1, 1) if backward else (1, -1)
     edge_in = p.chips - 1 if backward else 0
     edge_out = 0 if backward else p.chips - 1
-    greet([p.other(), p.along(1), p.along(-1)])
     swap_copy = copy_to(
         source.at[pl.ds(theirs, half)], swap, swap_sem.at[0], swap_sem.at[1], p.other()
     )
@@ -960,24 +878,171 @@
             hop(h).wait_send()
 
 
+def chain_scratch(heads, size, rows, backward):
+    half = heads // 2
+    dma = pltpu.SemaphoreType.DMA
+    scratch = [
+        pltpu.VMEM((half, rows, size), BF16),
+        pltpu.VMEM((half, size, size), BF16),
+        pltpu.VMEM((half, size, size), F32),
+        pltpu.VMEM((heads, size, size), BF16),
+    ]
+    if not backward:
+        scratch.append(pltpu.VMEM((half, size, size), F32))
+    return scratch + [dma((2,)), dma((half, 2)), dma((2,))]
+
+
+def chain_kernel(streams, spans, backward, *refs):
+    p = Place(streams, spans)
+    greet([p.other(), p.along(1), p.along(-1)])
+    if backward:
+        chain_body(p, True, refs[0], refs[1:4], refs[4], refs[5:])
+    else:
+        chain_body(p, False, refs[0], refs[2:5], refs[1], refs[5:])
+
+
+def readout_body(readout, gain):
+    inv = lax.rsqrt(jnp.mean(readout * readout, -1, keepdims=True) + EPSILON)
+    return (readout * inv * gain).astype(BF16)
+
+
+def spread_steps(steps, slots, index):
+    count = len(steps)
+    return steps[count * index // slots : count * (index + 1) // slots]
+
+
+def forward_kernel(streams, spans, heads, weights, *refs):
+    ins, refs = refs[:10], refs[10:]
+    shards, refs = refs[:weights], refs[weights:]
+    outs, refs = refs[:14], refs[14:]
+    fulls, refs = refs[:weights], refs[weights:]
+    gather_sems, refs = refs[:3], refs[3:]
+    map_buf, read_buf, rmap_buf, state_buf = refs[:4]
+    chain_bufs = refs[4:]
+    gain_ref = ins[9]
+    (q_ref, k_ref, v_ref, inv_ref, wk_ref, pre_ref, nv_ref, np_ref,
+     state_ref, p_low, p_high, p_chip, out_ref, normal_ref) = outs
+    step_id = pl.program_id(0)
+    place = Place(streams, spans)
+    work = Gather(place, shards, fulls, gather_sems)
+    steps = work.steps()
+
+    @pl.when(step_id == 0)
+    def _():
+        greet(work.neighbours())
+
+    for index in range(heads + 1):
+
+        @pl.when(step_id == index)
+        def _():
+            for step in spread_steps(steps, heads + 2, index):
+                step()
+
+    @pl.when(step_id < heads)
+    def _():
+        local_kernel(
+            *ins[:9], q_ref, k_ref, v_ref, inv_ref, wk_ref, pre_ref, map_buf.at[pl.ds(step_id, 1)],
+            read_buf.at[step_id], rmap_buf.at[step_id], nv_ref, np_ref,
+        )
+
+    @pl.when(step_id == heads)
+    def _():
+        chain_body(place, False, map_buf, (p_low, p_high, p_chip), state_buf, chain_bufs)
+        state_ref[...] = state_buf[...]
+        size = gain_ref.shape[1]
+        for h in range(heads):
+            cols = slice(h * size, (h + 1) * size)
+            readout = read_buf[h] + nt(rmap_buf[h], state_buf[h])
+            out_ref[:, cols] = readout
+            normal_ref[:, cols] = readout_body(readout, gain_ref[...])
+        for step in spread_steps(steps, heads + 2, heads + 1):
+            step()
+
+
+def forward_call(keep, ext, conv, rate, allow, gain, shards, heads, collective_id):
+    streams, spans = lax.axis_size("stream"), lax.axis_size("span")
+    tok = rate.shape[0]
+    width = ext.shape[1] // 3
+    size = width // heads
+    count = tok // STRETCH
+    taps = conv.shape[0]
+    rows = ext.shape[0]
+    half = heads // 2
+    hbm = pl.BlockSpec(memory_space=pl.ANY)
+
+    def at(i):
+        return jnp.minimum(i, heads - 1)
+
+    def third(i, r):
+        return pl.BlockSpec((r, size), lambda h: (0, at(h) + i * heads))
+
+    def token_block():
+        return pl.BlockSpec((tok, size), lambda h: (0, at(h)))
+
+    def whole(*shape):
+        return pl.BlockSpec(shape, lambda h: (0,) * len(shape))
+
+    token_shape = jax.ShapeDtypeStruct((tok, width), BF16)
+    square = jax.ShapeDtypeStruct((half, size, size), BF16)
+    shapes = [s.shape for s in shards]
+    outs = pl.pallas_call(
+        functools.partial(forward_kernel, streams, spans, heads, len(shards)),
+        grid=(heads + 1,),
+        in_specs=[
+            pl.BlockSpec(memory_space=pltpu.SMEM),
+            third(0, rows), third(1, rows), third(2, rows),
+            third(0, taps), third(1, taps), third(2, taps),
+            whole(tok, heads), whole(tok, taps), whole(1, size),
+        ]
+        + [hbm] * len(shards),
+        out_specs=[
+            token_block(), token_block(), token_block(),
+            pl.BlockSpec((1, tok, STRETCH), lambda h: (at(h), 0, 0)),
+            token_block(),
+            pl.BlockSpec((1, count, 2 * size, size), lambda h: (at(h), 0, 0, 0)),
+            token_block(), token_block(),
+            whole(heads, size, size),
+            whole(half, size, size), whole(half, size, size), whole(half, size, size),
+            whole(tok, width), whole(tok, width),
+        ]
+        + [hbm] * len(shards),
+        out_shape=[
+            token_shape, token_shape, token_shape,
+            jax.ShapeDtypeStruct((heads, tok, STRETCH), BF16),
+            token_shape,
+            jax.ShapeDtypeStruct((heads, count, 2 * size, size), BF16),
+            token_shape, token_shape,
+            jax.ShapeDtypeStruct((heads, size, size), BF16),
+            square, square, square,
+            jax.ShapeDtypeStruct((tok, width), F32),
+            token_shape,
+        ]
+        + [jax.ShapeDtypeStruct((spans,) + s.shape, s.dtype) for s in shards],
+        scratch_shapes=Gather.sem_shapes(shapes, streams, spans)
+        + [
+            pltpu.VMEM((heads, 2 * size, size), BF16),
+            pltpu.VMEM((heads, tok, size), F32),
+            pltpu.VMEM((heads, tok, size), BF16),
+            pltpu.VMEM((heads, size, size), BF16),
+        ]
+        + chain_scratch(heads, size, 2 * size, False),
+        compiler_params=pltpu.CompilerParams(
+            collective_id=collective_id, has_side_effects=True, vmem_limit_bytes=VMEM_LIMIT
+        ),
+        name="delta_forward",
+    )(keep, ext, ext, ext, conv, conv, conv, rate, allow, gain, *shards)
+    return outs[:14], outs[14:]
+
+
 def chain_call(maps, carried, collective_id):
     streams, spans = lax.axis_size("stream"), lax.axis_size("span")
     backward = carried is not None
     heads, size = maps.shape[0], maps.shape[2]
     half = heads // 2
     vmem = pl.BlockSpec(memory_space=pltpu.VMEM)
-    dma = pltpu.SemaphoreType.DMA
     square = jax.ShapeDtypeStruct((half, size, size), BF16)
     state = jax.ShapeDtypeStruct((heads, size, size), BF16)
-    scratch = [
-        pltpu.VMEM((half,) + maps.shape[1:], BF16),
-        pltpu.VMEM((half, size, size), BF16),
-        pltpu.VMEM((half, size, size), F32),
-        pltpu.VMEM((heads, size, size), BF16),
-    ]
-    if not backward:
-        scratch.append(pltpu.VMEM((half, size, size), F32))
-    scratch += [dma((2,)), dma((half, 2)), dma((2,))]
+    scratch = chain_scratch(heads, size, maps.shape[1], backward)
     operands = [maps] + (list(carried) if backward else [])
     return pl.pallas_call(
         functools.partial(chain_kernel, streams, spans, backward),
@@ -1010,10 +1075,7 @@
     small_len = small.shape[0]
     small = jnp.pad(small, (0, 16 * 512 - small_len)).reshape(16, 512)
     full_qkv, smalls = gather_call([w_qkv, small], 1)
-    full_out, full_gate, full_up, full_down = gather_call([w_out, w_gate, w_up, w_down], 2)
-    full_qkv, full_out, full_gate, full_up, full_down = (
-        w.reshape(-1, w.shape[2]) for w in (full_qkv, full_out, full_gate, full_up, full_down)
-    )
+    full_qkv = full_qkv.reshape(-1, full_qkv.shape[2])
     smalls = smalls.reshape(span_count, -1)
 
     def small_part(shape, start):
@@ -1058,10 +1120,13 @@
         jnp.dot(normed, full_beta, preferred_element_type=F32) + beta_bias
     )
     (
-        queries, keys, values, invs, wkeys, prefix, device_map, read_local, read_map, new_v, new_p
-    ) = local_call(stretch_keep, projected, full_conv, strength, allow, heads)
-    state_in, p_low, p_high, p_chip = chain_call(device_map, None, 3)
-    readout, normal_heads = readout_call(state_in, read_local, read_map, head_gain)
+        queries, keys, values, invs, wkeys, prefix, new_v, new_p,
+        state_in, p_low, p_high, p_chip, readout, normal_heads,
+    ), rest = forward_call(
+        stretch_keep, projected, full_conv, strength, allow, head_gain,
+        [w_out, w_gate, w_up, w_down], heads, 2,
+    )
+    full_out, full_gate, full_up, full_down = (w.reshape(-1, w.shape[2]) for w in rest)
 
     middle = inputs_f + jnp.dot(normal_heads, full_out, preferred_element_type=F32)
     inv_second = lax.rsqrt(jnp.mean(middle * middle, -1, keepdims=True) + EPSILON)
@@ -1138,18 +1203,17 @@
         1,
     )
     packed = jnp.pad(packed, ((0, 0), (0, 16 * 512 - packed.shape[1])))
-    packed = packed.astype(BF16).reshape(span_count // 2, 2, 16, 512)
+    packed = packed.reshape(span_count // 2, 2, 16, 512)
     core = place % 2
-    half_small = (
-        lax.dynamic_index_in_dim(packed, core, 1, keepdims=False).astype(F32)
-        + swap_core(lax.dynamic_index_in_dim(packed, 1 - core, 1, keepdims=False)).astype(F32)
-    ).astype(BF16)
+    half_small = lax.dynamic_index_in_dim(packed, core, 1, keepdims=False) + swap_core(
+        lax.dynamic_index_in_dim(packed, 1 - core, 1, keepdims=False)
+    )
     parts = reduce_call(
         [half_down, half_gate, half_up, half_out, half_q, half_k, half_v, half_small], 5
     )
     part_down, part_gate, part_up, part_out = (x.astype(F32) for x in parts[:4])
     part_qkv = jnp.concatenate([x.astype(F32) for x in parts[4:7]], 1)
-    part_small = parts[7].reshape(-1).astype(F32)
+    part_small = parts[7].reshape(-1)
     sums = []
     at = 0
     for like in (conv_weight, w_beta, norm_attn, norm_ffn, norm_head, beta_bias):

time: 562 us -> 522 us (0.929)
  Pallas kernels: 418 us -> 376 us
    pallas_call x2 -> x1, Pallas kernels: 129 us -> 40.3 us  [gather_call(): pl.pallas_call(functools.partial(gather_kernel, streams, spans, len(shard...]
    pallas_call x2 -> x1, Pallas kernels: 39 us -> 97.6 us  [forward_call(): pl.pallas_call(functools.partial(forward_kernel, streams, spans, heads, l...]
    pallas_call x2 -> x1, Pallas kernels: 38.4 us -> 24.7 us  [chain_call(): pl.pallas_call(functools.partial(chain_kernel, streams, spans, backward),...]
    unnamed x112 -> x108, local copies, waits for them, and re-layouts: 14.4 us -> 17 us
  transfers between devices with their start and end apart: 14 -> 14, of which waited for: 0 -> 0; matrix products, arithmetic and copies ran while one was open for 13% -> 14% of each run, Pallas kernels for 23% -> 8%
where the time goes in v2:
time: 522 us; the launch traced here: 513 us
  Pallas kernels  376 us (72%)
  matrix products  63.2 us (12%)
  local copies, waits for them, and re-layouts  46.6 us (9%)
  other arithmetic  18.1 us (3%)
  starting transfers between devices  7.8 us (1%)
    pallas_call x1, Pallas kernels, reduce_call(): pl.pallas_call(functools.partial(reduce_kernel, streams, spans, len(grads...  172 us
    pallas_call x1, Pallas kernels, forward_call(): pl.pallas_call(functools.partial(forward_kernel, streams, spans, heads, l...  97.6 us
    dot_general x16, matrix products, product(): jnp.einsum(pattern, first, second, preferred_element_type=F32).astype(kind)  44.3 us
    pallas_call x1, Pallas kernels, gather_call(): pl.pallas_call(functools.partial(gather_kernel, streams, spans, len(shard...  40.3 us
    pallas_call x1, Pallas kernels, backward_call(): pl.pallas_call(backward_kernel, grid=(heads,), in_specs=[pl.BlockSpec(mem...  27.4 us
    pallas_call x1, Pallas kernels, chain_call(): pl.pallas_call(functools.partial(chain_kernel, streams, spans, backward),...  24.7 us
    unnamed x108, local copies, waits for them, and re-layouts  17 us
    pallas_call x1, Pallas kernels, adjoint_call(): pl.pallas_call(adjoint_kernel, grid=(heads,), in_specs=[pl.BlockSpec(memo...  14.2 us
  transfers between devices with their start and end apart: 14, of which 0 were waited for; matrix products, arithmetic and copies ran while one was open for 14% of the time, Pallas kernels for 8%

profile of v2, /device:TPU:0, one launch (start us, length us, event | category | flops | bytes accessed | tf_op | source)
XLA Modules:
  0.0 513.3 jit_solution(9269288823260411480)
XLA Ops:
  0.7 0.8 slice_bitcast_fusion.3
  1.5 2.3 collective-permute-start
  3.9 0.8 reduce-window_clone.1
  6.1 0.8 copy.61
  8.0 0.8 dynamic-update-slice.4
  8.9 0.8 dynamic-update-slice.5
  9.7 0.8 dynamic-update-slice.6
  11.2 40.3 %gather_weights.1 = (bf16[8,128,3072]{2,1,0:T(8,128)(2,1)}, bf16[8,16,512]{2,1,0:T(8,128)(2,1)}) custom-call(bf16[128,3072]{1,0:T(8,128)(2,1)} %refs_0_.1, bf16[16,512]{1,0:T(8,128)(2,1)} %reshape.354.refs_1_), custom_call_target="tpu_custom_call" | custom-call | tf_op jit(solution)/shard_map/gather_weights/pallas_call | solution.py:599
  51.5 1.0 copy.82
  52.7 1.4 concatenate.65
  54.5 0.8 copy.63.refs_8_.allow_ref
  56.5 0.9 copy.71
  57.9 6.2 %convolution_convert_fusion.2.refs_1_.refs_2_.refs_3_.eq_ref.ek_ref.ev_ref = bf16[272,3072]{1,0:T(8,128)(2,1)} fusion(bf16[272,1024]{1,0:T(8,128)(2,1)S(1)} %multiply_convert_fusion.4, bf16[1024,3072]{1,0:T(8,128)(2,1)} %bitcast.139), kind=kOutput, calls=%fused_computation.3 | convolution fusion | flops 1712111616 | bytes 8519680 | tf_op jit(solution)/shard_map/dot_general | solution.py:1118
  64.1 1.0 fusion.27.refs_7_.rate_ref
  65.0 97.6 %delta_forward.1 = (bf16[256,1024]{1,0:T(8,128)(2,1)}, bf16[256,1024]{1,0:T(8,128)(2,1)}, bf16[256,1024]{1,0:T(8,128)(2,1)}, bf16[8,256,64]{2,1,0:T(8,128)(2,1)}...) custom-call(f32[4]{0:T(128)} %broadcast_subtract_fusion.refs_0_.keep, ...), custom_call_target="tpu_custom_call" | custom-call | tf_op jit(solution)/shard_map/delta_forward/pallas_call | solution.py:988
  162.7 2.7 multiply_reduce_fusion.5
  166.1 1.7 fusion.68
  167.8 0.9 copy-done.38
  168.8 1.7 fusion.67
  170.7 3.9 multiply_convert_fusion
  174.6 1.7 fusion.69
  176.3 2.5 multiply_reduce_fusion.1
  178.8 1.5 fusion.65
  180.9 2.8 fusion.70.gn_ref
  183.7 14.2 %delta_adjoint.1 = (bf16[256,1024]{1,0:T(8,128)(2,1)}, bf16[8,128,128]{2,1,0:T(8,128)(2,1)}, f32[8,1,128]{2,1,0:T(1,128)}) custom-call(f32[4]{0:T(128)} %broadcast_subtract_fusion.refs_0_.keep_ref, f32[256,1024]{1,0:T(8,128)} %fusion.70.gn_ref, f32[256,1024]{1,0:T(8,128)} %get-tuple-element.54.read_ref, f32[1,128]{1,0:T(1,128)} %reshape.393.refs_9_.gain_ref, ...), custom_call_target="tpu_custom_call" | custom-call | flops 500000000 | bytes 6000000 | tf_op jit(solution)/shard_map/delta_adjoint/pallas_call | solution.py:173
  197.9 24.7 %span_chain.1.din_ref = bf16[8,128,128]{2,1,0:T(8,128)(2,1)} custom-call(bf16[8,128,128]{2,1,0:T(8,128)(2,1)} %get-tuple-element.58.refs_0_, bf16[4,128,128]{2,1,0:T(8,128)(2,1)} %get-tuple-element.59.refs_1_, bf16[4,128,128]{2,1,0:T(8,128)(2,1)} %get-tuple-element.60.refs_2_, bf16[4,128,128]{2,1,0:T(8,128)(2,1)} %get-tuple-element.61.refs_3_), custom_call_target="tpu_custom_call" | custom-call | tf_op jit(solution)/shard_map/span_chain/pallas_call | solution.py:1047
  222.7 27.4 %delta_backward.1 = (bf16[3,272,1024]{2,1,0:T(8,128)(2,1)}, f32[3,4,1024]{2,1,0:T(4,128)}, f32[256,8]{1,0:T(8,128)}) custom-call(f32[4]{0:T(128)} %broadcast_subtract_fusion.refs_0_.keep_ref, bf16[8,128,128]{2,1,0:T(8,128)(2,1)} %span_chain.1.din_ref, bf16[8,128,128]{2,1,0:T(8,128)(2,1)} %get-tuple-element.62.min_ref, ...), custom_call_target="tpu_custom_call" | custom-call | flops 2000000000 | bytes 12000000 | tf_op jit(solution)/shard_map/delta_backward/pallas_call | solution.py:296
  250.1 3.7 fusion.9
  253.8 3.4 fusion.7
  257.3 1.2 slice_bitcast_fusion
  258.9 1.2 reshape.373
  260.0 1.4 reshape.368
  261.5 2.5 copy.65
  264.0 5.7 %fusion.23 = bf16[1,256,1024]{2,1,0:T(8,128)(2,1)} fusion(f32[256,1024]{1,0:T(8,128)S(1)} %get-tuple-element.167, bf16[256,2816]{1,0:T(8,128)(2,1)} %get-tuple-element.141, bf16[2816,1024]{1,0:T(8,128)(2,1)} %bitcast.167), kind=kOutput, calls=%fused_computation.36 | convolution fusion | flops 1476919296 | bytes 8781824 | tf_op jit(solution)/shard_map/dot_general | solution.py:1151
  270.2 1.1 fusion.46
  271.4 2.6 fusion.19
  274.7 1.3 collective-permute-start.1
  276.6 1.1 collective-permute-start.12
  277.8 1.4 multiply_convert_fusion.3
  281.0 3.3 constant_dynamic-slice_fusion.3
  284.3 1.9 copy.81
  286.7 1.2 constant_dynamic-slice_fusion.7
  288.4 2.1 constant_dynamic-slice_fusion.5
  290.5 2.0 reshape.384
  292.6 1.9 copy.80
  294.4 1.9 copy.79
  296.3 1.3 copy.78
  297.7 2.9 multiply_reduce_fusion.2
  300.6 0.9 concatenate.71
  302.6 2.6 add_bitcast_fusion
  306.8 1.0 constant_dynamic-update-slice_fusion
  308.0 3.1 convolution_convert_fusion.7
  311.5 3.0 convolution_convert_fusion.4
  314.8 2.0 convolution_convert_fusion.5
  317.2 2.0 convolution_convert_fusion.6
  319.2 3.2 convolution_convert_fusion.3
  322.4 3.3 convolution_convert_fusion
  325.7 3.3 convolution_convert_fusion.1
  328.9 171.7 %reduce_grads.1 = (bf16[352,1024]{1,0:T(8,128)(2,1)}, bf16[128,2816]{1,0:T(8,128)(2,1)}, bf16[128,2816]{1,0:T(8,128)(2,1)}, bf16[128,1024]{1,0:T(8,128)(2,1)}, b...) custom-call(bf16[4,352,1024]{2,1,0:T(8,128)(2,1)} %bitcast.119, ...), custom_call_target="tpu_custom_call" | custom-call | tf_op jit(solution)/shard_map/reduce_grads/pallas_call | solution.py:784
  504.5 2.4 convert_element_type.151
  506.9 1.2 convert_element_type.152
  508.1 1.3 convert_element_type.153
  509.4 0.8 convert_element_type.150
  511.6 1.3 maximum_convert_fusion
  (176 shorter events, 21.6 us)
Async XLA Ops:
  0.6 56.8 %copy-start = (bf16[1,256,1024]{2,1,0:T(8,128)(2,1)S(1)}, bf16[1,256,1024]{2,1,0:T(8,128)(2,1)}, u32[]{:S(2)}) copy-start(bf16[1,256,1024]{2,1,0:T(8,128)(2,1)} %param.14) | copy-start | bytes 1572868
  1.5 55.9 %collective-permute-start = (bf16[16,1024]{1,0:T(8,128)(2,1)S(1)}, bf16[16,1024]{1,0:T(8,128)(2,1)S(1)}, u32[]{:S(2)}, u32[]{:S(2)}) collective-permute-start(bf16[16,1024]{1,0:T(8,128)(2,1)S(1)} %slice_bitcast_fusion.3), channel_id=1, source_target_pairs={{0,1},{1,2},{2,3},{3,4},{4,5},{5,6},{6,7},{8,9},{9,10},{10,11},{11... | collective-permute-start | bytes 98312 | tf_op jit(solution)/shard_map/ppermute | solution.py:1111
  57.8 6.2 %copy-start.7 = (bf16[272,1024]{1,0:T(8,128)(2,1)}, bf16[272,1024]{1,0:T(8,128)(2,1)S(1)}, u32[]{:S(2)}) copy-start(bf16[272,1024]{1,0:T(8,128)(2,1)S(1)} %multiply_convert_fusion.4) | copy-start | bytes 1671172
  57.8 6.2 %copy-start.43 = (f32[8]{0:T(128)S(1)}, f32[8]{0:T(128)}, u32[]{:S(2)}) copy-start(f32[8]{0:T(128)} %param.20) | copy-start | bytes 100
  162.7 3.4 copy-start.37
  165.6 2.2 copy-start.10
  166.1 2.6 copy-start.38
  166.1 4.3 slice-start
  167.8 2.8 slice-start.1
  168.8 1.9 copy-start.23
  174.6 1.7 copy-start.39
  174.6 1.7 copy-start.41
  178.8 2.2 copy-start.1
  250.1 3.7 copy-start.6
  257.2 1.7 copy-start.9
  258.5 49.3 %collective-permute-start.8 = (bf16[256,1024]{1,0:T(8,128)(2,1)}, bf16[256,1024]{1,0:T(8,128)(2,1)}, u32[]{:S(2)}, u32[]{:S(2)}) collective-permute-start(bf16[256,1024]{1,0:T(8,128)(2,1)} %get-tuple-element.137), channel_id=1, source_target_pairs={{0,1},{1,0},{2,3},{3,2},{4,5},{5,4},{6,7},{7,6},{8,9},{9,8},{10,11... | collective-permute-start | bytes 1572872 | tf_op jit(solution)/shard_map/ppermute | solution.py:349
  264.0 5.7 %copy-start.12 = (f32[256,8]{1,0:T(8,128)S(1)}, f32[256,8]{1,0:T(8,128)}, u32[]{:S(2)}) copy-start(f32[256,8]{1,0:T(8,128)} %fusion.27.refs_7_.rate_ref) | copy-start | bytes 24580
  264.0 5.7 %copy-start.33 = (f32[256,8]{1,0:T(8,128)S(1)}, f32[256,8]{1,0:T(8,128)}, u32[]{:S(2)}) copy-start(f32[256,8]{1,0:T(8,128)} %get-tuple-element.70) | copy-start | bytes 24580
  264.0 6.2 %copy-start.8 = (bf16[272,1024]{1,0:T(8,128)(2,1)S(1)}, bf16[272,1024]{1,0:T(8,128)(2,1)}, u32[]{:S(2)}) copy-start(bf16[272,1024]{1,0:T(8,128)(2,1)} %copy-done.7) | copy-start | bytes 1671172
  264.0 7.4 %copy-start.14 = (f32[272,1024]{1,0:T(8,128)S(1)}, f32[272,1024]{1,0:T(8,128)}, u32[]{:S(2)}) copy-start(f32[272,1024]{1,0:T(8,128)} %fusion.7) | copy-start | bytes 3342340
  269.7 1.7 copy-start.13
  270.2 3.7 copy-start.19
  271.4 4.6 copy-start.34
  274.0 5.3 %copy-start.3 = (f32[272,1024]{1,0:T(8,128)}, f32[272,1024]{1,0:T(8,128)S(1)}, u32[]{:S(2)}) copy-start(f32[272,1024]{1,0:T(8,128)S(1)} %fusion.19) | copy-start | bytes 3342340
  274.7 23.0 %collective-permute-start.1 = (bf16[16,1024]{1,0:T(8,128)(2,1)}, bf16[16,1024]{1,0:T(8,128)(2,1)}, u32[]{:S(2)}, u32[]{:S(2)}) collective-permute-start(bf16[16,1024]{1,0:T(8,128)(2,1)} %slice.152), channel_id=1, source_target_pairs={{1,0},{2,1},{3,2},{4,3},{5,4},{6,5},{7,6},{9,8},{10,9},{11,10},{12... | collective-permute-start | bytes 98312 | tf_op jit(solution)/shard_map/ppermute | solution.py:1179
  276.6 34.5 %collective-permute-start.12 = (bf16[272,1024]{1,0:T(8,128)(2,1)}, bf16[272,1024]{1,0:T(8,128)(2,1)}, u32[]{:S(2)}, u32[]{:S(2)}) collective-permute-start(bf16[272,1024]{1,0:T(8,128)(2,1)} %get-tuple-element.142), channel_id=1, source_target_pairs={{0,1},{1,0},{2,3},{3,2},{4,5},{5,4},{6,7},{7,6},{8,9},{9,8},{10,11... | collective-permute-start | bytes 1671176 | tf_op jit(solution)/shard_map/ppermute | solution.py:349
  279.5 7.2 %copy-start.2 = (bf16[256,2816]{0,1:T(8,128)(2,1)S(1)}, bf16[256,2816]{0,1:T(8,128)(2,1)}, u32[]{:S(2)}) copy-start(bf16[256,2816]{0,1:T(8,128)(2,1)} %copy.65) | copy-start | bytes 4325380
  280.3 26.2 %collective-permute-start.9 = (bf16[272,512]{1,0:T(8,128)(2,1)}, bf16[272,512]{1,0:T(8,128)(2,1)}, u32[]{:S(2)}, u32[]{:S(2)}) collective-permute-start(bf16[272,512]{1,0:T(8,128)(2,1)} %bitcast.112), channel_id=1, source_target_pairs={{0,1},{1,0},{2,3},{3,2},{4,5},{5,4},{6,7},{7,6},{8,9},{9,8},{10,11... | collective-permute-start | bytes 835592 | tf_op jit(solution)/shard_map/ppermute | solution.py:349
  286.1 19.5 %collective-permute-start.7 = (bf16[256,512]{0,1:T(8,128)(2,1)}, bf16[256,512]{0,1:T(8,128)(2,1)}, u32[]{:S(2)}, u32[]{:S(2)}) collective-permute-start(bf16[256,512]{0,1:T(8,128)(2,1)} %bitcast.149), channel_id=1, source_target_pairs={{0,1},{1,0},{2,3},{3,2},{4,5},{5,4},{6,7},{7,6},{8,9},{9,8},{10,11... | collective-permute-start | bytes 786440 | tf_op jit(solution)/shard_map/ppermute | solution.py:349
  286.7 5.8 %copy-start.35 = (f32[8,1,128]{2,1,0:T(1,128)S(1)}, f32[8,1,128]{2,1,0:T(1,128)}, u32[]{:S(2)}) copy-start(f32[8,1,128]{2,1,0:T(1,128)} %get-tuple-element.72) | copy-start | bytes 12292
  288.4 9.3 %copy-start.4 = (f32[272,1024]{1,0:T(8,128)S(1)}, f32[272,1024]{1,0:T(8,128)}, u32[]{:S(2)}) copy-start(f32[272,1024]{1,0:T(8,128)} %copy-done.3) | copy-start | bytes 3342340
  290.5 5.8 %copy-start.11 = (bf16[256,4,1,128]{3,2,1,0:T(2,128)(2,1)S(1)}, bf16[256,4,1,128]{3,2,1,0:T(2,128)(2,1)}, u32[]{:S(2)}) copy-start(bf16[256,4,1,128]{3,2,1,0:T(2,128)(2,1)} %get-tuple-element.151) | copy-start | bytes 786436
  297.6 2.9 copy-start.36
  297.7 4.9 copy-start.5
  301.7 3.6 copy-start.42
  301.7 3.5 collective-permute-start.13
  302.6 3.1 copy-start.21
  302.6 3.9 copy-start.40
  302.6 4.3 copy-start.32
  302.6 5.3 %copy-start.20 = (bf16[272,1024]{1,0:T(8,128)(2,1)S(1)}, bf16[272,1024]{1,0:T(8,128)(2,1)}, u32[]{:S(2)}) copy-start(bf16[272,1024]{1,0:T(8,128)(2,1)} %get-tuple-element.144) | copy-start | bytes 1671172
  302.6 5.5 %copy-start.27 = (bf16[256,4,1,128]{0,3,1,2:T(8,128)(2,1)S(1)}, bf16[256,4,1,128]{0,3,1,2:T(8,128)(2,1)}, u32[]{:S(2)}) copy-start(bf16[256,4,1,128]{0,3,1,2:T(8,128)(2,1)} %copy.80) | copy-start | bytes 786436
  305.2 17.1 %collective-permute-start.6 = (bf16[256,2816]{1,0:T(8,128)(2,1)S(1)}, bf16[256,2816]{1,0:T(8,128)(2,1)S(1)}, u32[]{:S(2)}, u32[]{:S(2)}) collective-permute-start(bf16[256,2816]{1,0:T(8,128)(2,1)S(1)} %copy-done.42), channel_id=1, source_target_pairs={{0,1},{1,0},{2,3},{3,2},{4,5},{5,4},{6,7},{7,6},{8,9},{9,8},{10,11... | collective-permute-start | bytes 4325384 | tf_op jit(solution)/shard_map/ppermute | solution.py:349
  305.6 8.9 %collective-permute-start.11 = (bf16[272,1024]{1,0:T(8,128)(2,1)S(1)}, bf16[272,1024]{1,0:T(8,128)(2,1)S(1)}, u32[]{:S(2)}, u32[]{:S(2)}) collective-permute-start(bf16[272,1024]{1,0:T(8,128)(2,1)S(1)} %copy-done.21), channel_id=1, source_target_pairs={{0,1},{1,0},{2,3},{3,2},{4,5},{5,4},{6,7},{7,6},{8,9},{9,8},{10,11... | collective-permute-start | bytes 1671176 | tf_op jit(solution)/shard_map/ppermute | solution.py:349
  306.4 19.2 %collective-permute-start.5 = (bf16[256,2816]{1,0:T(8,128)(2,1)S(1)}, bf16[256,2816]{1,0:T(8,128)(2,1)S(1)}, u32[]{:S(2)}, u32[]{:S(2)}) collective-permute-start(bf16[256,2816]{1,0:T(8,128)(2,1)S(1)} %copy-done.40), channel_id=1, source_target_pairs={{0,1},{1,0},{2,3},{3,2},{4,5},{5,4},{6,7},{7,6},{8,9},{9,8},{10,11... | collective-permute-start | bytes 4325384 | tf_op jit(solution)/shard_map/ppermute | solution.py:349
  307.8 3.3 copy-start.18
  307.8 3.7 copy-start.22
  307.9 8.9 %collective-permute-start.10 = (bf16[272,1024]{1,0:T(8,128)(2,1)S(1)}, bf16[272,1024]{1,0:T(8,128)(2,1)S(1)}, u32[]{:S(2)}, u32[]{:S(2)}) collective-permute-start(bf16[272,1024]{1,0:T(8,128)(2,1)S(1)} %copy-done.20), channel_id=1, source_target_pairs={{0,1},{1,0},{2,3},{3,2},{4,5},{5,4},{6,7},{7,6},{8,9},{9,8},{10,11... | collective-permute-start | bytes 1671176 | tf_op jit(solution)/shard_map/ppermute | solution.py:349
  311.1 3.4 copy-start.24
  311.1 8.0 %collective-permute-start.2 = (bf16[256,1408]{0,1:T(8,128)(2,1)S(1)}, bf16[256,1408]{0,1:T(8,128)(2,1)S(1)}, u32[]{:S(2)}, u32[]{:S(2)}) collective-permute-start(bf16[256,1408]{0,1:T(8,128)(2,1)S(1)} %bitcast.138), channel_id=1, source_target_pairs={{0,1},{1,0},{2,3},{3,2},{4,5},{5,4},{6,7},{7,6},{8,9},{9,8},{10,11... | collective-permute-start | bytes 2162696 | tf_op jit(solution)/shard_map/ppermute | solution.py:349
  314.5 2.3 copy-start.26
  314.5 4.6 collective-permute-start.3
  316.8 2.3 copy-start.17
  316.8 5.6 %collective-permute-start.4 = (bf16[256,512]{0,1:T(8,128)(2,1)S(1)}, bf16[256,512]{0,1:T(8,128)(2,1)S(1)}, u32[]{:S(2)}, u32[]{:S(2)}) collective-permute-start(bf16[256,512]{0,1:T(8,128)(2,1)S(1)} %bitcast.147), channel_id=1, source_target_pairs={{0,1},{1,0},{2,3},{3,2},{4,5},{5,4},{6,7},{7,6},{8,9},{9,8},{10,11... | collective-permute-start | bytes 786440 | tf_op jit(solution)/shard_map/ppermute | solution.py:349
  319.1 3.2 copy-start.25
  500.6 6.3 %copy-start.16 = (bf16[128,2816]{1,0:T(8,128)(2,1)S(1)}, bf16[128,2816]{1,0:T(8,128)(2,1)}, u32[]{:S(2)}) copy-start(bf16[128,2816]{1,0:T(8,128)(2,1)} %get-tuple-element.79) | copy-start | bytes 2162692
  504.5 3.6 copy-start.15
  506.9 2.5 copy-start.31
  506.9 4.7 copy-start.28
  506.9 4.7 copy-start.29
  506.9 4.7 copy-start.30

commit v3 on v2

--- a/solution.py
+++ b/solution.py
@@ -135,7 +135,7 @@
     end_ref[0] = running.astype(BF16)
 
 
-def adjoint_kernel(
+def adjoint_body(
     keep_ref, gn_ref, read_ref, gain_ref, q_ref, k_ref, wk_ref, go_ref, adj_ref, gain_grad_ref
 ):
     grad, readout = gn_ref[...], read_ref[...]
@@ -166,43 +166,13 @@
     adj_ref[0] = adj.astype(BF16)
 
 
-def adjoint_call(keep, grad_normal, readout, gain, queries, keys, wkeys, heads):
-    tok, width = readout.shape
-    size = width // heads
-    block = pl.BlockSpec((tok, size), lambda h: (0, h))
-    return pl.pallas_call(
-        adjoint_kernel,
-        grid=(heads,),
-        in_specs=[
-            pl.BlockSpec(memory_space=pltpu.SMEM),
-            block, block,
-            pl.BlockSpec((1, size), lambda h: (0, 0)),
-            block, block, block,
-        ],
-        out_specs=[
-            block,
-            pl.BlockSpec((1, size, size), lambda h: (h, 0, 0)),
-            pl.BlockSpec((1, 1, size), lambda h: (h, 0, 0)),
-        ],
-        out_shape=[
-            jax.ShapeDtypeStruct((tok, width), BF16),
-            jax.ShapeDtypeStruct((heads, size, size), BF16),
-            jax.ShapeDtypeStruct((heads, 1, size), F32),
-        ],
-        compiler_params=pltpu.CompilerParams(vmem_limit_bytes=VMEM_LIMIT),
-        cost_estimate=pl.CostEstimate(flops=5 * 10**8, bytes_accessed=6 * 10**6, transcendentals=0),
-        name="delta_adjoint",
-    )(keep, grad_normal, readout, gain, queries, keys, wkeys)
-
-
-def backward_kernel(
-    keep_ref, din_ref, min_ref, pre_ref, go_ref, q_ref, k_ref, v_ref, inv_ref, wk_ref,
+def backward_body(
+    head, keep_ref, din_ref, min_ref, pre_ref, go_ref, q_ref, k_ref, v_ref, inv_ref, wk_ref,
     nv_ref, np_ref, rate_ref, allow_ref,
     eq_ref, ek_ref, ev_ref, cq_ref, ck_ref, cv_ref,
     gext_ref, gconv_ref, grate_ref,
     gq_buf, gk_buf, gv_buf,
 ):
-    head = pl.program_id(0)
     size = q_ref.shape[1]
     tok = q_ref.shape[0]
     count = tok // STRETCH
@@ -278,56 +248,6 @@
         gext_ref[i] = total.astype(BF16)
 
 
-def backward_call(
-    keep, state_grad, state, prefix, grad_read, queries, keys, values, invs, wkeys,
-    new_v, new_p, rate, allow, ext, conv, heads,
-):
-    tok, width = queries.shape
-    size = width // heads
-    count = tok // STRETCH
-    taps = conv.shape[0]
-    rows = ext.shape[0]
-    block = pl.BlockSpec((tok, size), lambda h: (0, h))
-    square = pl.BlockSpec((1, size, size), lambda h: (h, 0, 0))
-
-    def third(i, r):
-        return pl.BlockSpec((r, size), lambda h: (0, h + i * heads))
-
-    return pl.pallas_call(
-        backward_kernel,
-        grid=(heads,),
-        in_specs=[
-            pl.BlockSpec(memory_space=pltpu.SMEM),
-            square, square,
-            pl.BlockSpec((1, count, 2 * size, size), lambda h: (h, 0, 0, 0)),
-            block, block, block, block,
-            pl.BlockSpec((1, tok, STRETCH), lambda h: (h, 0, 0)),
-            block, block, block,
-            pl.BlockSpec((tok, heads), lambda h: (0, 0)),
-            pl.BlockSpec((tok, taps), lambda h: (0, 0)),
-            third(0, rows), third(1, rows), third(2, rows),
-            third(0, taps), third(1, taps), third(2, taps),
-        ],
-        out_specs=[
-            pl.BlockSpec((3, rows, size), lambda h: (0, 0, h)),
-            pl.BlockSpec((3, taps, size), lambda h: (0, 0, h)),
-            pl.BlockSpec((tok, heads), lambda h: (0, 0)),
-        ],
-        out_shape=[
-            jax.ShapeDtypeStruct((3, rows, width), BF16),
-            jax.ShapeDtypeStruct((3, taps, width), F32),
-            jax.ShapeDtypeStruct((tok, heads), F32),
-        ],
-        scratch_shapes=[pltpu.VMEM((tok, size), F32)] * 3,
-        compiler_params=pltpu.CompilerParams(vmem_limit_bytes=VMEM_LIMIT),
-        cost_estimate=pl.CostEstimate(flops=2 * 10**9, bytes_accessed=12 * 10**6, transcendentals=10**6),
-        name="delta_backward",
-    )(
-        keep, state_grad, state, prefix, grad_read, queries, keys, values, invs, wkeys,
-        new_v, new_p, rate, allow, ext, ext, ext, conv, conv, conv,
-    )
-
-
 def silu_slope(pre_act, sig_value):
     return sig_value * (1.0 + pre_act * (1.0 - sig_value))
 
@@ -890,15 +810,6 @@
     if not backward:
         scratch.append(pltpu.VMEM((half, size, size), F32))
     return scratch + [dma((2,)), dma((half, 2)), dma((2,))]
-
-
-def chain_kernel(streams, spans, backward, *refs):
-    p = Place(streams, spans)
-    greet([p.other(), p.along(1), p.along(-1)])
-    if backward:
-        chain_body(p, True, refs[0], refs[1:4], refs[4], refs[5:])
-    else:
-        chain_body(p, False, refs[0], refs[2:5], refs[1], refs[5:])
 
 
 def readout_body(readout, gain):
@@ -1034,27 +945,142 @@
     return outs[:14], outs[14:]
 
 
-def chain_call(maps, carried, collective_id):
+def backward_kernel(streams, spans, heads, weights, *refs):
+    (keep_ref, gn_ref, read_ref, gain_ref, q_ref, k_ref, v_ref, wk_ref, inv_ref, min_ref, pre_ref,
+     nv_ref, np_ref, rate_ref, allow_ref, eq_ref, ek_ref, ev_ref, cq_ref, ck_ref, cv_ref,
+     p_low, p_high, p_chip) = refs[:24]
+    refs = refs[24:]
+    grads, refs = refs[:weights], refs[weights:]
+    gext_ref, gconv_ref, grate_ref, gain_grad_ref = refs[:4]
+    sums, refs = refs[4 : 4 + weights], refs[4 + weights :]
+    bufs, refs = [refs[6 * w : 6 * w + 6] for w in range(weights)], refs[6 * weights :]
+    reduce_sems, refs = refs[:3], refs[3:]
+    go_buf, adj_buf, din_buf = refs[:3]
+    row_bufs, chain_bufs = refs[3:6], refs[6:]
+    step_id = pl.program_id(0)
+    place = Place(streams, spans)
+    work = Reduce(place, grads, sums, bufs, reduce_sems)
+    steps = work.steps()
+    slots = 2 * heads + 2
+
+    @pl.when(step_id == 0)
+    def _():
+        greet(work.neighbours() + [place.other()])
+
+    for index in range(2 * heads + 1):
+
+        @pl.when(step_id == index)
+        def _():
+            for step in spread_steps(steps, slots, index):
+                step()
+
+    @pl.when(step_id < heads)
+    def _():
+        adjoint_body(
+            keep_ref, gn_ref, read_ref, gain_ref, q_ref, k_ref, wk_ref,
+            go_buf.at[step_id], adj_buf.at[pl.ds(step_id, 1)], gain_grad_ref,
+        )
+
+    @pl.when(step_id == heads)
+    def _():
+        chain_body(place, True, adj_buf, (p_low, p_high, p_chip), din_buf, chain_bufs)
+
+    @pl.when(step_id > heads)
+    def _():
+        head = step_id - heads - 1
+        backward_body(
+            head, keep_ref, din_buf.at[pl.ds(head, 1)], min_ref, pre_ref, go_buf.at[head],
+            q_ref, k_ref, v_ref, inv_ref, wk_ref, nv_ref, np_ref, rate_ref, allow_ref,
+            eq_ref, ek_ref, ev_ref, cq_ref, ck_ref, cv_ref,
+            gext_ref, gconv_ref, grate_ref, *row_bufs,
+        )
+
+    @pl.when(step_id == 2 * heads)
+    def _():
+        for step in spread_steps(steps, slots, slots - 1):
+            step()
+
+
+def backward_call(
+    keep, grad_normal, readout, gain, queries, keys, values, wkeys, invs, state, prefix,
+    new_v, new_p, rate, allow, ext, conv, maps, grads, heads, collective_id,
+):
     streams, spans = lax.axis_size("stream"), lax.axis_size("span")
-    backward = carried is not None
-    heads, size = maps.shape[0], maps.shape[2]
+    tok, width = queries.shape
+    size = width // heads
+    count = tok // STRETCH
+    taps = conv.shape[0]
+    rows = ext.shape[0]
     half = heads // 2
+
+    def first(i):
+        return jnp.minimum(i, heads - 1)
+
+    def second(i):
+        return jnp.maximum(i - heads - 1, 0)
+
+    def both(i):
+        return jnp.where(i < heads, i, jnp.maximum(i - heads - 1, 0))
+
+    def block(at):
+        return pl.BlockSpec((tok, size), lambda h: (0, at(h)))
+
+    def third(i, r):
+        return pl.BlockSpec((r, size), lambda h: (0, second(h) + i * heads))
+
+    def whole(*shape):
+        return pl.BlockSpec(shape, lambda h: (0,) * len(shape))
+
     vmem = pl.BlockSpec(memory_space=pltpu.VMEM)
-    square = jax.ShapeDtypeStruct((half, size, size), BF16)
-    state = jax.ShapeDtypeStruct((heads, size, size), BF16)
-    scratch = chain_scratch(heads, size, maps.shape[1], backward)
-    operands = [maps] + (list(carried) if backward else [])
-    return pl.pallas_call(
-        functools.partial(chain_kernel, streams, spans, backward),
-        in_specs=[vmem] * len(operands),
-        out_specs=[vmem] * (1 if backward else 4),
-        out_shape=[state] if backward else [state, square, square, square],
-        scratch_shapes=scratch,
+    shapes = [g.shape for g in grads]
+    outs = pl.pallas_call(
+        functools.partial(backward_kernel, streams, spans, heads, len(grads)),
+        grid=(2 * heads + 1,),
+        in_specs=[
+            pl.BlockSpec(memory_space=pltpu.SMEM),
+            block(first), block(first), whole(1, size),
+            block(both), block(both), block(second), block(both),
+            pl.BlockSpec((1, tok, STRETCH), lambda h: (second(h), 0, 0)),
+            pl.BlockSpec((1, size, size), lambda h: (second(h), 0, 0)),
+            pl.BlockSpec((1, count, 2 * size, size), lambda h: (second(h), 0, 0, 0)),
+            block(second), block(second),
+            whole(tok, heads), whole(tok, taps),
+            third(0, rows), third(1, rows), third(2, rows),
+            third(0, taps), third(1, taps), third(2, taps),
+            whole(half, size, size), whole(half, size, size), whole(half, size, size),
+        ]
+        + [vmem] * len(grads),
+        out_specs=[
+            pl.BlockSpec((3, rows, size), lambda h: (0, 0, second(h))),
+            pl.BlockSpec((3, taps, size), lambda h: (0, 0, second(h))),
+            whole(tok, heads),
+            pl.BlockSpec((1, 1, size), lambda h: (first(h), 0, 0)),
+        ]
+        + [vmem] * len(grads),
+        out_shape=[
+            jax.ShapeDtypeStruct((3, rows, width), BF16),
+            jax.ShapeDtypeStruct((3, taps, width), F32),
+            jax.ShapeDtypeStruct((tok, heads), F32),
+            jax.ShapeDtypeStruct((heads, 1, size), F32),
+        ]
+        + [jax.ShapeDtypeStruct(g.shape[1:], g.dtype) for g in grads],
+        scratch_shapes=Reduce.scratch(shapes, [g.dtype for g in grads], streams)
+        + [
+            pltpu.VMEM((heads, tok, size), BF16),
+            pltpu.VMEM((heads, size, size), BF16),
+            pltpu.VMEM((heads, size, size), BF16),
+        ]
+        + [pltpu.VMEM((tok, size), F32)] * 3
+        + chain_scratch(heads, size, size, True),
         compiler_params=pltpu.CompilerParams(
             collective_id=collective_id, has_side_effects=True, vmem_limit_bytes=VMEM_LIMIT
         ),
-        name="span_chain",
-    )(*operands)
+        name="delta_backward",
+    )(
+        keep, grad_normal, readout, gain, queries, keys, values, wkeys, invs, state, prefix,
+        new_v, new_p, rate, allow, ext, ext, ext, conv, conv, conv, *maps, *grads,
+    )
+    return outs[:4], outs[4:]
 
 
 def local(
@@ -1154,15 +1180,12 @@
     grad_middle = grad_branch.astype(F32) + norm_back(grad_nffn, middle, inv_second, ffn_gain)
     grad_attn_in = grad_middle.astype(BF16)
     grad_normal = product("td,kd->tk", grad_attn_in, full_out)
-    grad_read, device_adjoint, head_grads = adjoint_call(
-        stretch_keep, grad_normal, readout, head_gain, queries, keys, wkeys, heads
-    )
     pair_heads = pair_columns(normal_heads, span_count)
     half_out = weight_grad(pair_heads, pair_tokens(grad_attn_in), span_count)
-    (state_grad,) = chain_call(device_adjoint, (p_low, p_high, p_chip), 4)
-    grad_ext, grad_conv, grad_strength = backward_call(
-        stretch_keep, state_grad, state_in, prefix, grad_read, queries, keys, values, invs, wkeys,
-        new_v, new_p, strength, allow, projected, full_conv, heads,
+    (grad_ext, grad_conv, grad_strength, head_grads), ffn_parts = backward_call(
+        stretch_keep, grad_normal, readout, head_gain, queries, keys, values, wkeys, invs,
+        state_in, prefix, new_v, new_p, strength, allow, projected, full_conv,
+        (p_low, p_high, p_chip), [half_down, half_gate, half_up], heads, 4,
     )
     pair_normed = pair_columns(normed_ext, span_count)
     half_q, half_k, half_v = (
@@ -1208,12 +1231,11 @@
     half_small = lax.dynamic_index_in_dim(packed, core, 1, keepdims=False) + swap_core(
         lax.dynamic_index_in_dim(packed, 1 - core, 1, keepdims=False)
     )
-    parts = reduce_call(
-        [half_down, half_gate, half_up, half_out, half_q, half_k, half_v, half_small], 5
-    )
-    part_down, part_gate, part_up, part_out = (x.astype(F32) for x in parts[:4])
-    part_qkv = jnp.concatenate([x.astype(F32) for x in parts[4:7]], 1)
-    part_small = parts[7].reshape(-1)
+    parts = reduce_call([half_out, half_q, half_k, half_v, half_small], 5)
+    part_down, part_gate, part_up = (x.astype(F32) for x in ffn_parts)
+    part_out = parts[0].astype(F32)
+    part_qkv = jnp.concatenate([x.astype(F32) for x in parts[1:4]], 1)
+    part_small = parts[4].reshape(-1)
     sums = []
     at = 0
     for like in (conv_weight, w_beta, norm_attn, norm_ffn, norm_head, beta_bias):

time: 522 us -> 500 us (0.958)
  Pallas kernels: 376 us -> 353 us
  local copies, waits for them, and re-layouts: 46.6 us -> 40.4 us
  matrix products: 63.2 us -> 69.1 us
    pallas_call x1, Pallas kernels: 172 us -> 78.4 us  [reduce_call(): pl.pallas_call(functools.partial(reduce_kernel, streams, spans, len(grads...]
    pallas_call x3 -> x1, Pallas kernels: 66.3 us -> 137 us  [backward_call(): pl.pallas_call(functools.partial(backward_kernel, streams, spans, heads,...]
    dot_general x16, matrix products: 44.3 us -> 53.7 us  [product(): jnp.einsum(pattern, first, second, preferred_element_type=F32).astype(kind)]
    unnamed x108 -> x72, local copies, waits for them, and re-layouts: 17 us -> 15.4 us
where the time goes in v3:
time: 500 us; the launch traced here: 492 us
  Pallas kernels  353 us (71%)
  matrix products  69.1 us (14%)
  local copies, waits for them, and re-layouts  40.4 us (8%)
  other arithmetic  19.4 us (4%)
  starting transfers between devices  7.72 us (2%)
    pallas_call x1, Pallas kernels, backward_call(): pl.pallas_call(functools.partial(backward_kernel, streams, spans, heads,...  137 us
    pallas_call x1, Pallas kernels, forward_call(): pl.pallas_call(functools.partial(forward_kernel, streams, spans, heads, l...  97.6 us
    pallas_call x1, Pallas kernels, reduce_call(): pl.pallas_call(functools.partial(reduce_kernel, streams, spans, len(grads...  78.4 us
    dot_general x16, matrix products, product(): jnp.einsum(pattern, first, second, preferred_element_type=F32).astype(kind)  53.7 us
    pallas_call x1, Pallas kernels, gather_call(): pl.pallas_call(functools.partial(gather_kernel, streams, spans, len(shard...  40.3 us
    unnamed x72, local copies, waits for them, and re-layouts  15.4 us
  transfers between devices with their start and end apart: 14, of which 0 were waited for; matrix products, arithmetic and copies ran while one was open for 14% of the time, Pallas kernels for 8%

profile of v3, /device:TPU:0, one launch (start us, length us, event | category | flops | bytes accessed | tf_op | source)
XLA Modules:
  0.0 491.5 jit_solution(9420856594403382534)
XLA Ops:
  0.7 0.8 slice_bitcast_fusion.3
  1.5 2.3 collective-permute-start
  3.8 0.8 reduce-window_clone.1
  6.7 0.8 copy.61
  8.1 0.8 dynamic-update-slice.4
  9.0 0.8 dynamic-update-slice.5
  9.8 0.8 dynamic-update-slice.6
  11.3 40.3 %gather_weights.1 = (bf16[8,128,3072]{2,1,0:T(8,128)(2,1)}, bf16[8,16,512]{2,1,0:T(8,128)(2,1)}) custom-call(bf16[128,3072]{1,0:T(8,128)(2,1)} %refs_0_.1, bf16[16,512]{1,0:T(8,128)(2,1)} %reshape.354.refs_1_), custom_call_target="tpu_custom_call" | custom-call | tf_op jit(solution)/shard_map/gather_weights/pallas_call | solution.py:519
  51.6 1.0 copy.82
  52.8 1.4 concatenate.65
  55.2 0.8 copy.63.refs_8_.refs_14_
  56.6 1.0 copy.71
  58.0 5.9 %convolution_convert_fusion.2.refs_1_.refs_2_.refs_3_.refs_15_.refs_16_.refs_17_ = bf16[272,3072]{1,0:T(8,128)(2,1)} fusion(bf16[272,1024]{1,0:T(8,128)(2,1)S(1)} %multiply_convert_fusion.4, bf16[1024,3072]{1,0:T(8,128)(2,1)} %bitcast.138), kind=kOutput, calls=%fused_computation.3 | convolution fusion | flops 1712111616 | bytes 8519680 | tf_op jit(solution)/shard_map/dot_general | solution.py:1144
  63.9 1.0 fusion.27.refs_7_.refs_13_
  64.9 97.6 %delta_forward.1 = (bf16[256,1024]{1,0:T(8,128)(2,1)}, bf16[256,1024]{1,0:T(8,128)(2,1)}, bf16[256,1024]{1,0:T(8,128)(2,1)}, bf16[8,256,64]{2,1,0:T(8,128)(2,1)}...) custom-call(f32[4]{0:T(128)} %broadcast_subtract_fusion.refs_0_, ...), custom_call_target="tpu_custom_call" | custom-call | tf_op jit(solution)/shard_map/delta_forward/pallas_call | solution.py:899
  162.6 2.7 multiply_reduce_fusion.5
  166.0 1.7 fusion.67
  168.2 1.7 fusion.68
  170.1 4.0 multiply_convert_fusion
  174.1 1.1 copy-done.8
  175.2 2.5 fusion.23
  177.6 2.7 copy.64
  180.4 4.8 fusion.69
  185.8 5.0 %multiply_reduce_fusion.1 = (f32[1024]{0:T(1024)S(1)}, f32[256]{0:T(256)S(1)}, f32[256,1024]{1,0:T(8,128)S(1)}) fusion(f32[256,1024]{1,0:T(8,128)S(1)} %get-tuple-element.163, f32[256]{0:T(256)S(1)} %get-tuple-element.157, f32[1024]{0:T(1024)S(1)} %get-tuple-element.153, f32[256,1024]{1,0:T(8,128)S(1)} %fusion.69, ...), kind=kOutput, calls=%fused_computation.60 | convolution fusion | flops 1478228736 | bytes 10364928 | tf_op jit(solution)/shard_map/tf,df->td/dot_general | solution.py:261
  190.8 1.5 fusion.65
  192.9 2.8 fusion.70.refs_1_
  196.3 2.1 constant_dynamic-slice_fusion.3
  198.3 2.0 copy.81
  200.7 1.4 multiply_convert_fusion.3
  202.3 0.8 copy.90
  203.3 1.2 constant_dynamic-slice_fusion.7
  204.8 1.4 reshape.368
  206.5 2.1 constant_dynamic-slice_fusion.5
  208.6 1.2 copy.79
  209.8 1.2 copy.78
  211.1 0.7 copy.80
  211.8 1.0 constant_dynamic-update-slice_fusion
  213.6 3.0 convolution_convert_fusion.7
  216.6 4.6 convolution_convert_fusion.3
  221.2 5.0 %convolution_convert_fusion.1 = bf16[512,2816]{1,0:T(8,128)(2,1)} fusion(bf16[256,2816]{1,0:T(8,128)(2,1)} %collective-permute-done.4, bf16[256,2816]{1,0:T(8,128)(2,1)} %get-tuple-element.136, bf16[256,512]{0,1:T(8,128)(2,1)S(1)} %collective-permute-done.3, bf16[256,512]{0,1:T(8,128)(2,1)S(1)} %bitcast.144), kind=kOutput, calls=%fused_computation.1 | convolution fusion | flops 1484652544 | bytes 6291456 | tf_op jit(solution)/shard_map/td,te->de/dot_general | solution.py:261
  226.2 5.0 %convolution_convert_fusion = bf16[512,2816]{1,0:T(8,128)(2,1)} fusion(bf16[256,2816]{1,0:T(8,128)(2,1)} %collective-permute-done.5, bf16[256,2816]{1,0:T(8,128)(2,1)} %get-tuple-element.135, bf16[256,512]{0,1:T(8,128)(2,1)S(1)} %collective-permute-done.3, bf16[256,512]{0,1:T(8,128)(2,1)S(1)} %bitcast.145), kind=kOutput, calls=%fused_computation | convolution fusion | flops 1484652544 | bytes 6291456 | tf_op jit(solution)/shard_map/td,te->de/dot_general | solution.py:261
  231.2 136.8 %delta_backward.1 = (bf16[3,272,1024]{2,1,0:T(8,128)(2,1)}, f32[3,4,1024]{2,1,0:T(4,128)}, f32[256,8]{1,0:T(8,128)}, f32[8,1,128]{2,1,0:T(1,128)}, bf16[352,1024...) custom-call(f32[4]{0:T(128)} %broadcast_subtract_fusion.refs_0_, f32[256,1024]{1,0:T(8,128)} %fusion.70.refs_1_, ...), custom_call_target="tpu_custom_call" | custom-call | tf_op jit(solution)/shard_map/delta_backward/pallas_call | solution.py:1036
  368.1 2.7 fusion.7
  370.7 2.4 fusion.9
  373.1 1.2 slice_bitcast_fusion
  374.4 2.4 fusion.19
  376.8 1.3 collective-permute-start.6
  378.2 1.2 collective-permute-start.10
  379.9 1.1 fusion.46
  381.1 1.3 reshape.384
  382.5 2.4 convert_element_type.151
  384.9 2.3 convert_element_type.152
  387.3 1.3 convert_element_type.153
  388.5 1.4 multiply_reduce_fusion.2
  390.4 2.5 add_bitcast_fusion
  393.6 3.2 convolution_convert_fusion.6
  396.8 3.2 convolution_convert_fusion.5
  400.0 3.2 convolution_convert_fusion.4
  403.2 78.4 %reduce_grads.1 = (bf16[128,1024]{1,0:T(8,128)(2,1)}, bf16[128,1024]{1,0:T(8,128)(2,1)}, bf16[128,1024]{1,0:T(8,128)(2,1)}, bf16[128,1024]{1,0:T(8,128)(2,1)}, f32[16,512]{1,0:T(8,128)}) custom-call(bf16[4,128,1024]{2,1,0:T(8,128)(2,1)} %bitcast.133, bf16[4,128,1024]{2,1,0:T(8,128)(2,1)} %bitcast.134, bf16[4,128,1024]{2,1,0:T(8,128)(2,1)} %bitcast.135, ...), custom_call_target="tpu_custom_call" | custom-call | tf_op jit(solution)/shard_map/reduce_grads/pallas_call | solution.py:704
  481.6 0.7 slice.96
  482.4 0.7 slice.97
  483.1 0.8 copy.87
  486.8 1.8 convert_element_type.150
  488.6 2.4 maximum_convert_fusion
  (139 shorter events, 15.8 us)
Async XLA Ops:
  0.6 56.9 %copy-start = (bf16[1,256,1024]{2,1,0:T(8,128)(2,1)S(1)}, bf16[1,256,1024]{2,1,0:T(8,128)(2,1)}, u32[]{:S(2)}) copy-start(bf16[1,256,1024]{2,1,0:T(8,128)(2,1)} %param.14) | copy-start | bytes 1572868
  1.5 56.1 %collective-permute-start = (bf16[16,1024]{1,0:T(8,128)(2,1)S(1)}, bf16[16,1024]{1,0:T(8,128)(2,1)S(1)}, u32[]{:S(2)}, u32[]{:S(2)}) collective-permute-start(bf16[16,1024]{1,0:T(8,128)(2,1)S(1)} %slice_bitcast_fusion.3), channel_id=1, source_target_pairs={{0,1},{1,2},{2,3},{3,4},{4,5},{5,6},{6,7},{8,9},{9,10},{10,11},{11... | collective-permute-start | bytes 98312 | tf_op jit(solution)/shard_map/ppermute | solution.py:1137
  55.2 8.7 %copy-start.10 = (bf16[1024,8]{1,0:T(8,128)(2,1)}, bf16[1024,8]{1,0:T(8,128)(2,1)S(1)}, u32[]{:S(2)}) copy-start(bf16[1024,8]{1,0:T(8,128)(2,1)S(1)} %reshape_reshape.3) | copy-start | bytes 49156
  58.0 5.9 %copy-start.23 = (f32[8]{0:T(128)S(1)}, f32[8]{0:T(128)}, u32[]{:S(2)}) copy-start(f32[8]{0:T(128)} %param.20) | copy-start | bytes 100
  162.6 3.4 copy-start.22
  165.3 2.6 slice-start
  165.5 2.2 copy-start.6
  166.0 2.2 slice-start.1
  166.0 3.9 slice-start.2
  167.7 2.3 slice-start.3
  168.2 1.9 copy-start.14
  174.1 1.1 copy-start.8
  185.1 36.0 %collective-permute-start.4 = (bf16[256,2816]{1,0:T(8,128)(2,1)}, bf16[256,2816]{1,0:T(8,128)(2,1)}, u32[]{:S(2)}, u32[]{:S(2)}) collective-permute-start(bf16[256,2816]{1,0:T(8,128)(2,1)} %get-tuple-element.136), channel_id=1, source_target_pairs={{0,1},{1,0},{2,3},{3,2},{4,5},{5,4},{6,7},{7,6},{8,9},{9,8},{10,11... | collective-permute-start | bytes 4325384 | tf_op jit(solution)/shard_map/ppermute | solution.py:269
  185.4 5.3 %copy-start.15 = (bf16[1,256,1024]{2,1,0:T(8,128)(2,1)S(1)}, bf16[1,256,1024]{2,1,0:T(8,128)(2,1)}, u32[]{:S(2)}) copy-start(bf16[1,256,1024]{2,1,0:T(8,128)(2,1)} %param.15) | copy-start | bytes 1572868
  185.4 40.8 %collective-permute-start.5 = (bf16[256,2816]{1,0:T(8,128)(2,1)}, bf16[256,2816]{1,0:T(8,128)(2,1)}, u32[]{:S(2)}, u32[]{:S(2)}) collective-permute-start(bf16[256,2816]{1,0:T(8,128)(2,1)} %get-tuple-element.135), channel_id=1, source_target_pairs={{0,1},{1,0},{2,3},{3,2},{4,5},{5,4},{6,7},{7,6},{8,9},{9,8},{10,11... | collective-permute-start | bytes 4325384 | tf_op jit(solution)/shard_map/ppermute | solution.py:269
  190.8 2.2 copy-start.1
  192.3 3.6 copy-start.5
  195.7 17.1 %collective-permute-start.8 = (bf16[256,1024]{1,0:T(8,128)(2,1)}, bf16[256,1024]{1,0:T(8,128)(2,1)}, u32[]{:S(2)}, u32[]{:S(2)}) collective-permute-start(bf16[256,1024]{1,0:T(8,128)(2,1)} %get-tuple-element.133), channel_id=1, source_target_pairs={{0,1},{1,0},{2,3},{3,2},{4,5},{5,4},{6,7},{7,6},{8,9},{9,8},{10,11... | collective-permute-start | bytes 1572872 | tf_op jit(solution)/shard_map/ppermute | solution.py:269
  198.3 4.9 %copy-start.2 = (bf16[256,2816]{0,1:T(8,128)(2,1)S(1)}, bf16[256,2816]{0,1:T(8,128)(2,1)}, u32[]{:S(2)}) copy-start(bf16[256,2816]{0,1:T(8,128)(2,1)} %copy.64) | copy-start | bytes 4325380
  200.3 4.2 collective-permute-start.7
  203.1 3.1 collective-permute-start.9
  204.5 12.1 %collective-permute-start.1 = (bf16[256,1408]{0,1:T(8,128)(2,1)}, bf16[256,1408]{0,1:T(8,128)(2,1)}, u32[]{:S(2)}, u32[]{:S(2)}) collective-permute-start(bf16[256,1408]{0,1:T(8,128)(2,1)} %bitcast.17), channel_id=1, source_target_pairs={{0,1},{1,0},{2,3},{3,2},{4,5},{5,4},{6,7},{7,6},{8,9},{9,8},{10,11... | collective-permute-start | bytes 2162696 | tf_op jit(solution)/shard_map/ppermute | solution.py:269
  206.2 4.8 copy-start.7
  206.3 10.3 %collective-permute-start.2 = (bf16[256,1024]{1,0:T(8,128)(2,1)}, bf16[256,1024]{1,0:T(8,128)(2,1)}, u32[]{:S(2)}, u32[]{:S(2)}) collective-permute-start(bf16[256,1024]{1,0:T(8,128)(2,1)} %bitcast.142), channel_id=1, source_target_pairs={{0,1},{1,0},{2,3},{3,2},{4,5},{5,4},{6,7},{7,6},{8,9},{9,8},{10,11... | collective-permute-start | bytes 1572872 | tf_op jit(solution)/shard_map/ppermute | solution.py:269
  212.8 0.8 copy-start.17
  212.8 3.8 copy-start.13
  212.8 3.8 copy-start.16
  212.8 8.3 %collective-permute-start.3 = (bf16[256,512]{0,1:T(8,128)(2,1)S(1)}, bf16[256,512]{0,1:T(8,128)(2,1)S(1)}, u32[]{:S(2)}, u32[]{:S(2)}) collective-permute-start(bf16[256,512]{0,1:T(8,128)(2,1)S(1)} %bitcast.146), channel_id=1, source_target_pairs={{0,1},{1,0},{2,3},{3,2},{4,5},{5,4},{6,7},{7,6},{8,9},{9,8},{10,11... | collective-permute-start | bytes 786440 | tf_op jit(solution)/shard_map/ppermute | solution.py:269
  368.1 2.7 copy-start.4
  374.4 3.8 copy-start.9
  374.4 3.8 copy-start.19
  374.4 6.7 %copy-start.20 = (f32[3,4,1024]{2,1,0:T(4,128)S(1)}, f32[3,4,1024]{2,1,0:T(4,128)}, u32[]{:S(2)}) copy-start(f32[3,4,1024]{2,1,0:T(4,128)} %get-tuple-element.67) | copy-start | bytes 147460
  376.8 5.6 %copy-start.21 = (f32[8,1,128]{2,1,0:T(1,128)S(1)}, f32[8,1,128]{2,1,0:T(1,128)}, u32[]{:S(2)}) copy-start(f32[8,1,128]{2,1,0:T(1,128)} %get-tuple-element.68) | copy-start | bytes 12292
  376.8 11.7 %collective-permute-start.6 = (bf16[16,1024]{1,0:T(8,128)(2,1)S(1)}, bf16[16,1024]{1,0:T(8,128)(2,1)S(1)}, u32[]{:S(2)}, u32[]{:S(2)}) collective-permute-start(bf16[16,1024]{1,0:T(8,128)(2,1)S(1)} %slice.152), channel_id=1, source_target_pairs={{1,0},{2,1},{3,2},{4,3},{5,4},{6,5},{7,6},{9,8},{10,9},{11,10},{12... | collective-permute-start | bytes 98312 | tf_op jit(solution)/shard_map/ppermute | solution.py:1202
  378.2 15.4 %collective-permute-start.10 = (bf16[272,1024]{1,0:T(8,128)(2,1)}, bf16[272,1024]{1,0:T(8,128)(2,1)}, u32[]{:S(2)}, u32[]{:S(2)}) collective-permute-start(bf16[272,1024]{1,0:T(8,128)(2,1)} %get-tuple-element.140), channel_id=1, source_target_pairs={{0,1},{1,0},{2,3},{3,2},{4,5},{5,4},{6,7},{7,6},{8,9},{9,8},{10,11... | collective-permute-start | bytes 1671176 | tf_op jit(solution)/shard_map/ppermute | solution.py:269
  379.4 17.4 %collective-permute-start.11 = (bf16[272,1024]{1,0:T(8,128)(2,1)}, bf16[272,1024]{1,0:T(8,128)(2,1)}, u32[]{:S(2)}, u32[]{:S(2)}) collective-permute-start(bf16[272,1024]{1,0:T(8,128)(2,1)} %get-tuple-element.139), channel_id=1, source_target_pairs={{0,1},{1,0},{2,3},{3,2},{4,5},{5,4},{6,7},{7,6},{8,9},{9,8},{10,11... | collective-permute-start | bytes 1671176 | tf_op jit(solution)/shard_map/ppermute | solution.py:269
  379.5 20.6 %collective-permute-start.12 = (bf16[272,1024]{1,0:T(8,128)(2,1)}, bf16[272,1024]{1,0:T(8,128)(2,1)}, u32[]{:S(2)}, u32[]{:S(2)}) collective-permute-start(bf16[272,1024]{1,0:T(8,128)(2,1)} %get-tuple-element.138), channel_id=1, source_target_pairs={{0,1},{1,0},{2,3},{3,2},{4,5},{5,4},{6,7},{7,6},{8,9},{9,8},{10,11... | collective-permute-start | bytes 1671176 | tf_op jit(solution)/shard_map/ppermute | solution.py:269
  382.5 4.7 copy-start.12
  384.9 3.6 copy-start.11
  388.5 1.9 copy-start.3
  390.2 2.7 collective-permute-start.13
  390.4 3.2 copy-start.18

commit v4 on v3

--- a/solution.py
+++ b/solution.py
@@ -14,6 +14,12 @@
 BF16 = jnp.bfloat16
 AXES = ("stream", "span")
 VMEM_LIMIT = 56 * 2**20
+GATHER_PIECE = 24 * 1024
+GATHER_AHEAD = 4
+GATHER_LAG = 2
+REDUCE_PIECE = 100 * 1024
+REDUCE_AHEAD = 6
+FORWARD_SLOTS = 12
 
 
 def nn(a, b):
@@ -61,8 +67,8 @@
     return jnp.sum(jnp.where(lanes == index, table, 0.0), -1, keepdims=True)
 
 
-def mix_rows(ext_ref, conv_ref, allow):
-    ext = ext_ref[...].astype(F32)
+def mix_rows(ext, conv_ref, allow):
+    ext = ext.astype(F32)
     conv = conv_ref[...].astype(F32)
     shifted = [
         (ext if tap == 0 else pltpu.roll(ext, tap, 0))[HALO:] * allow[tap]
@@ -73,22 +79,25 @@
 
 
 def local_kernel(
-    keep_ref, eq_ref, ek_ref, ev_ref, cq_ref, ck_ref, cv_ref, rate_ref, allow_ref,
-    q_ref, k_ref, v_ref, inv_ref, wk_ref, pre_ref, end_ref, read_ref, rmap_ref, nv_ref, np_ref,
+    keep_ref, normed_ref, wq_ref, wkey_ref, wv_ref, cq_ref, ck_ref, cv_ref, rate_ref, allow_ref,
+    ext_ref, q_ref, k_ref, v_ref, inv_ref, wk_ref, pre_ref, end_ref, read_ref, rmap_ref, nv_ref, np_ref,
 ):
     head = pl.program_id(0)
     allow_all = allow_ref[...]
     allow = [allow_all[:, tap : tap + 1] for tap in range(cq_ref.shape[0])]
     rate = column_of(rate_ref[...], head)
 
-    def unit(ref, conv):
-        _, mixed, _ = mix_rows(ref, conv, allow)
-        act = mixed * jax.nn.sigmoid(mixed)
-        return act
-
-    act_q = unit(eq_ref, cq_ref)
-    act_k = unit(ek_ref, ck_ref)
-    act_v = unit(ev_ref, cv_ref)
+    normed = normed_ref[...]
+
+    def activation(index, weight_ref, conv_ref):
+        ext = nn(normed, weight_ref[...]).astype(BF16)
+        ext_ref[index] = ext
+        _, mixed, _ = mix_rows(ext, conv_ref, allow)
+        return mixed * jax.nn.sigmoid(mixed)
+
+    act_q = activation(0, wq_ref, cq_ref)
+    act_k = activation(1, wkey_ref, ck_ref)
+    act_v = activation(2, wv_ref, cv_ref)
     queries = (act_q * lax.rsqrt(jnp.sum(act_q * act_q, -1, keepdims=True) + EPSILON)).astype(BF16)
     keys = (act_k * lax.rsqrt(jnp.sum(act_k * act_k, -1, keepdims=True) + EPSILON)).astype(BF16)
     values = act_v.astype(BF16)
@@ -167,7 +176,7 @@
 
 
 def backward_body(
-    head, keep_ref, din_ref, min_ref, pre_ref, go_ref, q_ref, k_ref, v_ref, inv_ref, wk_ref,
+    head, begins, keep_ref, din_ref, min_ref, pre_ref, go_ref, q_ref, k_ref, v_ref, inv_ref, wk_ref,
     nv_ref, np_ref, rate_ref, allow_ref,
     eq_ref, ek_ref, ev_ref, cq_ref, ck_ref, cv_ref,
     gext_ref, gconv_ref, grate_ref,
@@ -222,7 +231,7 @@
         gv_buf[part, :] = grad_v
     grate = jnp.concatenate(grate_parts, 0)
     lanes = lax.broadcasted_iota(jnp.int32, grate_ref.shape, 1)
-    before = jnp.where(head == 0, jnp.zeros(grate_ref.shape, F32), grate_ref[...])
+    before = jnp.where(begins, jnp.zeros(grate_ref.shape, F32), grate_ref[...])
     grate_ref[...] = jnp.where(lanes == head, grate, before)
     allow_all = allow_ref[...]
     allow = [allow_all[:, tap : tap + 1] for tap in range(cq_ref.shape[0])]
@@ -230,7 +239,7 @@
     for i, (ext, conv_ref, buf) in enumerate(
         ((eq_ref, cq_ref, gq_buf), (ek_ref, ck_ref, gk_buf), (ev_ref, cv_ref, gv_buf))
     ):
-        shifted, mixed, conv = mix_rows(ext, conv_ref, allow)
+        shifted, mixed, conv = mix_rows(ext[0], conv_ref, allow)
         sig = jax.nn.sigmoid(mixed)
         grad = buf[...]
         if i < 2:
@@ -245,11 +254,98 @@
             if tap:
                 term = pltpu.roll(term, tok + HALO - tap, 0)
             total = term if total is None else total + term
-        gext_ref[i] = total.astype(BF16)
-
-
-def silu_slope(pre_act, sig_value):
-    return sig_value * (1.0 + pre_act * (1.0 - sig_value))
+        gext_ref[:, i * size : (i + 1) * size] = total.astype(BF16)
+
+
+def feed_kernel(
+    core_ref, heads_ref, tok_ref, cot_ref, out_w_ref, gain_ref, gate_ref, up_ref, down_ref,
+    nffn_ref, hidden_ref, mine_ref, theirs_ref, result_ref, gmid_ref, gattn_ref, gnormal_ref,
+    ggain_ref, mid_buf, grad_buf, res_buf,
+):
+    step_id = pl.program_id(0)
+    cot = cot_ref[...]
+
+    @pl.when(step_id == 0)
+    def _():
+        middle = tok_ref[...].astype(F32) + nn(heads_ref[...], out_w_ref[...])
+        inv = lax.rsqrt(jnp.mean(middle * middle, -1, keepdims=True) + EPSILON)
+        mid_buf[...] = middle
+        nffn_ref[...] = (middle * inv * gain_ref[...]).astype(BF16)
+        grad_buf[...] = jnp.zeros(grad_buf.shape, F32)
+        res_buf[...] = middle
+
+    normed = nffn_ref[...]
+    gate_w, up_w, down_w = gate_ref[...], up_ref[...], down_ref[...]
+    gate = nn(normed, gate_w)
+    up = nn(normed, up_w)
+    grad_hidden = nt(cot, down_w)
+    sig = jax.nn.sigmoid(gate)
+    act = gate * sig
+    hidden = (act * up).astype(BF16)
+    grad_gate = (grad_hidden * up * (sig * (1.0 + gate * (1.0 - sig)))).astype(BF16)
+    grad_up = (grad_hidden * act).astype(BF16)
+    low = core_ref[0] == 0
+    hidden_ref[...] = hidden
+    mine_ref[...] = jnp.where(low, grad_gate, grad_up)
+    theirs_ref[...] = jnp.where(low, grad_up, grad_gate)
+    grad_buf[...] += nt(grad_gate, gate_w) + nt(grad_up, up_w)
+    res_buf[...] += nn(hidden, down_w)
+
+    @pl.when(step_id == pl.num_programs(0) - 1)
+    def _():
+        result_ref[...] = res_buf[...].astype(BF16)
+        middle, grad = mid_buf[...], grad_buf[...]
+        inv = lax.rsqrt(jnp.mean(middle * middle, -1, keepdims=True) + EPSILON)
+        ggain_ref[...] = jnp.sum(grad * middle * inv, 0, keepdims=True)
+        scaled = grad * gain_ref[...]
+        total = cot.astype(F32) + inv * scaled - middle * (inv * inv * inv) * jnp.mean(
+            scaled * middle, -1, keepdims=True
+        )
+        gmid_ref[...] = total
+        low_total = total.astype(BF16)
+        gattn_ref[...] = low_total
+        gnormal_ref[...] = nt(low_total, out_w_ref[...])
+
+
+def feed_call(core, normal_heads, tokens, cotangent, w_out, gain, w_gate, w_up, w_down):
+    tok, width = tokens.shape
+    units = w_gate.shape[1]
+    step = 256
+
+    def whole(*shape):
+        return pl.BlockSpec(shape, lambda f: (0,) * len(shape))
+
+    wide = pl.BlockSpec((tok, step), lambda f: (0, f))
+    rows = whole(tok, width)
+    return pl.pallas_call(
+        feed_kernel,
+        grid=(units // step,),
+        in_specs=[
+            pl.BlockSpec(memory_space=pltpu.SMEM),
+            rows, rows, rows, whole(width, width), whole(1, width),
+            pl.BlockSpec((width, step), lambda f: (0, f)),
+            pl.BlockSpec((width, step), lambda f: (0, f)),
+            pl.BlockSpec((step, width), lambda f: (f, 0)),
+        ],
+        out_specs=[rows, wide, wide, wide, rows, rows, rows, rows, whole(1, width)],
+        out_shape=[
+            jax.ShapeDtypeStruct((tok, width), BF16),
+            jax.ShapeDtypeStruct((tok, units), BF16),
+            jax.ShapeDtypeStruct((tok, units), BF16),
+            jax.ShapeDtypeStruct((tok, units), BF16),
+            jax.ShapeDtypeStruct((tok, width), BF16),
+            jax.ShapeDtypeStruct((tok, width), F32),
+            jax.ShapeDtypeStruct((tok, width), BF16),
+            jax.ShapeDtypeStruct((tok, width), F32),
+            jax.ShapeDtypeStruct((1, width), F32),
+        ],
+        scratch_shapes=[pltpu.VMEM((tok, width), F32)] * 3,
+        compiler_params=pltpu.CompilerParams(vmem_limit_bytes=VMEM_LIMIT),
+        cost_estimate=pl.CostEstimate(
+            flops=10**10, bytes_accessed=3 * 10**7, transcendentals=10**6
+        ),
+        name="feed_forward",
+    )(core, normal_heads, tokens, cotangent, w_out, gain, w_gate, w_up, w_down)
 
 
 def norm_back(grad_in, values, inv_rms, gain_vec):
@@ -273,18 +369,17 @@
     return jnp.concatenate([block, swap_core(block)], 0)
 
 
-def pair_columns(block, spans):
+def pair_half(block):
+    width = block.shape[1] // 2
     core = lax.axis_index("span") % 2
-    rows, width = block.shape
-    split = block.reshape(rows, spans // 2, 2, width // spans)
-    mine = lax.dynamic_index_in_dim(split, core, 2, keepdims=False).reshape(rows, -1)
-    theirs = lax.dynamic_index_in_dim(split, 1 - core, 2, keepdims=False).reshape(rows, -1)
+    mine = lax.dynamic_slice_in_dim(block, core * width, width, 1)
+    theirs = lax.dynamic_slice_in_dim(block, (1 - core) * width, width, 1)
     return jnp.concatenate([mine, swap_core(theirs)], 0)
 
 
 def weight_grad(left, right, spans):
     grad = product("td,te->de", left, right, BF16)
-    return grad.reshape(spans // 2, -1, grad.shape[1])
+    return grad.reshape(spans, -1, grad.shape[1])
 
 
 MESH = pl.DeviceIdType.MESH
@@ -324,12 +419,41 @@
     return 2, streams // 2
 
 
-def quarter_index(rows, width, streams, at, piece=0, pieces=1):
+def pieces_of(rows, width, streams, most):
     down, across = quarter_of(rows, width, streams)
     r, c = rows // down, width // across
-    row = pl.ds(0, rows) if down == 1 else pl.ds(pl.multiple_of(lax.div(at, across) * r, r), r)
-    start = lax.rem(at, across) * c + piece * (c // pieces)
-    return row, pl.ds(pl.multiple_of(start, 128), c // pieces)
+    best = (1, 1)
+    for cut_r in range(1, max(r // 16, 1) + 1):
+        for cut_c in range(1, c // 128 + 1):
+            if (cut_r > 1 and r % (16 * cut_r)) or c % (128 * cut_c):
+                continue
+            small = r * c <= most * cut_r * cut_c
+            best_small = r * c <= most * best[0] * best[1]
+            fewer = (cut_r * cut_c, cut_c) < (best[0] * best[1], best[1])
+            if (small and (not best_small or fewer)) or (not best_small and not fewer):
+                best = (cut_r, cut_c)
+    return best
+
+
+def units_of(shapes, streams, most):
+    units = []
+    for w, (rows, width) in enumerate(shapes):
+        cut_r, cut_c = pieces_of(rows, width, streams, most)
+        units += [(w, i, j, cut_r, cut_c) for i in range(cut_r) for j in range(cut_c)]
+    return units
+
+
+def quarter_index(rows, width, streams, at, unit):
+    _, i, j, cut_r, cut_c = unit
+    down, across = quarter_of(rows, width, streams)
+    r, c = rows // down, width // across
+    pr, pc = r // cut_r, c // cut_c
+    if down == 1:
+        row = pl.ds(i * pr, pr)
+    else:
+        row = pl.ds(pl.multiple_of(lax.div(at, across) * r + i * pr, pr), pr)
+    start = lax.rem(at, across) * c + j * pc
+    return row, pl.ds(pl.multiple_of(start, 128), pc)
 
 
 def copy_to(source, target, send_sem, recv_sem, device):
@@ -343,28 +467,19 @@
     def __init__(self, place, shards, fulls, sems):
         self.place, self.shards, self.fulls = place, shards, fulls
         self.sems = sems
-        self.units = []
-        for w, shard in enumerate(shards):
-            rows, width = shard.shape
-            _, across = quarter_of(rows, width, place.streams)
-            pieces = 2 if (width // across) % 256 == 0 else 1
-            for piece in range(pieces):
-                self.units.append((w, piece, pieces))
+        self.units = units_of([x.shape for x in shards], place.streams, GATHER_PIECE)
 
     @staticmethod
     def sem_shapes(shapes, streams, spans):
-        units = 0
-        for rows, width in shapes:
-            _, across = quarter_of(rows, width, streams)
-            units += 2 if (width // across) % 256 == 0 else 1
+        units = len(units_of(shapes, streams, GATHER_PIECE))
         slots = spans // 2
         dma = pltpu.SemaphoreType.DMA
         return [dma((units, slots, 4, 2)), dma((len(shapes), slots, 2)), dma((len(shapes),))]
 
     def part(self, unit, at, span=None):
-        w, piece, pieces = self.units[unit]
+        w = self.units[unit][0]
         rows, width = self.shards[w].shape
-        index = quarter_index(rows, width, self.place.streams, at, piece, pieces)
+        index = quarter_index(rows, width, self.place.streams, at, self.units[unit])
         if span is None:
             return self.shards[w].at[index]
         return self.fulls[w].at[(span,) + index]
@@ -446,19 +561,18 @@
         p = self.place
         slots = range(1, p.chips)
         count = len(self.units)
-        ends = {}
-        for unit, (w, piece, pieces) in enumerate(self.units):
-            if piece == pieces - 1:
-                ends[unit] = w
+        owner = [unit[0] for unit in self.units]
+        ends = {u: w for u, w in enumerate(owner) if u + 1 == count or owner[u + 1] != w}
+        starts = {u for u, w in enumerate(owner) if u == 0 or owner[u - 1] != w}
         steps = []
 
         def begin(unit):
-            w, piece, pieces = self.units[unit]
             for k in slots:
                 self.along(unit, k).start()
-            if piece == 0:
-                self.across(w, 0).start()
-                self.own(w).start()
+
+        def hand_over(w):
+            self.across(w, 0).start()
+            self.own(w).start()
 
         def beside(unit, k):
             self.along_wait(unit, k)
@@ -470,8 +584,8 @@
             self.corner(unit, k).start()
 
         def close(w, k):
-            for unit, (owner, _, _) in enumerate(self.units):
-                if owner == w:
+            for unit in range(count):
+                if owner[unit] == w:
                     self.sideways_wait(unit, k, self.turns(unit, k)[1])
                     self.corner_wait(unit, k)
             self.across(w, k).start()
@@ -481,25 +595,28 @@
                 self.across_wait(w, k)
                 self.across(w, k).wait_send()
             self.own(w).wait()
-            for unit, (owner, _, _) in enumerate(self.units):
-                if owner == w:
+            for unit in range(count):
+                if owner[unit] == w:
                     for k in slots:
                         self.along(unit, k).wait_send()
                         self.sideways(unit, k, 1).wait_send()
                         self.sideways(unit, k, 2).wait_send()
                         self.corner(unit, k).wait_send()
 
-        for unit in range(min(2, count)):
+        ahead, lag = GATHER_AHEAD, GATHER_LAG
+        for unit in range(min(ahead, count)):
             steps.append(functools.partial(begin, unit))
-        for turn_at in range(count + 2):
-            if turn_at + 2 < count:
-                steps.append(functools.partial(begin, turn_at + 2))
-            if turn_at < count:
-                steps += [functools.partial(beside, turn_at, k) for k in slots]
-            if 0 <= turn_at - 1 < count:
-                steps += [functools.partial(turn, turn_at - 1, k) for k in slots]
-            if turn_at - 2 in ends:
-                steps += [functools.partial(close, ends[turn_at - 2], k) for k in slots]
+        for t in range(count + 2 * lag):
+            if t < count:
+                steps += [functools.partial(beside, t, k) for k in slots]
+                if t in starts:
+                    steps.append(functools.partial(hand_over, owner[t]))
+            if t + ahead < count:
+                steps.append(functools.partial(begin, t + ahead))
+            if 0 <= t - lag < count:
+                steps += [functools.partial(turn, t - lag, k) for k in slots]
+            if t - 2 * lag in ends:
+                steps += [functools.partial(close, ends[t - 2 * lag], k) for k in slots]
         steps += [functools.partial(finish, w) for w in range(len(self.shards))]
         return steps
 
@@ -518,7 +635,7 @@
     shapes = [shard.shape for shard in shards]
     outs = pl.pallas_call(
         functools.partial(gather_kernel, streams, spans, len(shards)),
-        in_specs=[pl.BlockSpec(memory_space=pl.ANY)] * len(shards),
+        in_specs=[pl.BlockSpec(memory_space=pltpu.VMEM)] * len(shards),
         out_specs=[pl.BlockSpec(memory_space=pl.ANY)] * len(shards),
         out_shape=[jax.ShapeDtypeStruct((spans,) + s.shape, s.dtype) for s in shards],
         scratch_shapes=Gather.sem_shapes(shapes, streams, spans),
@@ -531,8 +648,14 @@
 
 
 class Reduce:
-    def __init__(self, place, grads, outs, bufs, sems):
-        self.place, self.grads, self.outs, self.bufs, self.sems = place, grads, outs, bufs, sems
+    def __init__(self, place, grads, targets, bufs, sems):
+        self.place, self.grads, self.bufs, self.sems = place, grads, bufs, sems
+        self.targets = targets
+        self.units = self.cut([g.shape for g in grads], place.streams)
+
+    @staticmethod
+    def cut(shapes, streams):
+        return units_of([s[1:] for s in shapes], streams, REDUCE_PIECE // shapes[0][0])
 
     @staticmethod
     def block(shape, streams):
@@ -544,154 +667,192 @@
     def scratch(shapes, kinds, streams):
         out = []
         dma = pltpu.SemaphoreType.DMA
+        spans = shapes[0][0]
         for shape, kind in zip(shapes, kinds):
-            chips = shape[0]
             r, c = Reduce.block(shape, streams)
             out += [
-                pltpu.VMEM((2, chips, r, c), kind),
-                pltpu.VMEM((2, chips, r, c), kind),
-                pltpu.VMEM((chips, r, c), kind),
-                pltpu.VMEM((chips, r, c), kind),
-                pltpu.VMEM((chips, r, c), kind),
-                pltpu.VMEM((streams, r, c), kind),
+                pltpu.VMEM((2, spans, r, c), kind),
+                pltpu.VMEM((2, spans, r, c), kind),
+                pltpu.VMEM((spans, r, c), kind),
+                pltpu.VMEM((spans, r, c), kind),
+                pltpu.VMEM((spans, r, c), kind),
+                pltpu.VMEM((r, c), kind),
+                pltpu.VMEM((streams, 2, r, c), kind),
             ]
-        n = len(shapes)
-        chips = shapes[0][0]
-        out += [dma((n, 2, 3, 2)), dma((n, chips, 2)), dma((n, streams, 2))]
+        n = len(Reduce.cut(shapes, streams))
+        out += [dma((n, 3, 2)), dma((n, spans // 2, 2)), dma((n, streams, 2))]
         return out
 
-    def turn(self, w, half):
-        return (1, 2) if (w + half) % 2 == 0 else (2, 1)
-
-    def chips_of(self, half):
-        n = self.place.chips // 2
-        return half * n, n
-
-    def region(self, w, half, at):
-        _, rows, width = self.grads[w].shape
-        start, n = self.chips_of(half)
-        return (pl.ds(start, n),) + quarter_index(rows, width, self.place.streams, at)
-
-    def first(self, w, half, slot):
-        p = self.place
-        a, b = self.turn(w, half)
-        start, n = self.chips_of(half)
+    @staticmethod
+    def turn(unit):
+        return (1, 2) if unit % 2 == 0 else (2, 1)
+
+    def inner(self, unit):
+        w, i, j, cut_r, cut_c = self.units[unit]
+        r, c = self.block(self.grads[w].shape, self.place.streams)
+        r, c = r // cut_r, c // cut_c
+        return pl.ds(i * r, r), pl.ds(j * c, c)
+
+    def outer(self, unit, at):
+        _, rows, width = self.grads[self.units[unit][0]].shape
+        return quarter_index(rows, width, self.place.streams, at, self.units[unit])
+
+    def buf(self, unit, which):
+        return self.bufs[self.units[unit][0]][which]
+
+    def first(self, unit, slot):
+        p = self.place
+        a, b = self.turn(unit)
+        spans = pl.ds(0, p.spans)
         at = p.stream ^ a if slot == 0 else p.stream ^ a ^ b
         return copy_to(
-            self.grads[w].at[self.region(w, half, at)],
-            self.bufs[w][0].at[slot, pl.ds(start, n)],
-            self.sems[0].at[w, half, slot, 0], self.sems[0].at[w, half, slot, 1], p.beside(a),
-        )
-
-    def second(self, w, half):
-        p = self.place
-        _, b = self.turn(w, half)
-        start, n = self.chips_of(half)
+            self.grads[self.units[unit][0]].at[(spans,) + self.outer(unit, at)],
+            self.buf(unit, 0).at[(slot, spans) + self.inner(unit)],
+            self.sems[0].at[unit, slot, 0], self.sems[0].at[unit, slot, 1], p.beside(a),
+        )
+
+    def second(self, unit):
+        p = self.place
+        _, b = self.turn(unit)
+        spans = pl.ds(0, p.spans)
         return copy_to(
-            self.bufs[w][1].at[1, pl.ds(start, n)], self.bufs[w][2].at[pl.ds(start, n)],
-            self.sems[0].at[w, half, 2, 0], self.sems[0].at[w, half, 2, 1], p.beside(b),
-        )
-
-    def third(self, w, k):
+            self.buf(unit, 1).at[(1, spans) + self.inner(unit)],
+            self.buf(unit, 2).at[(spans,) + self.inner(unit)],
+            self.sems[0].at[unit, 2, 0], self.sems[0].at[unit, 2, 1], p.beside(b),
+        )
+
+    def third(self, unit, k):
         p = self.place
         return copy_to(
-            self.bufs[w][3].at[p.shifted(k)], self.bufs[w][4].at[k],
-            self.sems[1].at[w, k, 0], self.sems[1].at[w, k, 1], p.along(k),
-        )
-
-    def fourth(self, w, step):
+            self.buf(unit, 3).at[(pl.ds(2 * p.shifted(k), 2),) + self.inner(unit)],
+            self.buf(unit, 4).at[(pl.ds(2 * k, 2),) + self.inner(unit)],
+            self.sems[1].at[unit, k, 0], self.sems[1].at[unit, k, 1], p.along(k),
+        )
+
+    def swap(self, unit):
         p = self.place
         return copy_to(
-            self.bufs[w][5].at[0], self.bufs[w][5].at[step],
-            self.sems[2].at[w, step, 0], self.sems[2].at[w, step, 1], p.beside(step),
+            self.buf(unit, 5).at[self.inner(unit)],
+            self.buf(unit, 6).at[(0, p.core) + self.inner(unit)],
+            self.sems[2].at[unit, 0, 0], self.sems[2].at[unit, 0, 1], p.other(),
+        )
+
+    def fourth(self, unit, step):
+        p = self.place
+        return copy_to(
+            self.buf(unit, 6).at[(0, pl.ds(0, 2)) + self.inner(unit)],
+            self.buf(unit, 6).at[(step, pl.ds(0, 2)) + self.inner(unit)],
+            self.sems[2].at[unit, step, 0], self.sems[2].at[unit, step, 1], p.beside(step),
         )
 
     def neighbours(self):
         p = self.place
         return [p.along(k) for k in range(1, p.chips)] + [
             p.beside(s) for s in range(1, p.streams)
-        ]
-
-    def begin(self, w):
-        for half in range(2):
-            for slot in (1, 0):
-                self.first(w, half, slot).start()
-
-    def add_first(self, w, half):
-        p = self.place
-        _, b = self.turn(w, half)
-        start, n = self.chips_of(half)
+        ] + [p.other()]
+
+    def begin(self, unit):
         for slot in (1, 0):
-            self.first(w, half, slot).wait_recv()
-            at = p.stream ^ b if slot else p.stream
-            _, row, col = self.region(w, half, at)
-            for chip in range(start, start + n):
-                self.bufs[w][1][slot, chip] = (
-                    self.grads[w][chip, row, col].astype(F32)
-                    + self.bufs[w][0][slot, chip].astype(F32)
-                ).astype(self.grads[w].dtype)
+            self.first(unit, slot).start()
+
+    def add_first(self, unit):
+        p = self.place
+        _, b = self.turn(unit)
+        grad = self.grads[self.units[unit][0]]
+        inner = self.inner(unit)
+        for slot in (1, 0):
+            self.first(unit, slot).wait_recv()
+            outer = self.outer(unit, p.stream ^ b if slot else p.stream)
+            for span in range(p.spans):
+                self.buf(unit, 1)[(slot, span) + inner] = (
+                    grad[(span,) + outer].astype(F32)
+                    + self.buf(unit, 0)[(slot, span) + inner].astype(F32)
+                ).astype(grad.dtype)
             if slot:
-                self.second(w, half).start()
-
-    def add_second(self, w, half):
-        start, n = self.chips_of(half)
-        self.second(w, half).wait_recv()
-        for chip in range(start, start + n):
-            self.bufs[w][3][chip] = (
-                self.bufs[w][1][0, chip].astype(F32) + self.bufs[w][2][chip].astype(F32)
-            ).astype(self.grads[w].dtype)
-
-    def spread(self, w):
-        for k in range(1, self.place.chips):
-            self.third(w, k).start()
-
-    def add_third(self, w):
-        p = self.place
-        total = self.bufs[w][3][p.chip].astype(F32)
+                self.second(unit).start()
+
+    def add_second(self, unit):
+        p = self.place
+        inner = self.inner(unit)
+        self.second(unit).wait_recv()
+        for span in range(p.spans):
+            self.buf(unit, 3)[(span,) + inner] = (
+                self.buf(unit, 1)[(0, span) + inner].astype(F32)
+                + self.buf(unit, 2)[(span,) + inner].astype(F32)
+            ).astype(self.buf(unit, 3).dtype)
         for k in range(1, p.chips):
-            self.third(w, k).wait_recv()
-            total = total + self.bufs[w][4][k].astype(F32)
-        self.bufs[w][5][0] = total.astype(self.grads[w].dtype)
-        for step in range(1, p.streams):
-            self.fourth(w, step).start()
-
-    def finish(self, w):
-        p = self.place
-        _, rows, width = self.grads[w].shape
+            self.third(unit, k).start()
+
+    def add_third(self, unit):
+        p = self.place
+        inner = self.inner(unit)
+        kind = self.buf(unit, 5).dtype
+        for k in range(1, p.chips):
+            self.third(unit, k).wait_recv()
+        for mine in (False, True):
+            core = p.core if mine else 1 - p.core
+            total = self.buf(unit, 3)[(2 * p.chip + core,) + inner].astype(F32)
+            for k in range(1, p.chips):
+                total = total + self.buf(unit, 4)[(2 * k + core,) + inner].astype(F32)
+            if mine:
+                self.buf(unit, 6)[(0, p.core) + inner] = total.astype(kind)
+            else:
+                self.buf(unit, 5)[inner] = total.astype(kind)
+                self.swap(unit).start()
+
+    def spread(self, unit):
+        self.swap(unit).wait_recv()
+        for step in range(1, self.place.streams):
+            self.fourth(unit, step).start()
+
+    def finish(self, unit):
+        p = self.place
         for step in range(p.streams):
             if step:
-                self.fourth(w, step).wait_recv()
-            row, col = quarter_index(rows, width, p.streams, p.stream ^ step)
-            self.outs[w][row, col] = self.bufs[w][5][step]
-        for half in range(2):
-            for slot in range(2):
-                self.first(w, half, slot).wait_send()
-            self.second(w, half).wait_send()
+                self.fourth(unit, step).wait_recv()
+            row, col = self.outer(unit, p.stream ^ step)
+            for part in range(2):
+                out, start = self.targets[self.units[unit][0]][part]
+                col_at = pl.ds(pl.multiple_of(start + col.start, 128), col.size)
+                out[row, col_at] = self.buf(unit, 6)[(step, part) + self.inner(unit)]
+        self.swap(unit).wait_send()
+        for slot in range(2):
+            self.first(unit, slot).wait_send()
+        self.second(unit).wait_send()
         for k in range(1, p.chips):
-            self.third(w, k).wait_send()
+            self.third(unit, k).wait_send()
         for step in range(1, p.streams):
-            self.fourth(w, step).wait_send()
+            self.fourth(unit, step).wait_send()
 
     def steps(self):
-        count = len(self.grads)
-        steps = [functools.partial(self.begin, w) for w in range(count)]
-        for t in range(count + 3):
-            if t < count:
-                steps += [functools.partial(self.add_first, t, half) for half in range(2)]
-            if 0 <= t - 1 < count:
-                steps += [functools.partial(self.add_second, t - 1, half) for half in range(2)]
-                steps.append(functools.partial(self.spread, t - 1))
-            if 0 <= t - 2 < count:
-                steps.append(functools.partial(self.add_third, t - 2))
-            if 0 <= t - 3 < count:
-                steps.append(functools.partial(self.finish, t - 3))
+        count = len(self.units)
+        ahead = REDUCE_AHEAD
+        steps = [functools.partial(self.begin, u) for u in range(min(ahead, count))]
+        lags = (
+            (0, self.add_first), (3, self.add_second), (6, self.add_third), (7, self.spread),
+            (10, self.finish),
+        )
+        for t in range(count + 10):
+            for lag, act in lags:
+                if 0 <= t - lag < count:
+                    steps.append(functools.partial(act, t - lag))
+                if lag == 0 and t + ahead < count:
+                    steps.append(functools.partial(self.begin, t + ahead))
         return steps
 
 
-def reduce_kernel(streams, spans, count, *refs):
-    grads, outs, rest = refs[:count], refs[count : 2 * count], refs[2 * count :]
-    bufs = [rest[6 * w : 6 * w + 6] for w in range(count)]
-    work = Reduce(Place(streams, spans), grads, outs, bufs, rest[6 * count :])
+def split_columns(out, width):
+    return [(out, 0), (out, width)]
+
+
+def reduce_kernel(streams, spans, *refs):
+    grads, outs, rest = refs[:5], refs[5:8], refs[8:]
+    half = grads[0].shape[2]
+    targets = [split_columns(outs[0], half)]
+    targets += [[(outs[1], 2 * i * half), (outs[1], (2 * i + 1) * half)] for i in range(3)]
+    targets += [split_columns(outs[2], grads[4].shape[2])]
+    bufs = [rest[7 * w : 7 * w + 7] for w in range(5)]
+    work = Reduce(Place(streams, spans), grads, targets, bufs, rest[35:])
     greet(work.neighbours())
     for step in work.steps():
         step()
@@ -701,11 +862,17 @@
     streams, spans = lax.axis_size("stream"), lax.axis_size("span")
     shapes = [grad.shape for grad in grads]
     vmem = pl.BlockSpec(memory_space=pltpu.VMEM)
+    rows, width = shapes[0][1:]
+    small_rows, small_width = shapes[4][1:]
     return pl.pallas_call(
-        functools.partial(reduce_kernel, streams, spans, len(grads)),
+        functools.partial(reduce_kernel, streams, spans),
         in_specs=[vmem] * len(grads),
-        out_specs=[vmem] * len(grads),
-        out_shape=[jax.ShapeDtypeStruct(g.shape[1:], g.dtype) for g in grads],
+        out_specs=[vmem] * 3,
+        out_shape=[
+            jax.ShapeDtypeStruct((rows, 2 * width), BF16),
+            jax.ShapeDtypeStruct((rows, 6 * width), BF16),
+            jax.ShapeDtypeStruct((small_rows, 2 * small_width), F32),
+        ],
         scratch_shapes=Reduce.scratch(shapes, [g.dtype for g in grads], streams),
         compiler_params=pltpu.CompilerParams(
             collective_id=collective_id, has_side_effects=True, vmem_limit_bytes=VMEM_LIMIT
@@ -823,15 +990,15 @@
 
 
 def forward_kernel(streams, spans, heads, weights, *refs):
-    ins, refs = refs[:10], refs[10:]
+    ins, refs = refs[:11], refs[11:]
     shards, refs = refs[:weights], refs[weights:]
-    outs, refs = refs[:14], refs[14:]
+    outs, refs = refs[:15], refs[15:]
     fulls, refs = refs[:weights], refs[weights:]
     gather_sems, refs = refs[:3], refs[3:]
     map_buf, read_buf, rmap_buf, state_buf = refs[:4]
     chain_bufs = refs[4:]
-    gain_ref = ins[9]
-    (q_ref, k_ref, v_ref, inv_ref, wk_ref, pre_ref, nv_ref, np_ref,
+    gain_ref = ins[10]
+    (ext_ref, q_ref, k_ref, v_ref, inv_ref, wk_ref, pre_ref, nv_ref, np_ref,
      state_ref, p_low, p_high, p_chip, out_ref, normal_ref) = outs
     step_id = pl.program_id(0)
     place = Place(streams, spans)
@@ -846,19 +1013,21 @@
 
         @pl.when(step_id == index)
         def _():
-            for step in spread_steps(steps, heads + 2, index):
+            for step in spread_steps(steps, FORWARD_SLOTS, index):
                 step()
 
     @pl.when(step_id < heads)
     def _():
         local_kernel(
-            *ins[:9], q_ref, k_ref, v_ref, inv_ref, wk_ref, pre_ref, map_buf.at[pl.ds(step_id, 1)],
+            *ins[:10], ext_ref, q_ref, k_ref, v_ref, inv_ref, wk_ref, pre_ref, map_buf.at[pl.ds(step_id, 1)],
             read_buf.at[step_id], rmap_buf.at[step_id], nv_ref, np_ref,
         )
 
     @pl.when(step_id == heads)
     def _():
-        chain_body(place, False, map_buf, (p_low, p_high, p_chip), state_buf, chain_bufs)
+        chain_body(
+            place, False, map_buf, (p_low, p_high, p_chip), state_buf, chain_bufs,
+        )
         state_ref[...] = state_buf[...]
         size = gain_ref.shape[1]
         for h in range(heads):
@@ -866,18 +1035,20 @@
             readout = read_buf[h] + nt(rmap_buf[h], state_buf[h])
             out_ref[:, cols] = readout
             normal_ref[:, cols] = readout_body(readout, gain_ref[...])
-        for step in spread_steps(steps, heads + 2, heads + 1):
-            step()
-
-
-def forward_call(keep, ext, conv, rate, allow, gain, shards, heads, collective_id):
+        for index in range(heads + 1, 20):
+            for step in spread_steps(steps, FORWARD_SLOTS, index):
+                step()
+
+
+def forward_call(
+    keep, normed, w_qkv, conv, rate, allow, gain, shards, heads, collective_id
+):
     streams, spans = lax.axis_size("stream"), lax.axis_size("span")
     tok = rate.shape[0]
-    width = ext.shape[1] // 3
+    rows, width = normed.shape
     size = width // heads
     count = tok // STRETCH
     taps = conv.shape[0]
-    rows = ext.shape[0]
     half = heads // 2
     hbm = pl.BlockSpec(memory_space=pl.ANY)
 
@@ -901,12 +1072,14 @@
         grid=(heads + 1,),
         in_specs=[
             pl.BlockSpec(memory_space=pltpu.SMEM),
-            third(0, rows), third(1, rows), third(2, rows),
+            whole(rows, width),
+            third(0, width), third(1, width), third(2, width),
             third(0, taps), third(1, taps), third(2, taps),
             whole(tok, heads), whole(tok, taps), whole(1, size),
         ]
-        + [hbm] * len(shards),
+        + [pl.BlockSpec(memory_space=pltpu.VMEM)] * len(shards),
         out_specs=[
+            pl.BlockSpec((3, rows, size), lambda h: (0, 0, at(h))),
             token_block(), token_block(), token_block(),
             pl.BlockSpec((1, tok, STRETCH), lambda h: (at(h), 0, 0)),
             token_block(),
@@ -918,6 +1091,7 @@
         ]
         + [hbm] * len(shards),
         out_shape=[
+            jax.ShapeDtypeStruct((3, rows, width), BF16),
             token_shape, token_shape, token_shape,
             jax.ShapeDtypeStruct((heads, tok, STRETCH), BF16),
             token_shape,
@@ -941,31 +1115,65 @@
             collective_id=collective_id, has_side_effects=True, vmem_limit_bytes=VMEM_LIMIT
         ),
         name="delta_forward",
-    )(keep, ext, ext, ext, conv, conv, conv, rate, allow, gain, *shards)
-    return outs[:14], outs[14:]
+    )(keep, normed, w_qkv, w_qkv, w_qkv, conv, conv, conv, rate, allow, gain, *shards)
+    return outs[:15], outs[15:]
+
+
+def head_of(turn, heads):
+    return lax.rem(turn, 2) * (heads // 2) + lax.div(turn, 2)
 
 
 def backward_kernel(streams, spans, heads, weights, *refs):
     (keep_ref, gn_ref, read_ref, gain_ref, q_ref, k_ref, v_ref, wk_ref, inv_ref, min_ref, pre_ref,
      nv_ref, np_ref, rate_ref, allow_ref, eq_ref, ek_ref, ev_ref, cq_ref, ck_ref, cv_ref,
-     p_low, p_high, p_chip) = refs[:24]
-    refs = refs[24:]
+     p_low, p_high, p_chip, pair_ref, wq_ref, wkey_ref, wv_ref) = refs[:28]
+    refs = refs[28:]
     grads, refs = refs[:weights], refs[weights:]
-    gext_ref, gconv_ref, grate_ref, gain_grad_ref = refs[:4]
-    sums, refs = refs[4 : 4 + weights], refs[4 + weights :]
-    bufs, refs = [refs[6 * w : 6 * w + 6] for w in range(weights)], refs[6 * weights :]
+    gconv_ref, grate_ref, gain_grad_ref, gnormed_ref = refs[:4]
+    halves, sums, refs = refs[4:7], refs[7:10], refs[10:]
+    bufs, refs = [refs[7 * w : 7 * w + 7] for w in range(weights)], refs[7 * weights :]
     reduce_sems, refs = refs[:3], refs[3:]
     go_buf, adj_buf, din_buf = refs[:3]
-    row_bufs, chain_bufs = refs[3:6], refs[6:]
+    pair_buf, own_buf, got_buf, pair_sem = refs[3:7]
+    row_bufs, chain_bufs = refs[7:10], refs[10:]
     step_id = pl.program_id(0)
     place = Place(streams, spans)
-    work = Reduce(place, grads, sums, bufs, reduce_sems)
+    targets = [
+        split_columns(sums[0], grads[0].shape[2]),
+        [(sums[1], 0), (sums[2], 0)],
+    ]
+    work = Reduce(place, grads, targets, bufs, reduce_sems)
     steps = work.steps()
-    slots = 2 * heads + 2
+    slots = 3 * heads
+    size = gain_ref.shape[1]
+
+    def hand_over(turn):
+        head, slot = head_of(turn, heads), lax.div(turn, 2)
+        return copy_to(
+            own_buf.at[head], got_buf.at[slot], pair_sem.at[slot, 0], pair_sem.at[slot, 1],
+            place.other(),
+        )
+
+    def weigh(turn):
+        @pl.when(place.core == lax.rem(turn, 2))
+        def _():
+            hand_over(turn).wait_recv()
+            slot = lax.div(turn, 2)
+            both = jnp.concatenate([own_buf[head_of(turn, heads)], got_buf[slot]], 0)
+            grad = nn(pair_buf[...], both).astype(BF16)
+            lanes = pl.ds(pl.multiple_of(slot * size, size), size)
+            for i in range(3):
+                rows = halves[i].shape[1]
+                halves[i][:, :, lanes] = grad[:, i * size : (i + 1) * size].reshape(-1, rows, size)
+
+        @pl.when(place.core != lax.rem(turn, 2))
+        def _():
+            hand_over(turn).wait_send()
 
     @pl.when(step_id == 0)
     def _():
-        greet(work.neighbours() + [place.other()])
+        greet(work.neighbours())
+        pair_buf[...] = pair_ref[...].T
 
     for index in range(2 * heads + 1):
 
@@ -985,48 +1193,67 @@
     def _():
         chain_body(place, True, adj_buf, (p_low, p_high, p_chip), din_buf, chain_bufs)
 
+    @pl.when(step_id > heads + 1)
+    def _():
+        weigh(step_id - heads - 2)
+
     @pl.when(step_id > heads)
     def _():
-        head = step_id - heads - 1
+        turn = step_id - heads - 1
+        head = head_of(turn, heads)
+        own = own_buf.at[head]
         backward_body(
-            head, keep_ref, din_buf.at[pl.ds(head, 1)], min_ref, pre_ref, go_buf.at[head],
-            q_ref, k_ref, v_ref, inv_ref, wk_ref, nv_ref, np_ref, rate_ref, allow_ref,
-            eq_ref, ek_ref, ev_ref, cq_ref, ck_ref, cv_ref,
-            gext_ref, gconv_ref, grate_ref, *row_bufs,
-        )
+            head, turn == 0, keep_ref, din_buf.at[pl.ds(head, 1)], min_ref, pre_ref,
+            go_buf.at[head], q_ref, k_ref, v_ref, inv_ref, wk_ref, nv_ref, np_ref, rate_ref,
+            allow_ref, eq_ref, ek_ref, ev_ref, cq_ref, ck_ref, cv_ref,
+            own, gconv_ref, grate_ref, *row_bufs,
+        )
+
+        @pl.when(place.core != lax.rem(turn, 2))
+        def _():
+            hand_over(turn).start()
+
+        part = nt(own[...], jnp.concatenate([wq_ref[...], wkey_ref[...], wv_ref[...]], 1))
+        before = jnp.where(turn == 0, jnp.zeros_like(part), gnormed_ref[...])
+        gnormed_ref[...] = before + part
 
     @pl.when(step_id == 2 * heads)
     def _():
-        for step in spread_steps(steps, slots, slots - 1):
-            step()
+        weigh(heads - 1)
+        for index in range(2 * heads + 1, slots):
+            for step in spread_steps(steps, slots, index):
+                step()
 
 
 def backward_call(
     keep, grad_normal, readout, gain, queries, keys, values, wkeys, invs, state, prefix,
-    new_v, new_p, rate, allow, ext, conv, maps, grads, heads, collective_id,
+    new_v, new_p, rate, allow, ext, conv, maps, pair_normed, w_qkv, grads, heads, collective_id,
 ):
     streams, spans = lax.axis_size("stream"), lax.axis_size("span")
     tok, width = queries.shape
     size = width // heads
     count = tok // STRETCH
     taps = conv.shape[0]
-    rows = ext.shape[0]
+    rows = ext.shape[1]
     half = heads // 2
 
     def first(i):
         return jnp.minimum(i, heads - 1)
 
     def second(i):
-        return jnp.maximum(i - heads - 1, 0)
+        return head_of(jnp.maximum(i - heads - 1, 0), heads)
 
     def both(i):
-        return jnp.where(i < heads, i, jnp.maximum(i - heads - 1, 0))
+        return jnp.where(i < heads, i, second(i))
 
     def block(at):
         return pl.BlockSpec((tok, size), lambda h: (0, at(h)))
 
     def third(i, r):
         return pl.BlockSpec((r, size), lambda h: (0, second(h) + i * heads))
+
+    def part(i):
+        return pl.BlockSpec((1, rows, size), lambda h: (i, 0, second(h)))
 
     def whole(*shape):
         return pl.BlockSpec(shape, lambda h: (0,) * len(shape))
@@ -1045,30 +1272,40 @@
             pl.BlockSpec((1, count, 2 * size, size), lambda h: (second(h), 0, 0, 0)),
             block(second), block(second),
             whole(tok, heads), whole(tok, taps),
-            third(0, rows), third(1, rows), third(2, rows),
+            part(0), part(1), part(2),
             third(0, taps), third(1, taps), third(2, taps),
             whole(half, size, size), whole(half, size, size), whole(half, size, size),
+            vmem, third(0, width), third(1, width), third(2, width),
         ]
         + [vmem] * len(grads),
         out_specs=[
-            pl.BlockSpec((3, rows, size), lambda h: (0, 0, second(h))),
             pl.BlockSpec((3, taps, size), lambda h: (0, 0, second(h))),
             whole(tok, heads),
             pl.BlockSpec((1, 1, size), lambda h: (first(h), 0, 0)),
+            whole(rows, width),
         ]
-        + [vmem] * len(grads),
+        + [vmem] * 6,
         out_shape=[
-            jax.ShapeDtypeStruct((3, rows, width), BF16),
             jax.ShapeDtypeStruct((3, taps, width), F32),
             jax.ShapeDtypeStruct((tok, heads), F32),
             jax.ShapeDtypeStruct((heads, 1, size), F32),
+            jax.ShapeDtypeStruct((rows, width), F32),
         ]
-        + [jax.ShapeDtypeStruct(g.shape[1:], g.dtype) for g in grads],
+        + [jax.ShapeDtypeStruct((spans, width // spans, width // 2), BF16)] * 3
+        + [
+            jax.ShapeDtypeStruct((shapes[0][1], 2 * shapes[0][2]), BF16),
+            jax.ShapeDtypeStruct(shapes[1][1:], BF16),
+            jax.ShapeDtypeStruct(shapes[1][1:], BF16),
+        ],
         scratch_shapes=Reduce.scratch(shapes, [g.dtype for g in grads], streams)
         + [
             pltpu.VMEM((heads, tok, size), BF16),
             pltpu.VMEM((heads, size, size), BF16),
             pltpu.VMEM((heads, size, size), BF16),
+            pltpu.VMEM((width, 2 * rows), BF16),
+            pltpu.VMEM((heads, rows, 3 * size), BF16),
+            pltpu.VMEM((half, rows, 3 * size), BF16),
+            pltpu.SemaphoreType.DMA((half, 2)),
         ]
         + [pltpu.VMEM((tok, size), F32)] * 3
         + chain_scratch(heads, size, size, True),
@@ -1078,9 +1315,10 @@
         name="delta_backward",
     )(
         keep, grad_normal, readout, gain, queries, keys, values, wkeys, invs, state, prefix,
-        new_v, new_p, rate, allow, ext, ext, ext, conv, conv, conv, *maps, *grads,
-    )
-    return outs[:4], outs[4:]
+        new_v, new_p, rate, allow, ext, ext, ext, conv, conv, conv, *maps, pair_normed,
+        w_qkv, w_qkv, w_qkv, *grads,
+    )
+    return outs[:4], outs[4:7], outs[7:]
 
 
 def local(
@@ -1141,64 +1379,40 @@
     inv_ext = lax.rsqrt(jnp.mean(inputs_ext * inputs_ext, -1, keepdims=True) + EPSILON)
     normed_ext = (inputs_ext * inv_ext * attn_gain).astype(BF16)
     inputs_f, inv_first, normed = inputs_ext[HALO:], inv_ext[HALO:], normed_ext[HALO:]
-    projected = jnp.dot(normed_ext, full_qkv, preferred_element_type=F32).astype(BF16)
     strength = jax.nn.sigmoid(
         jnp.dot(normed, full_beta, preferred_element_type=F32) + beta_bias
     )
     (
-        queries, keys, values, invs, wkeys, prefix, new_v, new_p,
+        projected, queries, keys, values, invs, wkeys, prefix, new_v, new_p,
         state_in, p_low, p_high, p_chip, readout, normal_heads,
     ), rest = forward_call(
-        stretch_keep, projected, full_conv, strength, allow, head_gain,
+        stretch_keep, normed_ext, full_qkv, full_conv, strength, allow, head_gain,
         [w_out, w_gate, w_up, w_down], heads, 2,
     )
     full_out, full_gate, full_up, full_down = (w.reshape(-1, w.shape[2]) for w in rest)
 
-    middle = inputs_f + jnp.dot(normal_heads, full_out, preferred_element_type=F32)
-    inv_second = lax.rsqrt(jnp.mean(middle * middle, -1, keepdims=True) + EPSILON)
-    normed_ffn = (middle * inv_second * ffn_gain).astype(BF16)
-    gate = jnp.dot(normed_ffn, full_gate, preferred_element_type=F32)
-    up_part = jnp.dot(normed_ffn, full_up, preferred_element_type=F32)
-    gate_sig = jax.nn.sigmoid(gate)
-    gate_act = gate * gate_sig
-    hidden = (gate_act * up_part).astype(BF16)
-    grad_branch = cotangent[0]
-    pair_cot = pair_tokens(grad_branch)
-    half_down = weight_grad(pair_columns(hidden, span_count), pair_cot, span_count)
-    grad_hidden = product("td,fd->tf", grad_branch, full_down)
-    grad_gate_in = (grad_hidden * up_part * silu_slope(gate, gate_sig)).astype(BF16)
-    grad_up_in = (grad_hidden * gate_act).astype(BF16)
-    grad_nffn = product("tf,df->td", grad_gate_in, full_gate) + product(
-        "tf,df->td", grad_up_in, full_up
-    )
-    pair_ffn = pair_columns(normed_ffn, span_count)
-    half_gate = weight_grad(pair_ffn, pair_tokens(grad_gate_in), span_count)
-    half_up = weight_grad(pair_ffn, pair_tokens(grad_up_in), span_count)
-    result = middle + jnp.dot(hidden, full_down, preferred_element_type=F32)
-
-    grad_norm_ffn = jnp.sum(grad_nffn * middle * inv_second, 0)
-    grad_middle = grad_branch.astype(F32) + norm_back(grad_nffn, middle, inv_second, ffn_gain)
-    grad_attn_in = grad_middle.astype(BF16)
-    grad_normal = product("td,kd->tk", grad_attn_in, full_out)
-    pair_heads = pair_columns(normal_heads, span_count)
-    half_out = weight_grad(pair_heads, pair_tokens(grad_attn_in), span_count)
-    (grad_ext, grad_conv, grad_strength, head_grads), ffn_parts = backward_call(
+    (
+        normed_ffn, hidden, gate_mine, gate_theirs, result, grad_middle, grad_attn_in, grad_normal,
+        grad_norm_ffn,
+    ) = feed_call(
+        jnp.reshape(place % 2, (1,)).astype(jnp.int32), normal_heads, tokens[0], cotangent[0],
+        full_out, ffn_gain[None], full_gate, full_up, full_down,
+    )
+    half_down = weight_grad(pair_tokens(hidden), pair_half(cotangent[0]), span_count)
+    half_ffn = weight_grad(
+        pair_tokens(normed_ffn), jnp.concatenate([gate_mine, swap_core(gate_theirs)], 0), span_count
+    )
+    half_out = weight_grad(pair_tokens(normal_heads), pair_half(grad_attn_in), span_count)
+    (
+        (grad_conv, grad_strength, head_grads, grad_normed_ext), (half_q, half_k, half_v), ffn_parts
+    ) = backward_call(
         stretch_keep, grad_normal, readout, head_gain, queries, keys, values, wkeys, invs,
         state_in, prefix, new_v, new_p, strength, allow, projected, full_conv,
-        (p_low, p_high, p_chip), [half_down, half_gate, half_up], heads, 4,
-    )
-    pair_normed = pair_columns(normed_ext, span_count)
-    half_q, half_k, half_v = (
-        weight_grad(pair_normed, pair_tokens(grad_ext[i]), span_count) for i in range(3)
-    )
-
+        (p_low, p_high, p_chip), pair_tokens(normed_ext), full_qkv, [half_down, half_ffn], heads, 4,
+    )
     grad_logit = grad_strength * strength * (1.0 - strength)
     grad_logit_low = grad_logit.astype(BF16)
     grad_w_beta = product("td,th->dh", normed, grad_logit_low)
-    grad_normed_ext = sum(
-        product("te,de->td", grad_ext[i], full_qkv[:, i * model_width : (i + 1) * model_width])
-        for i in range(3)
-    )
     halo_back = lax.ppermute(
         grad_normed_ext[:HALO].astype(BF16), "span", [(i, i - 1) for i in range(1, span_count)]
     )
@@ -1225,17 +1439,16 @@
         ],
         1,
     )
-    packed = jnp.pad(packed, ((0, 0), (0, 16 * 512 - packed.shape[1])))
-    packed = packed.reshape(span_count // 2, 2, 16, 512)
+    packed = jnp.pad(packed, ((0, 0), (0, 16 * 1024 - packed.shape[1])))
+    packed = packed.reshape(span_count, 16, 2, 512)
     core = place % 2
-    half_small = lax.dynamic_index_in_dim(packed, core, 1, keepdims=False) + swap_core(
-        lax.dynamic_index_in_dim(packed, 1 - core, 1, keepdims=False)
+    half_small = lax.dynamic_index_in_dim(packed, core, 2, keepdims=False) + swap_core(
+        lax.dynamic_index_in_dim(packed, 1 - core, 2, keepdims=False)
     )
     parts = reduce_call([half_out, half_q, half_k, half_v, half_small], 5)
     part_down, part_gate, part_up = (x.astype(F32) for x in ffn_parts)
-    part_out = parts[0].astype(F32)
-    part_qkv = jnp.concatenate([x.astype(F32) for x in parts[1:4]], 1)
-    part_small = parts[4].reshape(-1)
+    part_out, part_qkv = parts[0].astype(F32), parts[1].astype(F32)
+    part_small = parts[2].reshape(-1)
     sums = []
     at = 0
     for like in (conv_weight, w_beta, norm_attn, norm_ffn, norm_head, beta_bias):
@@ -1243,7 +1456,7 @@
         at += like.size
 
     return (
-        result.astype(BF16)[None],
+        result[None],
         grad_tokens[None],
         part_qkv,
         sums[0],

time: 500 us -> 408 us (0.82); the launches traced: 492 us -> 407 us
  matrix products: 69.1 us -> 15.9 us
  local copies, waits for them, and re-layouts: 40.4 us -> 22.8 us
  Pallas kernels: 353 us -> 345 us
  other arithmetic: 19.4 us -> 13.3 us
    dot_general x16 -> x5, matrix products: 53.7 us -> 14.9 us  [product(): jnp.einsum(pattern, first, second, preferred_element_type=F32).astype(kind)]
    dot_general x5 -> x0, matrix products: 14.5 us -> none  [the longest x1 5.93 us: local(): jnp.dot(normed_ext, full_qkv, preferred_element_type=F32).astype(BF16)]
    pallas_call x1, Pallas kernels: 97.6 us -> 86.2 us  [forward_call(): pl.pallas_call(functools.partial(forward_kernel, streams, spans, heads, l...]
    pallas_call x1 -> x2, Pallas kernels: 78.4 us -> 85.4 us  [the longest x1 62.4 us: reduce_call(): pl.pallas_call(functools.partial(reduce_kernel, streams, spans), in_specs...]
    unnamed x72 -> x58, local copies, waits for them, and re-layouts: 15.4 us -> 8.51 us
    pallas_call x1, Pallas kernels: 137 us -> 131 us  [backward_call(): pl.pallas_call(functools.partial(backward_kernel, streams, spans, heads,...]
  transfers between devices with their start and end apart: 14 -> 10, of which waited for: 0 -> 1; matrix products, arithmetic and copies ran while one was open for 14% -> 7% of each run, Pallas kernels for 8% -> 10%
where the time goes in v4:
time: 408 us; the launch traced here: 407 us
  Pallas kernels  345 us (85%)
  local copies, waits for them, and re-layouts  22.8 us (6%)
  matrix products  15.9 us (4%)
  other arithmetic  13.3 us (3%)
  starting transfers between devices  7.1 us (2%)
    pallas_call x1, Pallas kernels, backward_call(): pl.pallas_call(functools.partial(backward_kernel, streams, spans, heads,...  131 us
    pallas_call x1, Pallas kernels, forward_call(): pl.pallas_call(functools.partial(forward_kernel, streams, spans, heads, l...  86.2 us
    pallas_call x1, Pallas kernels, reduce_call(): pl.pallas_call(functools.partial(reduce_kernel, streams, spans), in_specs...  62.4 us
    pallas_call x1, Pallas kernels, gather_call(): pl.pallas_call(functools.partial(gather_kernel, streams, spans, len(shard...  41.9 us
    pallas_call x1, Pallas kernels, feed_call(): pl.pallas_call(feed_kernel, grid=(units // step,), in_specs=[pl.BlockSpec...  23 us
    dot_general x5, matrix products, product(): jnp.einsum(pattern, first, second, preferred_element_type=F32).astype(kind)  14.9 us
    unnamed x58, local copies, waits for them, and re-layouts  8.51 us
  transfers between devices with their start and end apart: 10, of which 1 were waited for; matrix products, arithmetic and copies ran while one was open for 7% of the time, Pallas kernels for 10%

profile of v4, /device:TPU:0, one launch (start us, length us, event | category | flops | bytes accessed | tf_op | source)
XLA Modules:
  0.0 407.0 jit_solution(391858058214195559)
XLA Ops:
  0.7 0.8 slice_bitcast_fusion
  1.5 2.3 collective-permute-start
  3.8 0.8 copy.45
  4.8 0.7 reshape.271
  5.6 0.2 dynamic-update-slice.1
  5.8 0.8 dynamic-update-slice.2
  6.7 0.8 dynamic-update-slice.3
  7.5 0.8 dynamic-update-slice.4
  8.3 0.6 reshape.273.refs_1_
  9.0 41.9 %gather_weights.1 = (bf16[8,128,3072]{2,1,0:T(8,128)(2,1)}, bf16[8,16,512]{2,1,0:T(8,128)(2,1)}) custom-call(bf16[128,3072]{1,0:T(8,128)(2,1)} %refs_0_.1, bf16[16,512]{1,0:T(8,128)(2,1)} %reshape.273.refs_1_), custom_call_target="tpu_custom_call" | custom-call | tf_op jit(solution)/shard_map/gather_weights/pallas_call | solution.py:636
  50.9 1.0 copy.56
  51.9 0.6 slice_convert_fusion.1
  52.5 0.8 reduce-window_clone.1
  53.3 0.7 subtract_bitcast_fusion
  54.2 0.5 broadcast_subtract_fusion.refs_0_
  54.9 0.3 reshape_reshape.3
  55.3 0.8 copy.47.refs_9_.refs_14_
  56.0 0.6 copy.57
  56.7 0.6 reshape.296.refs_10_.refs_3_
  57.3 0.2 multiply_reduce_fusion
  57.5 0.2 multiply_convert_fusion.refs_1_
  57.7 1.0 fusion.9.refs_8_.refs_13_
  58.7 86.2 %delta_forward.1 = (bf16[3,272,1024]{2,1,0:T(8,128)(2,1)}, bf16[256,1024]{1,0:T(8,128)(2,1)}, bf16[256,1024]{1,0:T(8,128)(2,1)}, bf16[256,1024]{1,0:T(8,128)(2,1...) custom-call(f32[4]{0:T(128)} %broadcast_subtract_fusion.refs_0_, ...), custom_call_target="tpu_custom_call" | custom-call | tf_op jit(solution)/shard_map/delta_forward/pallas_call | solution.py:1070
  144.9 23.0 %feed_forward.1 = (bf16[256,1024]{1,0:T(8,128)(2,1)}, bf16[256,2816]{1,0:T(8,128)(2,1)}, bf16[256,2816]{1,0:T(8,128)(2,1)}, bf16[256,2816]{1,0:T(8,128)(2,1)}, b...) custom-call(s32[1]{0:T(128)} %bitcast.core_ref, ...), custom_call_target="tpu_custom_call" | custom-call | flops 10000000000 | bytes 30000000 | tf_op jit(solution)/shard_map/feed_forward/pallas_call | solution.py:320
  167.8 0.4 collective-permute-start.5
  168.4 1.8 constant_dynamic-slice_fusion.3
  170.2 0.4 collective-permute-start.8
  170.7 0.4 collective-permute-start.1
  171.1 0.7 dynamic-slice_bitcast_fusion.1
  171.8 2.1 collective-permute-done.8
  173.9 0.7 copy-done.20
  174.6 0.4 collective-permute-start.4
  175.2 0.2 collective-permute-start.3
  175.4 0.5 copy-done.21
  176.0 2.9 convolution_convert_fusion.2
  178.9 1.1 pad_maximum_fusion.refs_24_
  180.1 0.7 copy-done.23
  180.9 6.4 %convolution_convert_fusion = bf16[1024,2816]{1,0:T(8,128)(2,1)} fusion(bf16[256,2816]{1,0:T(8,128)(2,1)} %collective-permute-done.5, bf16[256,2816]{1,0:T(8,128)(2,1)S(1)} %copy-done.23, bf16[256,1024]{1,0:T(8,128)(2,1)S(1)} %collective-permute-done.4, bf16[256,1024]{1,0:T(8,128)(2,1)S(1)} %copy-done.19), kind=kOutput, calls=%fused_computation | convolution fusion | flops 2963537920 | bytes 9699328 | tf_op jit(solution)/shard_map/td,te->de/dot_general | solution.py:357
  187.3 4.7 %convolution_convert_fusion.1 = bf16[2816,512]{1,0:T(8,128)(2,1)} fusion(bf16[256,2816]{1,0:T(8,128)(2,1)} %collective-permute-done.2, bf16[256,2816]{1,0:T(8,128)(2,1)S(1)} %copy-done.18, bf16[256,512]{1,0:T(8,128)(2,1)S(1)} %collective-permute-done.3, bf16[256,512]{1,0:T(8,128)(2,1)S(1)} %get-tuple-element.145), kind=kOutput, calls=%fused_computation.1 | convolution fusion | flops 1484652544 | bytes 6291456 | tf_op jit(solution)/shard_map/td,te->de/dot_general | solution.py:357
  192.0 131.3 %delta_backward.1 = (f32[3,4,1024]{2,1,0:T(4,128)}, f32[256,8]{1,0:T(8,128)}, f32[8,1,128]{2,1,0:T(1,128)}, f32[272,1024]{1,0:T(8,128)}, bf16[8,128,512]{2,1,0:T...) custom-call(f32[4]{0:T(128)} %broadcast_subtract_fusion.refs_0_, ...), custom_call_target="tpu_custom_call" | custom-call | tf_op jit(solution)/shard_map/delta_backward/pallas_call | solution.py:1263
  323.4 1.0 fusion.25
  324.4 1.5 slice.106
  325.8 1.5 collective-permute-start.6
  327.4 0.3 fusion.22
  327.7 0.3 reshape.288
  328.2 1.2 convert_element_type.91
  329.4 1.2 convert_element_type.92
  330.8 1.3 convert_element_type.93
  332.1 0.5 multiply_reduce_fusion.1
  332.9 0.4 reshape.292
  333.3 0.6 constant_dynamic-slice_fusion.1
  333.9 1.2 collective-permute-start.9
  335.1 1.3 add_bitcast_fusion
  336.4 0.7 bitcast_add_fusion.refs_4_
  337.1 62.4 %reduce_grads.1 = (bf16[128,1024]{1,0:T(8,128)(2,1)}, bf16[128,3072]{1,0:T(8,128)(2,1)}, f32[16,1024]{1,0:T(8,128)}) custom-call(bf16[8,128,512]{2,1,0:T(8,128)(2,1)} %bitcast.72, bf16[8,128,512]{2,1,0:T(8,128)(2,1)} %get-tuple-element.87.refs_1_, bf16[8,128,512]{2,1,0:T(8,128)(2,1)} %get-tuple-element.88.refs_2_, ...), custom_call_target="tpu_custom_call" | custom-call | tf_op jit(solution)/shard_map/reduce_grads/pallas_call | solution.py:867
  399.6 1.5 slice.71
  401.1 0.9 copy.58
  402.0 0.5 fusion.35
  402.5 0.6 slice.87
  403.1 0.5 slice.89
  403.6 1.3 convert_element_type.89
  404.9 0.7 copy.51
  405.6 0.8 convert_element_type.90
  406.4 0.6 reshape.294
  (85 shorter events, 2.0 us)
Async XLA Ops:
  0.6 56.6 %copy-start.2 = (bf16[1,256,1024]{2,1,0:T(8,128)(2,1)S(1)}, bf16[1,256,1024]{2,1,0:T(8,128)(2,1)}, u32[]{:S(2)}) copy-start(bf16[1,256,1024]{2,1,0:T(8,128)(2,1)} %param.14) | copy-start | bytes 1572868
  1.5 55.8 %collective-permute-start = (bf16[16,1024]{1,0:T(8,128)(2,1)S(1)}, bf16[16,1024]{1,0:T(8,128)(2,1)S(1)}, u32[]{:S(2)}, u32[]{:S(2)}) collective-permute-start(bf16[16,1024]{1,0:T(8,128)(2,1)S(1)} %slice_bitcast_fusion), channel_id=1, source_target_pairs={{0,1},{1,2},{2,3},{3,4},{4,5},{5,6},{6,7},{8,9},{9,10},{10,11},{11... | collective-permute-start | bytes 98312 | tf_op jit(solution)/shard_map/ppermute | solution.py:1375
  50.9 6.8 %copy-start.22 = (f32[8]{0:T(128)S(1)}, f32[8]{0:T(128)}, u32[]{:S(2)}) copy-start(f32[8]{0:T(128)} %param.20) | copy-start | bytes 100
  57.7 1.0 copy-start
  144.8 25.9 %copy-start.1 = (bf16[272,1024]{1,0:T(8,128)(2,1)S(1)}, bf16[272,1024]{1,0:T(8,128)(2,1)}, u32[]{:S(2)}) copy-start(bf16[272,1024]{1,0:T(8,128)(2,1)} %copy-done) | copy-start | bytes 1671172
  144.9 26.2 %copy-start.11 = (bf16[1,256,1024]{2,1,0:T(8,128)(2,1)S(1)}, bf16[1,256,1024]{2,1,0:T(8,128)(2,1)}, u32[]{:S(2)}) copy-start(bf16[1,256,1024]{2,1,0:T(8,128)(2,1)} %param.15) | copy-start | bytes 1572868
  167.8 7.2 %copy-start.3 = (bf16[1,256,1024]{2,1,0:T(8,128)(2,1)S(1)}, bf16[1,256,1024]{2,1,0:T(8,128)(2,1)}, u32[]{:S(2)}) copy-start(bf16[1,256,1024]{2,1,0:T(8,128)(2,1)} %param.14) | copy-start | bytes 1572868
  167.8 12.2 %collective-permute-start.5 = (bf16[256,2816]{1,0:T(8,128)(2,1)}, bf16[256,2816]{1,0:T(8,128)(2,1)}, u32[]{:S(2)}, u32[]{:S(2)}) collective-permute-start(bf16[256,2816]{1,0:T(8,128)(2,1)} %get-tuple-element.83), channel_id=1, source_target_pairs={{0,1},{1,0},{2,3},{3,2},{4,5},{5,4},{6,7},{7,6},{8,9},{9,8},{10,11... | collective-permute-start | bytes 4325384 | tf_op jit(solution)/shard_map/ppermute | solution.py:365
  168.3 19.0 %collective-permute-start.2 = (bf16[256,2816]{1,0:T(8,128)(2,1)}, bf16[256,2816]{1,0:T(8,128)(2,1)}, u32[]{:S(2)}, u32[]{:S(2)}) collective-permute-start(bf16[256,2816]{1,0:T(8,128)(2,1)} %get-tuple-element.80), channel_id=1, source_target_pairs={{0,1},{1,0},{2,3},{3,2},{4,5},{5,4},{6,7},{7,6},{8,9},{9,8},{10,11... | collective-permute-start | bytes 4325384 | tf_op jit(solution)/shard_map/ppermute | solution.py:365
  170.2 3.7 collective-permute-start.8
  170.6 4.7 %collective-permute-start.7 = (bf16[256,1024]{1,0:T(8,128)(2,1)}, bf16[256,1024]{1,0:T(8,128)(2,1)}, u32[]{:S(2)}, u32[]{:S(2)}) collective-permute-start(bf16[256,1024]{1,0:T(8,128)(2,1)} %get-tuple-element.58.heads_ref), channel_id=1, source_target_pairs={{0,1},{1,0},{2,3},{3,2},{4,5},{5,4},{6,7},{7,6},{8,9},{9,8},{10,11... | collective-permute-start | bytes 1572872 | tf_op jit(solution)/shard_map/ppermute | solution.py:365
  170.7 8.2 %collective-permute-start.1 = (bf16[272,1024]{1,0:T(8,128)(2,1)S(1)}, bf16[272,1024]{1,0:T(8,128)(2,1)S(1)}, u32[]{:S(2)}, u32[]{:S(2)}) collective-permute-start(bf16[272,1024]{1,0:T(8,128)(2,1)S(1)} %copy-done.1), channel_id=1, source_target_pairs={{0,1},{1,0},{2,3},{3,2},{4,5},{5,4},{6,7},{7,6},{8,9},{9,8},{10,11... | collective-permute-start | bytes 1671176 | tf_op jit(solution)/shard_map/ppermute | solution.py:365
  171.8 3.4 copy-start.12
  171.8 3.6 copy-start.13
  173.9 0.7 copy-start.20
  174.6 5.3 %collective-permute-start.4 = (bf16[256,1024]{1,0:T(8,128)(2,1)}, bf16[256,1024]{1,0:T(8,128)(2,1)S(1)}, u32[]{:S(2)}, u32[]{:S(2)}) collective-permute-start(bf16[256,1024]{1,0:T(8,128)(2,1)} %get-tuple-element.81), channel_id=1, source_target_pairs={{0,1},{1,0},{2,3},{3,2},{4,5},{5,4},{6,7},{7,6},{8,9},{9,8},{10,11... | collective-permute-start | bytes 1572872 | tf_op jit(solution)/shard_map/ppermute | solution.py:365
  175.0 1.0 copy-start.21
  175.2 12.1 %collective-permute-start.3 = (bf16[256,512]{1,0:T(8,128)(2,1)S(1)}, bf16[256,512]{1,0:T(8,128)(2,1)S(1)}, u32[]{:S(2)}, u32[]{:S(2)}) collective-permute-start(bf16[256,512]{1,0:T(8,128)(2,1)S(1)} %copy-done.12), channel_id=1, source_target_pairs={{0,1},{1,0},{2,3},{3,2},{4,5},{5,4},{6,7},{7,6},{8,9},{9,8},{10,11... | collective-permute-start | bytes 786440 | tf_op jit(solution)/shard_map/ppermute | solution.py:365
  178.9 1.2 copy-start.19
  178.9 1.9 copy-start.23
  180.8 6.4 %copy-start.18 = (bf16[256,2816]{1,0:T(8,128)(2,1)S(1)}, bf16[256,2816]{1,0:T(8,128)(2,1)}, u32[]{:S(2)}) copy-start(bf16[256,2816]{1,0:T(8,128)(2,1)} %get-tuple-element.80) | copy-start | bytes 4325380
  192.0 131.4 %copy-start.4 = (f32[256,8]{1,0:T(8,128)S(1)}, f32[256,8]{1,0:T(8,128)}, u32[]{:S(2)}) copy-start(f32[256,8]{1,0:T(8,128)} %fusion.9.refs_8_.refs_13_) | copy-start | bytes 24580
  323.3 4.7 %copy-start.15 = (f32[3,4,1024]{2,1,0:T(4,128)S(1)}, f32[3,4,1024]{2,1,0:T(4,128)}, u32[]{:S(2)}) copy-start(f32[3,4,1024]{2,1,0:T(4,128)} %get-tuple-element.90) | copy-start | bytes 147460
  323.3 4.8 %copy-start.17 = (f32[8,1,128]{2,1,0:T(1,128)S(1)}, f32[8,1,128]{2,1,0:T(1,128)}, u32[]{:S(2)}) copy-start(f32[8,1,128]{2,1,0:T(1,128)} %get-tuple-element.92) | copy-start | bytes 12292
  323.3 4.9 %copy-start.10 = (bf16[128,2816]{1,0:T(8,128)(2,1)S(1)}, bf16[128,2816]{1,0:T(8,128)(2,1)}, u32[]{:S(2)}) copy-start(bf16[128,2816]{1,0:T(8,128)(2,1)} %get-tuple-element.96) | copy-start | bytes 2162692
  325.8 6.2 %collective-permute-start.6 = (bf16[16,1024]{1,0:T(8,128)(2,1)}, bf16[16,1024]{1,0:T(8,128)(2,1)S(1)}, u32[]{:S(2)}, u32[]{:S(2)}) collective-permute-start(bf16[16,1024]{1,0:T(8,128)(2,1)} %slice.106), channel_id=1, source_target_pairs={{1,0},{2,1},{3,2},{4,3},{5,4},{6,5},{7,6},{9,8},{10,9},{11,10},{12... | collective-permute-start | bytes 98312 | tf_op jit(solution)/shard_map/ppermute | solution.py:1416
  327.7 1.7 copy-start.9
  329.4 1.4 copy-start.8
  330.6 1.4 copy-start.5
  332.1 0.7 copy-start.16
  333.3 1.8 copy-start.6
  333.9 2.5 collective-permute-start.9
  399.6 4.0 copy-start.7
  401.1 4.5 %copy-start.14 = (bf16[128,1024]{1,0:T(8,128)(2,1)S(1)}, bf16[128,1024]{1,0:T(8,128)(2,1)}, u32[]{:S(2)}) copy-start(bf16[128,1024]{1,0:T(8,128)(2,1)} %get-tuple-element.95) | copy-start | bytes 786436

commit v5 on v4

--- a/solution.py
+++ b/solution.py
@@ -9,6 +9,7 @@
 
 STRETCH = 64
 HALO = 16
+GROUP = 2
 EPSILON = 1e-06
 F32 = jnp.float32
 BF16 = jnp.bfloat16
@@ -20,6 +21,7 @@
 REDUCE_PIECE = 100 * 1024
 REDUCE_AHEAD = 6
 FORWARD_SLOTS = 12
+BACKWARD_SLOTS = 11
 
 
 def nn(a, b):
@@ -69,7 +71,7 @@
 
 def mix_rows(ext, conv_ref, allow):
     ext = ext.astype(F32)
-    conv = conv_ref[...].astype(F32)
+    conv = conv_ref.astype(F32)
     shifted = [
         (ext if tap == 0 else pltpu.roll(ext, tap, 0))[HALO:] * allow[tap]
         for tap in range(conv.shape[0])
@@ -92,7 +94,7 @@
     def activation(index, weight_ref, conv_ref):
         ext = nn(normed, weight_ref[...]).astype(BF16)
         ext_ref[index] = ext
-        _, mixed, _ = mix_rows(ext, conv_ref, allow)
+        _, mixed, _ = mix_rows(ext, conv_ref[...], allow)
         return mixed * jax.nn.sigmoid(mixed)
 
     act_q = activation(0, wq_ref, cq_ref)
@@ -144,208 +146,134 @@
     end_ref[0] = running.astype(BF16)
 
 
+def lanes_of(index, size):
+    return slice(index * size, (index + 1) * size)
+
+
 def adjoint_body(
     keep_ref, gn_ref, read_ref, gain_ref, q_ref, k_ref, wk_ref, go_ref, adj_ref, gain_grad_ref
 ):
-    grad, readout = gn_ref[...], read_ref[...]
-    inv = lax.rsqrt(jnp.mean(readout * readout, -1, keepdims=True) + EPSILON)
-    scaled = grad * gain_ref[...]
-    grad_read = inv * scaled - readout * (inv * inv * inv) * jnp.mean(
-        scaled * readout, -1, keepdims=True
-    )
-    gain_grad_ref[0] = jnp.sum(grad * readout * inv, 0, keepdims=True)
-    grad_read = grad_read.astype(BF16)
-    go_ref[...] = grad_read
-    count = grad.shape[0] // STRETCH
+    size = gain_ref.shape[1]
+    tok = gn_ref.shape[0]
+    grads = []
+    for g in range(GROUP):
+        grad, readout = gn_ref[:, lanes_of(g, size)], read_ref[:, lanes_of(g, size)]
+        inv = lax.rsqrt(jnp.mean(readout * readout, -1, keepdims=True) + EPSILON)
+        scaled = grad * gain_ref[...]
+        grad_read = inv * scaled - readout * (inv * inv * inv) * jnp.mean(
+            scaled * readout, -1, keepdims=True
+        )
+        gain_grad_ref[g] = jnp.sum(grad * readout * inv, 0, keepdims=True)
+        grads.append(grad_read.astype(BF16))
+        go_ref[:, lanes_of(g, size)] = grads[g]
     rows, cols = grid_ids(STRETCH)
-    size = grad.shape[1]
-    adj = jnp.zeros((size, size), F32)
-    for n in range(count - 1, -1, -1):
+    adj = [jnp.zeros((size, size), F32)] * GROUP
+    for n in range(tok // STRETCH - 1, -1, -1):
         part = slice(n * STRETCH, (n + 1) * STRETCH)
-        key, query, out = k_ref[part, :], q_ref[part, :], grad_read[part]
-        scores = jnp.where(rows >= cols, nt(query, key), 0.0).astype(BF16)
-        new_grad = tn(scores, out) + nt(key, adj.astype(BF16))
-        adj = (
-            adj
-            + tn(
-                jnp.concatenate([out, (-new_grad).astype(BF16)], 0),
-                jnp.concatenate([query, wk_ref[part, :]], 0),
-            )
-        ) * keep_ref[n]
-    adj_ref[0] = adj.astype(BF16)
+        for g in range(GROUP):
+            lanes = lanes_of(g, size)
+            key, query, out = k_ref[part, lanes], q_ref[part, lanes], grads[g][part]
+            scores = jnp.where(rows >= cols, nt(query, key), 0.0).astype(BF16)
+            new_grad = tn(scores, out) + nt(key, adj[g].astype(BF16))
+            adj[g] = (
+                adj[g]
+                + tn(
+                    jnp.concatenate([out, (-new_grad).astype(BF16)], 0),
+                    jnp.concatenate([query, wk_ref[part, lanes]], 0),
+                )
+            ) * keep_ref[n]
+    for g in range(GROUP):
+        adj_ref[g] = adj[g].astype(BF16)
 
 
 def backward_body(
-    head, begins, keep_ref, din_ref, min_ref, pre_ref, go_ref, q_ref, k_ref, v_ref, inv_ref, wk_ref,
+    turn, keep_ref, din_ref, min_ref, pre_ref, go_ref, q_ref, k_ref, v_ref, inv_ref, wk_ref,
     nv_ref, np_ref, rate_ref, allow_ref,
     eq_ref, ek_ref, ev_ref, cq_ref, ck_ref, cv_ref,
     gext_ref, gconv_ref, grate_ref,
     gq_buf, gk_buf, gv_buf,
 ):
-    size = q_ref.shape[1]
+    size = min_ref.shape[1]
     tok = q_ref.shape[0]
     count = tok // STRETCH
     rows, cols = grid_ids(STRETCH)
-    rate = column_of(rate_ref[...], head)
-    low_in = min_ref[0]
-    adj = din_ref[0].astype(F32)
-    grate_parts = [None] * count
+    rates = [column_of(rate_ref[...], GROUP * turn + g) for g in range(GROUP)]
+    low_in = [min_ref[g] for g in range(GROUP)]
+    adj = [din_ref[g].astype(F32) for g in range(GROUP)]
+    grate_parts = [[None] * count for _ in range(GROUP)]
     for n in range(count - 1, -1, -1):
         part = slice(n * STRETCH, (n + 1) * STRETCH)
-        key, query, value, out = k_ref[part, :], q_ref[part, :], v_ref[part, :], go_ref[part, :]
-        beta = rate[part]
-        pre = pre_ref[0, n]
-        state = (nn(low_in, pre[size:]) + pre[:size].astype(F32)).astype(BF16)
-        new = (nt(np_ref[part, :], low_in) + nv_ref[part, :].astype(F32)).astype(BF16)
-        low_adj = adj.astype(BF16)
-        gram_both = nt(jnp.concatenate([key, query], 0), key)
-        gram = gram_both[:STRETCH]
-        scores = jnp.where(rows >= cols, gram_both[STRETCH:], 0.0).astype(BF16)
-        new_grad = tn(scores, out) + nt(key, low_adj)
-        low_new_grad = new_grad.astype(BF16)
-        adj = (
-            adj
-            + tn(
-                jnp.concatenate([out, -low_new_grad], 0),
-                jnp.concatenate([query, wk_ref[part, :]], 0),
+        for g in range(GROUP):
+            lanes = lanes_of(g, size)
+            key, query, value = k_ref[part, lanes], q_ref[part, lanes], v_ref[part, lanes]
+            out = go_ref[part, lanes]
+            beta = rates[g][part]
+            pre = pre_ref[g, n]
+            state = (nn(low_in[g], pre[size:]) + pre[:size].astype(F32)).astype(BF16)
+            new = (nt(np_ref[part, lanes], low_in[g]) + nv_ref[part, lanes].astype(F32)).astype(BF16)
+            low_adj = adj[g].astype(BF16)
+            gram_both = nt(jnp.concatenate([key, query], 0), key)
+            gram = gram_both[:STRETCH]
+            scores = jnp.where(rows >= cols, gram_both[STRETCH:], 0.0).astype(BF16)
+            new_grad = tn(scores, out) + nt(key, low_adj)
+            low_new_grad = new_grad.astype(BF16)
+            adj[g] = (
+                adj[g]
+                + tn(
+                    jnp.concatenate([out, -low_new_grad], 0),
+                    jnp.concatenate([query, wk_ref[part, lanes]], 0),
+                )
+            ) * keep_ref[n]
+            grad_b = tn(inv_ref[g, part, :], low_new_grad)
+            both = nt(jnp.concatenate([out, grad_b.astype(BF16)], 0), new)
+            grad_scores = jnp.where(rows >= cols, both[:STRETCH], 0.0).astype(BF16)
+            grad_low = jnp.where(rows > cols, -both[STRETCH:], 0.0)
+            left = value.astype(F32) - nt(key, state)
+            grate_parts[g][n] = jnp.sum(grad_low * gram, -1, keepdims=True) + jnp.sum(
+                grad_b * left, -1, keepdims=True
             )
-        ) * keep_ref[n]
-        grad_b = tn(inv_ref[0, part, :], low_new_grad)
-        both = nt(jnp.concatenate([out, grad_b.astype(BF16)], 0), new)
-        grad_scores = jnp.where(rows >= cols, both[:STRETCH], 0.0).astype(BF16)
-        grad_low = jnp.where(rows > cols, -both[STRETCH:], 0.0)
-        left = value.astype(F32) - nt(key, state)
-        grate_parts[n] = jnp.sum(grad_low * gram, -1, keepdims=True) + jnp.sum(
-            grad_b * left, -1, keepdims=True
-        )
-        grad_v = beta * grad_b
-        grad_gram = beta * grad_low
-        symmetric = (grad_gram + grad_gram.T).astype(BF16)
-        by_state = nn(jnp.concatenate([out, -grad_v.astype(BF16)], 0), state)
-        gq_buf[part, :] = by_state[:STRETCH] + nn(grad_scores, key)
-        gk_buf[part, :] = (
-            by_state[STRETCH:]
-            + tn(grad_scores, query)
-            + nn(jnp.concatenate([new, symmetric], 1), jnp.concatenate([low_adj, key], 0))
-        )
-        gv_buf[part, :] = grad_v
-    grate = jnp.concatenate(grate_parts, 0)
-    lanes = lax.broadcasted_iota(jnp.int32, grate_ref.shape, 1)
-    before = jnp.where(begins, jnp.zeros(grate_ref.shape, F32), grate_ref[...])
-    grate_ref[...] = jnp.where(lanes == head, grate, before)
+            grad_v = beta * grad_b
+            grad_gram = beta * grad_low
+            symmetric = (grad_gram + grad_gram.T).astype(BF16)
+            by_state = nn(jnp.concatenate([out, -grad_v.astype(BF16)], 0), state)
+            gq_buf[part, lanes] = by_state[:STRETCH] + nn(grad_scores, key)
+            gk_buf[part, lanes] = (
+                by_state[STRETCH:]
+                + tn(grad_scores, query)
+                + nn(jnp.concatenate([new, symmetric], 1), jnp.concatenate([low_adj, key], 0))
+            )
+            gv_buf[part, lanes] = grad_v
+    heads_at = lax.broadcasted_iota(jnp.int32, grate_ref.shape, 1)
+    grate = jnp.where(turn == 0, jnp.zeros(grate_ref.shape, F32), grate_ref[...])
+    for g in range(GROUP):
+        grate = jnp.where(
+            heads_at == GROUP * turn + g, jnp.concatenate(grate_parts[g], 0), grate
+        )
+    grate_ref[...] = grate
     allow_all = allow_ref[...]
     allow = [allow_all[:, tap : tap + 1] for tap in range(cq_ref.shape[0])]
     zeros = jnp.zeros((HALO, size), F32)
     for i, (ext, conv_ref, buf) in enumerate(
         ((eq_ref, cq_ref, gq_buf), (ek_ref, ck_ref, gk_buf), (ev_ref, cv_ref, gv_buf))
     ):
-        shifted, mixed, conv = mix_rows(ext[0], conv_ref, allow)
-        sig = jax.nn.sigmoid(mixed)
-        grad = buf[...]
-        if i < 2:
-            raw = mixed * sig
-            inv = lax.rsqrt(jnp.sum(raw * raw, -1, keepdims=True) + EPSILON)
-            grad = inv * grad - raw * (inv * inv * inv) * jnp.sum(grad * raw, -1, keepdims=True)
-        grad = grad * (sig * (1.0 + mixed * (1.0 - sig)))
-        total = None
-        for tap in range(conv.shape[0]):
-            gconv_ref[i, tap : tap + 1, :] = jnp.sum(grad * shifted[tap], 0, keepdims=True)
-            term = jnp.concatenate([zeros, grad * (conv[tap : tap + 1] * allow[tap])], 0)
-            if tap:
-                term = pltpu.roll(term, tok + HALO - tap, 0)
-            total = term if total is None else total + term
-        gext_ref[:, i * size : (i + 1) * size] = total.astype(BF16)
-
-
-def feed_kernel(
-    core_ref, heads_ref, tok_ref, cot_ref, out_w_ref, gain_ref, gate_ref, up_ref, down_ref,
-    nffn_ref, hidden_ref, mine_ref, theirs_ref, result_ref, gmid_ref, gattn_ref, gnormal_ref,
-    ggain_ref, mid_buf, grad_buf, res_buf,
-):
-    step_id = pl.program_id(0)
-    cot = cot_ref[...]
-
-    @pl.when(step_id == 0)
-    def _():
-        middle = tok_ref[...].astype(F32) + nn(heads_ref[...], out_w_ref[...])
-        inv = lax.rsqrt(jnp.mean(middle * middle, -1, keepdims=True) + EPSILON)
-        mid_buf[...] = middle
-        nffn_ref[...] = (middle * inv * gain_ref[...]).astype(BF16)
-        grad_buf[...] = jnp.zeros(grad_buf.shape, F32)
-        res_buf[...] = middle
-
-    normed = nffn_ref[...]
-    gate_w, up_w, down_w = gate_ref[...], up_ref[...], down_ref[...]
-    gate = nn(normed, gate_w)
-    up = nn(normed, up_w)
-    grad_hidden = nt(cot, down_w)
-    sig = jax.nn.sigmoid(gate)
-    act = gate * sig
-    hidden = (act * up).astype(BF16)
-    grad_gate = (grad_hidden * up * (sig * (1.0 + gate * (1.0 - sig)))).astype(BF16)
-    grad_up = (grad_hidden * act).astype(BF16)
-    low = core_ref[0] == 0
-    hidden_ref[...] = hidden
-    mine_ref[...] = jnp.where(low, grad_gate, grad_up)
-    theirs_ref[...] = jnp.where(low, grad_up, grad_gate)
-    grad_buf[...] += nt(grad_gate, gate_w) + nt(grad_up, up_w)
-    res_buf[...] += nn(hidden, down_w)
-
-    @pl.when(step_id == pl.num_programs(0) - 1)
-    def _():
-        result_ref[...] = res_buf[...].astype(BF16)
-        middle, grad = mid_buf[...], grad_buf[...]
-        inv = lax.rsqrt(jnp.mean(middle * middle, -1, keepdims=True) + EPSILON)
-        ggain_ref[...] = jnp.sum(grad * middle * inv, 0, keepdims=True)
-        scaled = grad * gain_ref[...]
-        total = cot.astype(F32) + inv * scaled - middle * (inv * inv * inv) * jnp.mean(
-            scaled * middle, -1, keepdims=True
-        )
-        gmid_ref[...] = total
-        low_total = total.astype(BF16)
-        gattn_ref[...] = low_total
-        gnormal_ref[...] = nt(low_total, out_w_ref[...])
-
-
-def feed_call(core, normal_heads, tokens, cotangent, w_out, gain, w_gate, w_up, w_down):
-    tok, width = tokens.shape
-    units = w_gate.shape[1]
-    step = 256
-
-    def whole(*shape):
-        return pl.BlockSpec(shape, lambda f: (0,) * len(shape))
-
-    wide = pl.BlockSpec((tok, step), lambda f: (0, f))
-    rows = whole(tok, width)
-    return pl.pallas_call(
-        feed_kernel,
-        grid=(units // step,),
-        in_specs=[
-            pl.BlockSpec(memory_space=pltpu.SMEM),
-            rows, rows, rows, whole(width, width), whole(1, width),
-            pl.BlockSpec((width, step), lambda f: (0, f)),
-            pl.BlockSpec((width, step), lambda f: (0, f)),
-            pl.BlockSpec((step, width), lambda f: (f, 0)),
-        ],
-        out_specs=[rows, wide, wide, wide, rows, rows, rows, rows, whole(1, width)],
-        out_shape=[
-            jax.ShapeDtypeStruct((tok, width), BF16),
-            jax.ShapeDtypeStruct((tok, units), BF16),
-            jax.ShapeDtypeStruct((tok, units), BF16),
-            jax.ShapeDtypeStruct((tok, units), BF16),
-            jax.ShapeDtypeStruct((tok, width), BF16),
-            jax.ShapeDtypeStruct((tok, width), F32),
-            jax.ShapeDtypeStruct((tok, width), BF16),
-            jax.ShapeDtypeStruct((tok, width), F32),
-            jax.ShapeDtypeStruct((1, width), F32),
-        ],
-        scratch_shapes=[pltpu.VMEM((tok, width), F32)] * 3,
-        compiler_params=pltpu.CompilerParams(vmem_limit_bytes=VMEM_LIMIT),
-        cost_estimate=pl.CostEstimate(
-            flops=10**10, bytes_accessed=3 * 10**7, transcendentals=10**6
-        ),
-        name="feed_forward",
-    )(core, normal_heads, tokens, cotangent, w_out, gain, w_gate, w_up, w_down)
+        for g in range(GROUP):
+            lanes = lanes_of(g, size)
+            shifted, mixed, conv = mix_rows(ext[0, :, lanes], conv_ref[:, lanes], allow)
+            sig = jax.nn.sigmoid(mixed)
+            grad = buf[:, lanes]
+            if i < 2:
+                raw = mixed * sig
+                inv = lax.rsqrt(jnp.sum(raw * raw, -1, keepdims=True) + EPSILON)
+                grad = inv * grad - raw * (inv * inv * inv) * jnp.sum(grad * raw, -1, keepdims=True)
+            grad = grad * (sig * (1.0 + mixed * (1.0 - sig)))
+            total = None
+            for tap in range(conv.shape[0]):
+                gconv_ref[i, tap : tap + 1, lanes] = jnp.sum(grad * shifted[tap], 0, keepdims=True)
+                term = jnp.concatenate([zeros, grad * (conv[tap : tap + 1] * allow[tap])], 0)
+                if tap:
+                    term = pltpu.roll(term, tok + HALO - tap, 0)
+                total = term if total is None else total + term
+            gext_ref[g, :, lanes_of(i, size)] = total.astype(BF16)
 
 
 def norm_back(grad_in, values, inv_rms, gain_vec):
@@ -648,14 +576,39 @@
 
 
 class Reduce:
-    def __init__(self, place, grads, targets, bufs, sems):
+    def __init__(self, place, grads, targets, bufs, sems, share):
         self.place, self.grads, self.bufs, self.sems = place, grads, bufs, sems
         self.targets = targets
         self.units = self.cut([g.shape for g in grads], place.streams)
+        self.modes = self.plan(self.units, [g.shape for g in grads], place.streams, share)
 
     @staticmethod
     def cut(shapes, streams):
-        return units_of([s[1:] for s in shapes], streams, REDUCE_PIECE // shapes[0][0])
+        units = units_of([s[1:] for s in shapes], streams, REDUCE_PIECE // shapes[0][0])
+        sizes = [sum(u[0] == w for u in units) for w in range(len(shapes))]
+        order = []
+        for w, size in enumerate(sizes):
+            own = [u for u in units if u[0] == w]
+            order += [((n + 0.5) / size, w, u) for n, u in enumerate(own)]
+        return [u for _, _, u in sorted(order)]
+
+    @staticmethod
+    def plan(units, shapes, streams, share):
+        whole = part = 0
+        modes = []
+        loads = [[0, 0], [0, 0]]
+        for w, _, _, cut_r, cut_c in units:
+            _, rows, width = shapes[w]
+            size = rows * width // (cut_r * cut_c)
+            plain = quarter_of(rows, width, streams)[0] == 1 and cut_c == 1 and rows > 16
+            whole += size
+            first = plain and part + size <= share * whole
+            part += size if first else 0
+            load = loads[first]
+            way = load.index(min(load))
+            load[way] += size
+            modes.append((first, (1, 2) if way == 0 else (2, 1)))
+        return modes
 
     @staticmethod
     def block(shape, streams):
@@ -679,13 +632,20 @@
                 pltpu.VMEM((r, c), kind),
                 pltpu.VMEM((streams, 2, r, c), kind),
             ]
+            across = quarter_of(*shape[1:], streams)[1]
+            out += [
+                pltpu.VMEM((spans, r, c * across) if across == streams else (2, 16, 128), kind),
+                pltpu.VMEM((2, r, c * across) if across == streams else (2, 16, 128), kind),
+            ]
         n = len(Reduce.cut(shapes, streams))
         out += [dma((n, 3, 2)), dma((n, spans // 2, 2)), dma((n, streams, 2))]
         return out
 
-    @staticmethod
-    def turn(unit):
-        return (1, 2) if unit % 2 == 0 else (2, 1)
+    def turn(self, unit):
+        return self.modes[unit][1]
+
+    def chips_first(self, unit):
+        return self.modes[unit][0]
 
     def inner(self, unit):
         w, i, j, cut_r, cut_c = self.units[unit]
@@ -700,13 +660,17 @@
     def buf(self, unit, which):
         return self.bufs[self.units[unit][0]][which]
 
+    def count(self, unit):
+        return 2 if self.chips_first(unit) else self.place.spans
+
     def first(self, unit, slot):
         p = self.place
         a, b = self.turn(unit)
-        spans = pl.ds(0, p.spans)
+        spans = pl.ds(0, self.count(unit))
         at = p.stream ^ a if slot == 0 else p.stream ^ a ^ b
+        source = self.buf(unit, 8) if self.chips_first(unit) else self.grads[self.units[unit][0]]
         return copy_to(
-            self.grads[self.units[unit][0]].at[(spans,) + self.outer(unit, at)],
+            source.at[(spans,) + self.outer(unit, at)],
             self.buf(unit, 0).at[(slot, spans) + self.inner(unit)],
             self.sems[0].at[unit, slot, 0], self.sems[0].at[unit, slot, 1], p.beside(a),
         )
@@ -714,7 +678,7 @@
     def second(self, unit):
         p = self.place
         _, b = self.turn(unit)
-        spans = pl.ds(0, p.spans)
+        spans = pl.ds(0, self.count(unit))
         return copy_to(
             self.buf(unit, 1).at[(1, spans) + self.inner(unit)],
             self.buf(unit, 2).at[(spans,) + self.inner(unit)],
@@ -723,6 +687,13 @@
 
     def third(self, unit, k):
         p = self.place
+        if self.chips_first(unit):
+            rows, _ = self.inner(unit)
+            return copy_to(
+                self.grads[self.units[unit][0]].at[pl.ds(2 * p.shifted(k), 2), rows],
+                self.buf(unit, 7).at[pl.ds(2 * k, 2), rows],
+                self.sems[1].at[unit, k, 0], self.sems[1].at[unit, k, 1], p.along(k),
+            )
         return copy_to(
             self.buf(unit, 3).at[(pl.ds(2 * p.shifted(k), 2),) + self.inner(unit)],
             self.buf(unit, 4).at[(pl.ds(2 * k, 2),) + self.inner(unit)],
@@ -752,18 +723,41 @@
         ] + [p.other()]
 
     def begin(self, unit):
+        if self.chips_first(unit):
+            for k in range(1, self.place.chips):
+                self.third(unit, k).start()
+            return
         for slot in (1, 0):
             self.first(unit, slot).start()
 
     def add_first(self, unit):
+        if self.chips_first(unit):
+            self.sum_chips(unit)
+            for slot in (1, 0):
+                self.first(unit, slot).start()
+            return
+        self.sum_first(unit, self.grads[self.units[unit][0]])
+
+    def sum_chips(self, unit):
+        p = self.place
+        grad = self.grads[self.units[unit][0]]
+        rows, _ = self.inner(unit)
+        for k in range(1, p.chips):
+            self.third(unit, k).wait_recv()
+        for part in range(2):
+            total = grad[2 * p.chip + part, rows, :].astype(F32)
+            for k in range(1, p.chips):
+                total = total + self.buf(unit, 7)[2 * k + part, rows, :].astype(F32)
+            self.buf(unit, 8)[part, rows, :] = total.astype(grad.dtype)
+
+    def sum_first(self, unit, grad):
         p = self.place
         _, b = self.turn(unit)
-        grad = self.grads[self.units[unit][0]]
         inner = self.inner(unit)
         for slot in (1, 0):
             self.first(unit, slot).wait_recv()
             outer = self.outer(unit, p.stream ^ b if slot else p.stream)
-            for span in range(p.spans):
+            for span in range(self.count(unit)):
                 self.buf(unit, 1)[(slot, span) + inner] = (
                     grad[(span,) + outer].astype(F32)
                     + self.buf(unit, 0)[(slot, span) + inner].astype(F32)
@@ -773,6 +767,9 @@
 
     def add_second(self, unit):
         p = self.place
+        if self.chips_first(unit):
+            self.sum_first(unit, self.buf(unit, 8))
+            return
         inner = self.inner(unit)
         self.second(unit).wait_recv()
         for span in range(p.spans):
@@ -787,13 +784,20 @@
         p = self.place
         inner = self.inner(unit)
         kind = self.buf(unit, 5).dtype
-        for k in range(1, p.chips):
-            self.third(unit, k).wait_recv()
+        if self.chips_first(unit):
+            self.second(unit).wait_recv()
+        else:
+            for k in range(1, p.chips):
+                self.third(unit, k).wait_recv()
         for mine in (False, True):
             core = p.core if mine else 1 - p.core
-            total = self.buf(unit, 3)[(2 * p.chip + core,) + inner].astype(F32)
-            for k in range(1, p.chips):
-                total = total + self.buf(unit, 4)[(2 * k + core,) + inner].astype(F32)
+            if self.chips_first(unit):
+                total = self.buf(unit, 1)[(0, core) + inner].astype(F32)
+                total = total + self.buf(unit, 2)[(core,) + inner].astype(F32)
+            else:
+                total = self.buf(unit, 3)[(2 * p.chip + core,) + inner].astype(F32)
+                for k in range(1, p.chips):
+                    total = total + self.buf(unit, 4)[(2 * k + core,) + inner].astype(F32)
             if mine:
                 self.buf(unit, 6)[(0, p.core) + inner] = total.astype(kind)
             else:
@@ -812,8 +816,8 @@
                 self.fourth(unit, step).wait_recv()
             row, col = self.outer(unit, p.stream ^ step)
             for part in range(2):
-                out, start = self.targets[self.units[unit][0]][part]
-                col_at = pl.ds(pl.multiple_of(start + col.start, 128), col.size)
+                out, start, stride = self.targets[self.units[unit][0]][part]
+                col_at = pl.ds(pl.multiple_of(start + stride * col.start, 128), col.size)
                 out[row, col_at] = self.buf(unit, 6)[(step, part) + self.inner(unit)]
         self.swap(unit).wait_send()
         for slot in range(2):
@@ -842,17 +846,19 @@
 
 
 def split_columns(out, width):
-    return [(out, 0), (out, width)]
+    return [(out, 0, 1), (out, width, 1)]
 
 
 def reduce_kernel(streams, spans, *refs):
     grads, outs, rest = refs[:5], refs[5:8], refs[8:]
     half = grads[0].shape[2]
     targets = [split_columns(outs[0], half)]
-    targets += [[(outs[1], 2 * i * half), (outs[1], (2 * i + 1) * half)] for i in range(3)]
+    targets += [
+        [(outs[1], 2 * i * half, 2), (outs[1], 2 * i * half + 128, 2)] for i in range(3)
+    ]
     targets += [split_columns(outs[2], grads[4].shape[2])]
-    bufs = [rest[7 * w : 7 * w + 7] for w in range(5)]
-    work = Reduce(Place(streams, spans), grads, targets, bufs, rest[35:])
+    bufs = [rest[9 * w : 9 * w + 9] for w in range(5)]
+    work = Reduce(Place(streams, spans), grads, targets, bufs, rest[45:], 0.3)
     greet(work.neighbours())
     for step in work.steps():
         step()
@@ -984,9 +990,12 @@
     return (readout * inv * gain).astype(BF16)
 
 
-def spread_steps(steps, slots, index):
-    count = len(steps)
-    return steps[count * index // slots : count * (index + 1) // slots]
+def spread_steps(steps, first, slots, index):
+    if index == 0:
+        return steps[:first]
+    rest = steps[first:]
+    count = len(rest)
+    return rest[count * (index - 1) // slots : count * index // slots]
 
 
 def forward_kernel(streams, spans, heads, weights, *refs):
@@ -1013,7 +1022,7 @@
 
         @pl.when(step_id == index)
         def _():
-            for step in spread_steps(steps, FORWARD_SLOTS, index):
+            for step in spread_steps(steps, GATHER_AHEAD, FORWARD_SLOTS, index):
                 step()
 
     @pl.when(step_id < heads)
@@ -1036,7 +1045,7 @@
             out_ref[:, cols] = readout
             normal_ref[:, cols] = readout_body(readout, gain_ref[...])
         for index in range(heads + 1, 20):
-            for step in spread_steps(steps, FORWARD_SLOTS, index):
+            for step in spread_steps(steps, GATHER_AHEAD, FORWARD_SLOTS, index):
                 step()
 
 
@@ -1119,10 +1128,6 @@
     return outs[:15], outs[15:]
 
 
-def head_of(turn, heads):
-    return lax.rem(turn, 2) * (heads // 2) + lax.div(turn, 2)
-
-
 def backward_kernel(streams, spans, heads, weights, *refs):
     (keep_ref, gn_ref, read_ref, gain_ref, q_ref, k_ref, v_ref, wk_ref, inv_ref, min_ref, pre_ref,
      nv_ref, np_ref, rate_ref, allow_ref, eq_ref, ek_ref, ev_ref, cq_ref, ck_ref, cv_ref,
@@ -1131,97 +1136,91 @@
     grads, refs = refs[:weights], refs[weights:]
     gconv_ref, grate_ref, gain_grad_ref, gnormed_ref = refs[:4]
     halves, sums, refs = refs[4:7], refs[7:10], refs[10:]
-    bufs, refs = [refs[7 * w : 7 * w + 7] for w in range(weights)], refs[7 * weights :]
+    bufs, refs = [refs[9 * w : 9 * w + 9] for w in range(weights)], refs[9 * weights :]
     reduce_sems, refs = refs[:3], refs[3:]
     go_buf, adj_buf, din_buf = refs[:3]
     pair_buf, own_buf, got_buf, pair_sem = refs[3:7]
     row_bufs, chain_bufs = refs[7:10], refs[10:]
     step_id = pl.program_id(0)
+    turns = heads // GROUP
     place = Place(streams, spans)
     targets = [
         split_columns(sums[0], grads[0].shape[2]),
-        [(sums[1], 0), (sums[2], 0)],
+        [(sums[1], 0, 1), (sums[2], 0, 1)],
     ]
-    work = Reduce(place, grads, targets, bufs, reduce_sems)
+    work = Reduce(place, grads, targets, bufs, reduce_sems, 0.2)
     steps = work.steps()
-    slots = 3 * heads
+    slots = BACKWARD_SLOTS
     size = gain_ref.shape[1]
 
     def hand_over(turn):
-        head, slot = head_of(turn, heads), lax.div(turn, 2)
         return copy_to(
-            own_buf.at[head], got_buf.at[slot], pair_sem.at[slot, 0], pair_sem.at[slot, 1],
-            place.other(),
+            own_buf.at[GROUP * turn + 1 - place.core], got_buf.at[turn],
+            pair_sem.at[turn, 0], pair_sem.at[turn, 1], place.other(),
         )
 
     def weigh(turn):
-        @pl.when(place.core == lax.rem(turn, 2))
-        def _():
-            hand_over(turn).wait_recv()
-            slot = lax.div(turn, 2)
-            both = jnp.concatenate([own_buf[head_of(turn, heads)], got_buf[slot]], 0)
-            grad = nn(pair_buf[...], both).astype(BF16)
-            lanes = pl.ds(pl.multiple_of(slot * size, size), size)
-            for i in range(3):
-                rows = halves[i].shape[1]
-                halves[i][:, :, lanes] = grad[:, i * size : (i + 1) * size].reshape(-1, rows, size)
-
-        @pl.when(place.core != lax.rem(turn, 2))
-        def _():
-            hand_over(turn).wait_send()
+        hand_over(turn).wait_recv()
+        both = jnp.concatenate([own_buf[GROUP * turn + place.core], got_buf[turn]], 0)
+        grad = nn(pair_buf[...], both).astype(BF16)
+        lanes = pl.ds(pl.multiple_of(turn * size, size), size)
+        for i in range(3):
+            rows = halves[i].shape[1]
+            halves[i][:, :, lanes] = grad[:, lanes_of(i, size)].reshape(-1, rows, size)
+        hand_over(turn).wait_send()
 
     @pl.when(step_id == 0)
     def _():
         greet(work.neighbours())
         pair_buf[...] = pair_ref[...].T
 
-    for index in range(2 * heads + 1):
+    for index in range(2 * turns + 1):
 
         @pl.when(step_id == index)
         def _():
-            for step in spread_steps(steps, slots, index):
+            for step in spread_steps(steps, REDUCE_AHEAD, slots, index):
                 step()
 
-    @pl.when(step_id < heads)
+    @pl.when(step_id < turns)
     def _():
         adjoint_body(
             keep_ref, gn_ref, read_ref, gain_ref, q_ref, k_ref, wk_ref,
-            go_buf.at[step_id], adj_buf.at[pl.ds(step_id, 1)], gain_grad_ref,
-        )
-
-    @pl.when(step_id == heads)
+            go_buf.at[step_id], adj_buf.at[pl.ds(GROUP * step_id, GROUP)], gain_grad_ref,
+        )
+
+    @pl.when(step_id == turns)
     def _():
         chain_body(place, True, adj_buf, (p_low, p_high, p_chip), din_buf, chain_bufs)
 
-    @pl.when(step_id > heads + 1)
+    @pl.when(step_id > turns + 1)
     def _():
-        weigh(step_id - heads - 2)
-
-    @pl.when(step_id > heads)
+        weigh(step_id - turns - 2)
+
+    @pl.when(step_id > turns)
     def _():
-        turn = step_id - heads - 1
-        head = head_of(turn, heads)
-        own = own_buf.at[head]
+        turn = step_id - turns - 1
+        pair = pl.ds(GROUP * turn, GROUP)
+        own = own_buf.at[pair]
         backward_body(
-            head, turn == 0, keep_ref, din_buf.at[pl.ds(head, 1)], min_ref, pre_ref,
-            go_buf.at[head], q_ref, k_ref, v_ref, inv_ref, wk_ref, nv_ref, np_ref, rate_ref,
-            allow_ref, eq_ref, ek_ref, ev_ref, cq_ref, ck_ref, cv_ref,
+            turn, keep_ref, din_buf.at[pair], min_ref, pre_ref, go_buf.at[turn],
+            q_ref, k_ref, v_ref, inv_ref, wk_ref, nv_ref, np_ref, rate_ref, allow_ref,
+            eq_ref, ek_ref, ev_ref, cq_ref, ck_ref, cv_ref,
             own, gconv_ref, grate_ref, *row_bufs,
         )
-
-        @pl.when(place.core != lax.rem(turn, 2))
-        def _():
-            hand_over(turn).start()
-
-        part = nt(own[...], jnp.concatenate([wq_ref[...], wkey_ref[...], wv_ref[...]], 1))
+        hand_over(turn).start()
+        part = None
+        for i, weight in enumerate((wq_ref, wkey_ref, wv_ref)):
+            grad = jnp.concatenate([own[g, :, lanes_of(i, size)] for g in range(GROUP)], 1)
+            term = nt(grad, weight[...])
+            part = term if part is None else part + term
         before = jnp.where(turn == 0, jnp.zeros_like(part), gnormed_ref[...])
         gnormed_ref[...] = before + part
 
-    @pl.when(step_id == 2 * heads)
+    @pl.when(step_id == 2 * turns)
     def _():
-        weigh(heads - 1)
-        for index in range(2 * heads + 1, slots):
-            for step in spread_steps(steps, slots, index):
+        weigh(turns - 1)
+        for index in range(2 * turns + 1, slots + 1):
+            for step in spread_steps(steps, REDUCE_AHEAD, slots, index):
                 step()
 
 
@@ -1237,23 +1236,26 @@
     rows = ext.shape[1]
     half = heads // 2
 
+    turns = heads // GROUP
+    wide = GROUP * size
+
     def first(i):
-        return jnp.minimum(i, heads - 1)
+        return jnp.minimum(i, turns - 1)
 
     def second(i):
-        return head_of(jnp.maximum(i - heads - 1, 0), heads)
+        return jnp.maximum(i - turns - 1, 0)
 
     def both(i):
-        return jnp.where(i < heads, i, second(i))
+        return jnp.where(i < turns, i, second(i))
 
     def block(at):
-        return pl.BlockSpec((tok, size), lambda h: (0, at(h)))
+        return pl.BlockSpec((tok, wide), lambda h: (0, at(h)))
 
     def third(i, r):
-        return pl.BlockSpec((r, size), lambda h: (0, second(h) + i * heads))
+        return pl.BlockSpec((r, wide), lambda h: (0, second(h) + i * turns))
 
     def part(i):
-        return pl.BlockSpec((1, rows, size), lambda h: (i, 0, second(h)))
+        return pl.BlockSpec((1, rows, wide), lambda h: (i, 0, second(h)))
 
     def whole(*shape):
         return pl.BlockSpec(shape, lambda h: (0,) * len(shape))
@@ -1262,14 +1264,14 @@
     shapes = [g.shape for g in grads]
     outs = pl.pallas_call(
         functools.partial(backward_kernel, streams, spans, heads, len(grads)),
-        grid=(2 * heads + 1,),
+        grid=(2 * turns + 1,),
         in_specs=[
             pl.BlockSpec(memory_space=pltpu.SMEM),
             block(first), block(first), whole(1, size),
             block(both), block(both), block(second), block(both),
-            pl.BlockSpec((1, tok, STRETCH), lambda h: (second(h), 0, 0)),
-            pl.BlockSpec((1, size, size), lambda h: (second(h), 0, 0)),
-            pl.BlockSpec((1, count, 2 * size, size), lambda h: (second(h), 0, 0, 0)),
+            pl.BlockSpec((GROUP, tok, STRETCH), lambda h: (second(h), 0, 0)),
+            pl.BlockSpec((GROUP, size, size), lambda h: (second(h), 0, 0)),
+            pl.BlockSpec((GROUP, count, 2 * size, size), lambda h: (second(h), 0, 0, 0)),
             block(second), block(second),
             whole(tok, heads), whole(tok, taps),
             part(0), part(1), part(2),
@@ -1279,9 +1281,9 @@
         ]
         + [vmem] * len(grads),
         out_specs=[
-            pl.BlockSpec((3, taps, size), lambda h: (0, 0, second(h))),
+            pl.BlockSpec((3, taps, wide), lambda h: (0, 0, second(h))),
             whole(tok, heads),
-            pl.BlockSpec((1, 1, size), lambda h: (first(h), 0, 0)),
+            pl.BlockSpec((GROUP, 1, size), lambda h: (first(h), 0, 0)),
             whole(rows, width),
         ]
         + [vmem] * 6,
@@ -1299,15 +1301,15 @@
         ],
         scratch_shapes=Reduce.scratch(shapes, [g.dtype for g in grads], streams)
         + [
-            pltpu.VMEM((heads, tok, size), BF16),
+            pltpu.VMEM((turns, tok, wide), BF16),
             pltpu.VMEM((heads, size, size), BF16),
             pltpu.VMEM((heads, size, size), BF16),
             pltpu.VMEM((width, 2 * rows), BF16),
             pltpu.VMEM((heads, rows, 3 * size), BF16),
-            pltpu.VMEM((half, rows, 3 * size), BF16),
-            pltpu.SemaphoreType.DMA((half, 2)),
+            pltpu.VMEM((turns, rows, 3 * size), BF16),
+            pltpu.SemaphoreType.DMA((turns, 2)),
         ]
-        + [pltpu.VMEM((tok, size), F32)] * 3
+        + [pltpu.VMEM((tok, wide), F32)] * 3
         + chain_scratch(heads, size, size, True),
         compiler_params=pltpu.CompilerParams(
             collective_id=collective_id, has_side_effects=True, vmem_limit_bytes=VMEM_LIMIT
@@ -1319,6 +1321,167 @@
         w_qkv, w_qkv, w_qkv, *grads,
     )
     return outs[:4], outs[4:7], outs[7:]
+
+
+def feed_kernel(
+    streams, spans,
+    heads_ref, tok_ref, cot_ref, out_w_ref, gain_ref, gate_ref, up_ref, down_ref,
+    result_ref, gmid_ref, gattn_ref, gnormal_ref, ggain_ref, ffn_grad_ref, down_grad_ref,
+    mid_buf, grad_buf, res_buf, normed_buf, turned_buf, cot_buf, hid_buf, mine_buf, give_buf,
+    hid_got, mine_got, row_sem, unit_sem,
+):
+    step_id = pl.program_id(0)
+    last = pl.num_programs(0) - 1
+    place = Place(streams, spans)
+    width = cot_ref.shape[1]
+    half = width // 2
+    tok = cot_ref.shape[0]
+
+    def exchange(source, target, sems):
+        return copy_to(source, target, sems.at[0], sems.at[1], place.other())
+
+    def rows(which):
+        buf = normed_buf if which == 0 else cot_buf
+        return exchange(buf.at[0 if which == 0 else 2], buf.at[1], row_sem.at[which])
+
+    def units(step, which):
+        source, target = (hid_buf, hid_got) if which == 0 else (give_buf, mine_got)
+        return exchange(source.at[step], target.at[step], unit_sem.at[step, which])
+
+    @pl.when(step_id == 0)
+    def _():
+        greet([place.other()])
+        for own in range(2):
+            which = place.core if own else 1 - place.core
+            lanes = pl.ds(pl.multiple_of(which * half, half), half)
+            cot_buf[0 if own else 2] = cot_ref[:, lanes]
+        rows(1).start()
+        middle = tok_ref[...].astype(F32) + nn(heads_ref[...], out_w_ref[...])
+        inv = lax.rsqrt(jnp.mean(middle * middle, -1, keepdims=True) + EPSILON)
+        mid_buf[...] = middle
+        normed_buf[0] = (middle * inv * gain_ref[...]).astype(BF16)
+        rows(0).start()
+        grad_buf[...] = jnp.zeros(grad_buf.shape, F32)
+        res_buf[...] = middle
+
+    @pl.when(step_id == 1)
+    def _():
+        rows(0).wait_recv()
+        rows(1).wait_recv()
+        turned_buf[:, :tok] = normed_buf[0].T
+        turned_buf[:, tok:] = normed_buf[1].T
+
+    @pl.when(step_id < last)
+    def _():
+        normed = normed_buf[0]
+        gate_w, up_w, down_w = gate_ref[...], up_ref[...], down_ref[...]
+        gate = nn(normed, gate_w)
+        up = nn(normed, up_w)
+        grad_hidden = nt(cot_ref[...], down_w)
+        sig = jax.nn.sigmoid(gate)
+        act = gate * sig
+        hidden = (act * up).astype(BF16)
+        grad_gate = (grad_hidden * up * (sig * (1.0 + gate * (1.0 - sig)))).astype(BF16)
+        grad_up = (grad_hidden * act).astype(BF16)
+        low = place.core == 0
+        hid_buf[step_id] = hidden
+        mine_buf[step_id] = jnp.where(low, grad_gate, grad_up)
+        give_buf[step_id] = jnp.where(low, grad_up, grad_gate)
+        units(step_id, 0).start()
+        units(step_id, 1).start()
+        grad_buf[...] += nt(grad_gate, gate_w) + nt(grad_up, up_w)
+        res_buf[...] += nn(hidden, down_w)
+
+    @pl.when(step_id == last)
+    def _():
+        result_ref[...] = res_buf[...].astype(BF16)
+        middle, grad = mid_buf[...], grad_buf[...]
+        inv = lax.rsqrt(jnp.mean(middle * middle, -1, keepdims=True) + EPSILON)
+        ggain_ref[...] = jnp.sum(grad * middle * inv, 0, keepdims=True)
+        scaled = grad * gain_ref[...]
+        total = cot_ref[...].astype(F32) + inv * scaled - middle * (inv * inv * inv) * jnp.mean(
+            scaled * middle, -1, keepdims=True
+        )
+        gmid_ref[...] = total
+        low_total = total.astype(BF16)
+        gattn_ref[...] = low_total
+        gnormal_ref[...] = nt(low_total, out_w_ref[...])
+
+    @pl.when(step_id > 0)
+    def _():
+        before = step_id - 1
+        units(before, 0).wait_recv()
+        units(before, 1).wait_recv()
+        mine = jnp.concatenate([mine_buf[before], mine_got[before]], 0)
+        grad = nn(turned_buf[...], mine).astype(BF16)
+        ffn_grad_ref[...] = grad.reshape(ffn_grad_ref.shape)
+        both = jnp.concatenate([hid_buf[before], hid_got[before]], 0)
+        cot = jnp.concatenate([cot_buf[0], cot_buf[1]], 0)
+        down_grad_ref[...] = tn(both, cot).astype(BF16)
+
+    @pl.when(step_id == last)
+    def _():
+        for which in range(2):
+            rows(which).wait_send()
+            for step in range(hid_buf.shape[0]):
+                units(step, which).wait_send()
+
+
+def feed_call(normal_heads, tokens, cotangent, w_out, gain, w_gate, w_up, w_down, collective_id):
+    streams, spans = lax.axis_size("stream"), lax.axis_size("span")
+    tok, width = tokens.shape
+    units = w_gate.shape[1]
+    step = 256
+    count = units // step
+    dma = pltpu.SemaphoreType.DMA
+
+    def now(f):
+        return jnp.minimum(f, count - 1)
+
+    def before(f):
+        return jnp.maximum(f - 1, 0)
+
+    def whole(*shape):
+        return pl.BlockSpec(shape, lambda f: (0,) * len(shape))
+
+    rows = whole(tok, width)
+    square = pltpu.VMEM((count, tok, step), BF16)
+    return pl.pallas_call(
+        functools.partial(feed_kernel, streams, spans),
+        grid=(count + 1,),
+        in_specs=[
+            rows, rows, rows, whole(width, width), whole(1, width),
+            pl.BlockSpec((width, step), lambda f: (0, now(f))),
+            pl.BlockSpec((width, step), lambda f: (0, now(f))),
+            pl.BlockSpec((step, width), lambda f: (now(f), 0)),
+        ],
+        out_specs=[
+            rows, rows, rows, rows, whole(1, width),
+            pl.BlockSpec((spans, width // spans, step), lambda f: (0, 0, before(f))),
+            pl.BlockSpec((step, width // 2), lambda f: (before(f), 0)),
+        ],
+        out_shape=[
+            jax.ShapeDtypeStruct((tok, width), BF16),
+            jax.ShapeDtypeStruct((tok, width), F32),
+            jax.ShapeDtypeStruct((tok, width), BF16),
+            jax.ShapeDtypeStruct((tok, width), F32),
+            jax.ShapeDtypeStruct((1, width), F32),
+            jax.ShapeDtypeStruct((spans, width // spans, units), BF16),
+            jax.ShapeDtypeStruct((units, width // 2), BF16),
+        ],
+        scratch_shapes=[pltpu.VMEM((tok, width), F32)] * 3
+        + [
+            pltpu.VMEM((2, tok, width), BF16),
+            pltpu.VMEM((width, 2 * tok), BF16),
+            pltpu.VMEM((3, tok, width // 2), BF16),
+            square, square, square, square, square,
+            dma((2, 2)), dma((count, 2, 2)),
+        ],
+        compiler_params=pltpu.CompilerParams(
+            collective_id=collective_id, has_side_effects=True, vmem_limit_bytes=VMEM_LIMIT
+        ),
+        name="feed_forward",
+    )(normal_heads, tokens, cotangent, w_out, gain, w_gate, w_up, w_down)
 
 
 def local(
@@ -1392,16 +1555,12 @@
     full_out, full_gate, full_up, full_down = (w.reshape(-1, w.shape[2]) for w in rest)
 
     (
-        normed_ffn, hidden, gate_mine, gate_theirs, result, grad_middle, grad_attn_in, grad_normal,
-        grad_norm_ffn,
+        result, grad_middle, grad_attn_in, grad_normal, grad_norm_ffn, half_ffn, half_down
     ) = feed_call(
-        jnp.reshape(place % 2, (1,)).astype(jnp.int32), normal_heads, tokens[0], cotangent[0],
-        full_out, ffn_gain[None], full_gate, full_up, full_down,
-    )
-    half_down = weight_grad(pair_tokens(hidden), pair_half(cotangent[0]), span_count)
-    half_ffn = weight_grad(
-        pair_tokens(normed_ffn), jnp.concatenate([gate_mine, swap_core(gate_theirs)], 0), span_count
-    )
+        normal_heads, tokens[0], cotangent[0], full_out, ffn_gain[None], full_gate, full_up,
+        full_down, 3,
+    )
+    half_down = half_down.reshape(span_count, -1, half_down.shape[1])
     half_out = weight_grad(pair_tokens(normal_heads), pair_half(grad_attn_in), span_count)
     (
         (grad_conv, grad_strength, head_grads, grad_normed_ext), (half_q, half_k, half_v), ffn_parts

time: 408 us -> 394 us (0.966)
  matrix products: 15.9 us -> 3.53 us
  Pallas kernels: 345 us -> 352 us
  local copies, waits for them, and re-layouts: 22.8 us -> 18.6 us
    dot_general x5 -> x3, matrix products: 14.9 us -> 2.57 us  [product(): jnp.einsum(pattern, first, second, preferred_element_type=F32).astype(kind)]
    pallas_call x1, Pallas kernels: 23 us -> 31 us  [feed_call(): pl.pallas_call(functools.partial(feed_kernel, streams, spans), grid=(coun...]
    pallas_call x1, Pallas kernels: 62.4 us -> 56.6 us  [reduce_call(): pl.pallas_call(functools.partial(reduce_kernel, streams, spans), in_specs...]
    unnamed x58 -> x51, local copies, waits for them, and re-layouts: 8.51 us -> 6.32 us
  transfers between devices with their start and end apart: 10 -> 6, of which waited for: 1 -> 1; matrix products, arithmetic and copies ran while one was open for 7% -> 5% of each run, Pallas kernels for 10% -> 19%
where the time goes in v5:
time: 394 us
  Pallas kernels  352 us (89%)
  local copies, waits for them, and re-layouts  18.6 us (5%)
  other arithmetic  12 us (3%)
  starting transfers between devices  5.73 us (1%)
    pallas_call x1, Pallas kernels, backward_call(): pl.pallas_call(functools.partial(backward_kernel, streams, spans, heads,...  134 us
    pallas_call x1, Pallas kernels, forward_call(): pl.pallas_call(functools.partial(forward_kernel, streams, spans, heads, l...  88.7 us
    pallas_call x1, Pallas kernels, reduce_call(): pl.pallas_call(functools.partial(reduce_kernel, streams, spans), in_specs...  56.6 us
    pallas_call x1, Pallas kernels, gather_call(): pl.pallas_call(functools.partial(gather_kernel, streams, spans, len(shard...  41.9 us
    pallas_call x1, Pallas kernels, feed_call(): pl.pallas_call(functools.partial(feed_kernel, streams, spans), grid=(coun...  31 us
  transfers between devices with their start and end apart: 6, of which 1 were waited for; matrix products, arithmetic and copies ran while one was open for 5% of the time, Pallas kernels for 19%

profile of v5, /device:TPU:0, one launch (start us, length us, event | category | flops | bytes accessed | tf_op | source)
XLA Modules:
  0.0 393.8 jit_solution(6243500060172254951)
XLA Ops:
  0.7 0.8 slice_bitcast_fusion
  1.5 2.3 collective-permute-start
  3.9 0.8 copy.45
  4.7 0.1 reshape.263
  4.8 0.7 reshape.262
  5.5 0.2 dynamic-update-slice
  5.6 0.2 dynamic-update-slice.1
  5.8 0.8 dynamic-update-slice.2
  6.7 0.8 dynamic-update-slice.3
  7.5 0.8 dynamic-update-slice.4
  8.3 0.6 reshape.264.refs_1_
  9.0 41.9 %gather_weights.1 = (bf16[8,128,3072]{2,1,0:T(8,128)(2,1)}, bf16[8,16,512]{2,1,0:T(8,128)(2,1)}) custom-call(bf16[128,3072]{1,0:T(8,128)(2,1)} %refs_0_.1, bf16[16,512]{1,0:T(8,128)(2,1)} %reshape.264.refs_1_), custom_call_target="tpu_custom_call" | custom-call | tf_op jit(solution)/shard_map/gather_weights/pallas_call | solution.py:564
  50.9 1.0 copy.56
  51.9 0.6 slice_convert_fusion.1
  52.5 0.2 reduce-window_clone.1
  52.7 0.2 compare_reduce_fusion
  52.9 0.5 broadcast_subtract_fusion.refs_0_
  53.5 0.1 reshape.269
  53.6 0.3 reshape_reshape.3
  54.0 0.8 copy.47.refs_9_.refs_14_
  54.8 0.6 copy.57
  55.4 0.6 reshape.286.refs_10_.refs_3_
  56.0 0.2 multiply_reduce_fusion
  56.2 0.2 multiply_convert_fusion.refs_1_
  56.4 1.0 fusion.3.refs_8_.refs_13_
  57.4 88.7 %delta_forward.1 = (bf16[3,272,1024]{2,1,0:T(8,128)(2,1)}, bf16[256,1024]{1,0:T(8,128)(2,1)}, bf16[256,1024]{1,0:T(8,128)(2,1)}, bf16[256,1024]{1,0:T(8,128)(2,1...) custom-call(f32[4]{0:T(128)} %broadcast_subtract_fusion.refs_0_, ...), custom_call_target="tpu_custom_call" | custom-call | tf_op jit(solution)/shard_map/delta_forward/pallas_call | solution.py:1079
  146.1 0.4 collective-permute-start.3
  146.5 0.1 collective-permute-start.1
  146.6 31.0 %feed_forward.1 = (bf16[256,1024]{1,0:T(8,128)(2,1)}, f32[256,1024]{1,0:T(8,128)}, bf16[256,1024]{1,0:T(8,128)(2,1)}, f32[256,1024]{1,0:T(8,128)}, f32[1,1024]{1...) custom-call(bf16[256,1024]{1,0:T(8,128)(2,1)} %get-tuple-element.56.heads_ref, ...), custom_call_target="tpu_custom_call" | custom-call | tf_op jit(solution)/shard_map/feed_forward/pallas_call | solution.py:1449
  177.6 1.2 constant_dynamic-slice_fusion.3
  178.8 0.3 collective-permute-start.4
  179.1 0.1 maximum_convert_fusion
  179.3 1.1 collective-permute-done.4
  180.4 1.7 convolution_convert_fusion
  182.1 1.1 pad_maximum_fusion.refs_24_
  183.2 133.8 %delta_backward.1 = (f32[3,4,1024]{2,1,0:T(4,128)}, f32[256,8]{1,0:T(8,128)}, f32[8,1,128]{2,1,0:T(1,128)}, f32[272,1024]{1,0:T(8,128)}, bf16[8,128,512]{2,1,0:T...) custom-call(f32[4]{0:T(128)} %broadcast_subtract_fusion.refs_0_, ...), custom_call_target="tpu_custom_call" | custom-call | tf_op jit(solution)/shard_map/delta_backward/pallas_call | solution.py:1265
  317.0 1.0 fusion.13
  318.0 0.8 slice.106
  318.9 1.3 collective-permute-start.2
  320.2 0.3 fusion.10
  320.5 0.3 reshape.278
  320.9 0.1 reshape.281
  321.0 1.2 convert_element_type.83
  322.2 1.2 convert_element_type.84
  323.4 0.2 copy-done.8
  323.6 1.3 convert_element_type.85
  324.9 0.5 multiply_reduce_fusion.1
  325.4 0.1 copy-done.16
  325.5 0.1 concatenate.23
  325.6 0.4 reshape.282
  326.1 0.5 constant_dynamic-slice_fusion.1
  326.7 1.2 collective-permute-start.5
  327.8 1.3 add_bitcast_fusion
  329.1 0.7 bitcast_add_fusion.refs_4_
  329.9 56.6 %reduce_grads.1 = (bf16[128,1024]{1,0:T(8,128)(2,1)}, bf16[128,3072]{1,0:T(8,128)(2,1)}, f32[16,1024]{1,0:T(8,128)}) custom-call(bf16[8,128,512]{2,1,0:T(8,128)(2,1)} %bitcast.69, bf16[8,128,512]{2,1,0:T(8,128)(2,1)} %get-tuple-element.83.refs_1_, bf16[8,128,512]{2,1,0:T(8,128)(2,1)} %get-tuple-element.84.refs_2_, ...), custom_call_target="tpu_custom_call" | custom-call | tf_op jit(solution)/shard_map/reduce_grads/pallas_call | solution.py:873
  386.4 1.5 slice.71
  388.0 0.5 fusion.21
  388.5 0.6 slice.87
  389.1 0.5 slice.89
  389.6 1.3 convert_element_type.81
  390.9 0.7 copy.51
  391.6 0.8 convert_element_type.82
  392.4 0.6 reshape.284
  393.0 0.8 copy.68
  (67 shorter events, 0.5 us)
Async XLA Ops:
  0.6 55.3 %copy-start = (bf16[1,256,1024]{2,1,0:T(8,128)(2,1)S(1)}, bf16[1,256,1024]{2,1,0:T(8,128)(2,1)}, u32[]{:S(2)}) copy-start(bf16[1,256,1024]{2,1,0:T(8,128)(2,1)} %param.14) | copy-start | bytes 1572868
  0.7 51.8 %copy-start.18 = (s32[1,3]{1,0:T(1,128)S(1)}, s32[1,3]{1,0:T(1,128)}, u32[]{:S(2)}) copy-start(s32[1,3]{1,0:T(1,128)} %param.16) | copy-start | bytes 40
  1.5 54.5 %collective-permute-start = (bf16[16,1024]{1,0:T(8,128)(2,1)S(1)}, bf16[16,1024]{1,0:T(8,128)(2,1)S(1)}, u32[]{:S(2)}, u32[]{:S(2)}) collective-permute-start(bf16[16,1024]{1,0:T(8,128)(2,1)S(1)} %slice_bitcast_fusion), channel_id=1, source_target_pairs={{0,1},{1,2},{2,3},{3,4},{4,5},{5,6},{6,7},{8,9},{9,10},{10,11},{11... | collective-permute-start | bytes 98312 | tf_op jit(solution)/shard_map/ppermute | solution.py:1538
  53.6 2.8 copy-start.19
  56.4 1.0 copy-start.2
  146.1 34.3 %collective-permute-start.3 = (bf16[256,1024]{1,0:T(8,128)(2,1)}, bf16[256,1024]{1,0:T(8,128)(2,1)S(1)}, u32[]{:S(2)}, u32[]{:S(2)}) collective-permute-start(bf16[256,1024]{1,0:T(8,128)(2,1)} %get-tuple-element.56.heads_ref), channel_id=1, source_target_pairs={{0,1},{1,0},{2,3},{3,2},{4,5},{5,4},{6,7},{7,6},{8,9},{9,8},{10,11... | collective-permute-start | bytes 1572872 | tf_op jit(solution)/shard_map/ppermute | solution.py:293
  146.5 35.6 %collective-permute-start.1 = (bf16[272,1024]{1,0:T(8,128)(2,1)}, bf16[272,1024]{1,0:T(8,128)(2,1)S(1)}, u32[]{:S(2)}, u32[]{:S(2)}) collective-permute-start(bf16[272,1024]{1,0:T(8,128)(2,1)} %copy-done.2), channel_id=1, source_target_pairs={{0,1},{1,0},{2,3},{3,2},{4,5},{5,4},{6,7},{7,6},{8,9},{9,8},{10,11... | collective-permute-start | bytes 1671176 | tf_op jit(solution)/shard_map/ppermute | solution.py:293
  177.6 1.5 copy-start.1
  177.6 2.8 copy-start.11
  178.8 1.6 collective-permute-start.4
  180.4 1.7 copy-start.3
  183.2 133.8 %copy-start.4 = (f32[256,8]{1,0:T(8,128)S(1)}, f32[256,8]{1,0:T(8,128)}, u32[]{:S(2)}) copy-start(f32[256,8]{1,0:T(8,128)} %fusion.3.refs_8_.refs_13_) | copy-start | bytes 24580
  317.0 3.8 copy-start.15
  317.0 3.9 copy-start.17
  317.0 4.0 %copy-start.10 = (bf16[128,2816]{1,0:T(8,128)(2,1)S(1)}, bf16[128,2816]{1,0:T(8,128)(2,1)}, u32[]{:S(2)}) copy-start(bf16[128,2816]{1,0:T(8,128)(2,1)} %get-tuple-element.92) | copy-start | bytes 2162692
  318.9 6.0 %collective-permute-start.2 = (bf16[16,1024]{1,0:T(8,128)(2,1)S(1)}, bf16[16,1024]{1,0:T(8,128)(2,1)S(1)}, u32[]{:S(2)}, u32[]{:S(2)}) collective-permute-start(bf16[16,1024]{1,0:T(8,128)(2,1)S(1)} %slice.106), channel_id=1, source_target_pairs={{1,0},{2,1},{3,2},{4,3},{5,4},{6,5},{7,6},{9,8},{10,9},{11,10},{12... | collective-permute-start | bytes 98312 | tf_op jit(solution)/shard_map/ppermute | solution.py:1575
  320.9 1.3 copy-start.9
  322.2 1.4 copy-start.8
  323.4 1.4 copy-start.5
  324.8 0.7 copy-start.16
  326.1 1.7 copy-start.6
  326.7 2.5 collective-permute-start.5
  386.4 1.5 copy-start.14
  386.4 3.2 copy-start.7
  389.6 2.0 copy-start.13
  389.6 3.4 copy-start.12

commit v6 on v5

--- a/solution.py
+++ b/solution.py
@@ -14,13 +14,13 @@
 F32 = jnp.float32
 BF16 = jnp.bfloat16
 AXES = ("stream", "span")
-VMEM_LIMIT = 56 * 2**20
+VMEM_LIMIT = 60 * 2**20
 GATHER_PIECE = 24 * 1024
-GATHER_AHEAD = 4
+GATHER_AHEAD = 3
 GATHER_LAG = 2
 REDUCE_PIECE = 100 * 1024
 REDUCE_AHEAD = 6
-FORWARD_SLOTS = 12
+FORWARD_SLOTS = 11
 BACKWARD_SLOTS = 11
 
 
@@ -333,6 +333,12 @@
     def other(self):
         return (self.stream, 2 * self.chip + 1 - self.core)
 
+    def span_at(self, step):
+        return (self.stream, lax.rem(self.span + step + self.spans, self.spans))
+
+    def either_side(self):
+        return [self.span_at(1), self.span_at(-1)]
+
 
 def greet(places):
     barrier = pltpu.get_barrier_semaphore()
@@ -550,29 +556,37 @@
 
 
 def gather_kernel(streams, spans, count, *refs):
-    shards, fulls, sems = refs[:count], refs[count : 2 * count], refs[2 * count :]
+    shards, tok_ref, fulls = refs[:count], refs[count], refs[count + 1 : 2 * count + 1]
+    halo_ref, sems, halo_sem = refs[2 * count + 1], refs[2 * count + 2 : -1], refs[-1]
     place = Place(streams, spans)
     work = Gather(place, shards, fulls, sems)
-    greet(work.neighbours())
+    greet(work.neighbours() + place.either_side())
+    halo = copy_to(
+        tok_ref.at[pl.ds(tok_ref.shape[0] - HALO, HALO)], halo_ref, halo_sem.at[0], halo_sem.at[1],
+        place.span_at(1),
+    )
+    halo.start()
     for step in work.steps():
         step()
-
-
-def gather_call(shards, collective_id):
+    halo.wait()
+
+
+def gather_call(shards, tokens, collective_id):
     streams, spans = lax.axis_size("stream"), lax.axis_size("span")
     shapes = [shard.shape for shard in shards]
-    outs = pl.pallas_call(
+    hbm = pl.BlockSpec(memory_space=pl.ANY)
+    return pl.pallas_call(
         functools.partial(gather_kernel, streams, spans, len(shards)),
-        in_specs=[pl.BlockSpec(memory_space=pltpu.VMEM)] * len(shards),
-        out_specs=[pl.BlockSpec(memory_space=pl.ANY)] * len(shards),
-        out_shape=[jax.ShapeDtypeStruct((spans,) + s.shape, s.dtype) for s in shards],
-        scratch_shapes=Gather.sem_shapes(shapes, streams, spans),
+        in_specs=[pl.BlockSpec(memory_space=pltpu.VMEM)] * len(shards) + [hbm],
+        out_specs=[hbm] * (len(shards) + 1),
+        out_shape=[jax.ShapeDtypeStruct((spans,) + s.shape, s.dtype) for s in shards]
+        + [jax.ShapeDtypeStruct((HALO, tokens.shape[1]), tokens.dtype)],
+        scratch_shapes=Gather.sem_shapes(shapes, streams, spans) + [pltpu.SemaphoreType.DMA((2,))],
         compiler_params=pltpu.CompilerParams(
             collective_id=collective_id, has_side_effects=True, vmem_limit_bytes=VMEM_LIMIT
         ),
         name="gather_weights",
-    )(*shards)
-    return outs
+    )(*shards, tokens)
 
 
 class Reduce:
@@ -1131,16 +1145,17 @@
 def backward_kernel(streams, spans, heads, weights, *refs):
     (keep_ref, gn_ref, read_ref, gain_ref, q_ref, k_ref, v_ref, wk_ref, inv_ref, min_ref, pre_ref,
      nv_ref, np_ref, rate_ref, allow_ref, eq_ref, ek_ref, ev_ref, cq_ref, ck_ref, cv_ref,
-     p_low, p_high, p_chip, pair_ref, wq_ref, wkey_ref, wv_ref) = refs[:28]
-    refs = refs[28:]
+     p_low, p_high, p_chip, pair_ref, wq_ref, wkey_ref, wv_ref, heads_ref, attn_ref) = refs[:30]
+    refs = refs[30:]
     grads, refs = refs[:weights], refs[weights:]
     gconv_ref, grate_ref, gain_grad_ref, gnormed_ref = refs[:4]
-    halves, sums, refs = refs[4:7], refs[7:10], refs[10:]
+    halves, edge_ref, out_grad_ref, sums, refs = refs[4:7], refs[7], refs[8], refs[9:12], refs[12:]
     bufs, refs = [refs[9 * w : 9 * w + 9] for w in range(weights)], refs[9 * weights :]
     reduce_sems, refs = refs[:3], refs[3:]
     go_buf, adj_buf, din_buf = refs[:3]
     pair_buf, own_buf, got_buf, pair_sem = refs[3:7]
-    row_bufs, chain_bufs = refs[7:10], refs[10:]
+    edge_buf, edge_got, attn_give, attn_got, edge_sem = refs[7:12]
+    row_bufs, chain_bufs = refs[12:15], refs[15:]
     step_id = pl.program_id(0)
     turns = heads // GROUP
     place = Place(streams, spans)
@@ -1169,10 +1184,26 @@
             halves[i][:, :, lanes] = grad[:, lanes_of(i, size)].reshape(-1, rows, size)
         hand_over(turn).wait_send()
 
+    half = attn_got.shape[1]
+
+    def columns(core):
+        return attn_ref[:, pl.ds(pl.multiple_of(core * half, half), half)]
+
+    attn_copy = copy_to(attn_give, attn_got, edge_sem.at[0], edge_sem.at[1], place.other())
+    edge_copy = copy_to(edge_buf, edge_got, edge_sem.at[2], edge_sem.at[3], place.span_at(-1))
+
     @pl.when(step_id == 0)
     def _():
-        greet(work.neighbours())
+        greet(work.neighbours() + place.either_side())
+        attn_give[...] = columns(1 - place.core)
+        attn_copy.start()
         pair_buf[...] = pair_ref[...].T
+
+    @pl.when(step_id == 1)
+    def _():
+        attn_copy.wait()
+        both = jnp.concatenate([columns(place.core), attn_got[...]], 0)
+        out_grad_ref[...] = tn(heads_ref[...], both).astype(BF16).reshape(out_grad_ref.shape)
 
     for index in range(2 * turns + 1):
 
@@ -1218,15 +1249,20 @@
 
     @pl.when(step_id == 2 * turns)
     def _():
+        edge_buf[...] = gnormed_ref[:HALO, :].astype(BF16)
+        edge_copy.start()
         weigh(turns - 1)
         for index in range(2 * turns + 1, slots + 1):
             for step in spread_steps(steps, REDUCE_AHEAD, slots, index):
                 step()
+        edge_copy.wait()
+        edge_ref[...] = edge_got[...]
 
 
 def backward_call(
     keep, grad_normal, readout, gain, queries, keys, values, wkeys, invs, state, prefix,
-    new_v, new_p, rate, allow, ext, conv, maps, pair_normed, w_qkv, grads, heads, collective_id,
+    new_v, new_p, rate, allow, ext, conv, maps, pair_normed, w_qkv,
+    pair_heads, grad_attn, grads, heads, collective_id,
 ):
     streams, spans = lax.axis_size("stream"), lax.axis_size("span")
     tok, width = queries.shape
@@ -1277,7 +1313,7 @@
             part(0), part(1), part(2),
             third(0, taps), third(1, taps), third(2, taps),
             whole(half, size, size), whole(half, size, size), whole(half, size, size),
-            vmem, third(0, width), third(1, width), third(2, width),
+            vmem, third(0, width), third(1, width), third(2, width), vmem, vmem,
         ]
         + [vmem] * len(grads),
         out_specs=[
@@ -1286,7 +1322,7 @@
             pl.BlockSpec((GROUP, 1, size), lambda h: (first(h), 0, 0)),
             whole(rows, width),
         ]
-        + [vmem] * 6,
+        + [vmem] * 8,
         out_shape=[
             jax.ShapeDtypeStruct((3, taps, width), F32),
             jax.ShapeDtypeStruct((tok, heads), F32),
@@ -1294,6 +1330,10 @@
             jax.ShapeDtypeStruct((rows, width), F32),
         ]
         + [jax.ShapeDtypeStruct((spans, width // spans, width // 2), BF16)] * 3
+        + [
+            jax.ShapeDtypeStruct((HALO, width), BF16),
+            jax.ShapeDtypeStruct((spans, width // spans, width // 2), BF16),
+        ]
         + [
             jax.ShapeDtypeStruct((shapes[0][1], 2 * shapes[0][2]), BF16),
             jax.ShapeDtypeStruct(shapes[1][1:], BF16),
@@ -1308,6 +1348,11 @@
             pltpu.VMEM((heads, rows, 3 * size), BF16),
             pltpu.VMEM((turns, rows, 3 * size), BF16),
             pltpu.SemaphoreType.DMA((turns, 2)),
+            pltpu.VMEM((HALO, width), BF16),
+            pltpu.VMEM((HALO, width), BF16),
+            pltpu.VMEM((tok, width // 2), BF16),
+            pltpu.VMEM((tok, width // 2), BF16),
+            pltpu.SemaphoreType.DMA((4,)),
         ]
         + [pltpu.VMEM((tok, wide), F32)] * 3
         + chain_scratch(heads, size, size, True),
@@ -1318,9 +1363,9 @@
     )(
         keep, grad_normal, readout, gain, queries, keys, values, wkeys, invs, state, prefix,
         new_v, new_p, rate, allow, ext, ext, ext, conv, conv, conv, *maps, pair_normed,
-        w_qkv, w_qkv, w_qkv, *grads,
-    )
-    return outs[:4], outs[4:7], outs[7:]
+        w_qkv, w_qkv, w_qkv, pair_heads, grad_attn, *grads,
+    )
+    return outs[:4], outs[4:9], outs[9:]
 
 
 def feed_kernel(
@@ -1501,7 +1546,7 @@
     )
     small_len = small.shape[0]
     small = jnp.pad(small, (0, 16 * 512 - small_len)).reshape(16, 512)
-    full_qkv, smalls = gather_call([w_qkv, small], 1)
+    full_qkv, smalls, before = gather_call([w_qkv, small], tokens[0], 1)
     full_qkv = full_qkv.reshape(-1, full_qkv.shape[2])
     smalls = smalls.reshape(span_count, -1)
 
@@ -1534,10 +1579,6 @@
         [1.0 - token_start * (token_offset < tap).astype(F32) for tap in range(taps)], 1
     )
 
-    ends = tokens[0, tok_rows - HALO :]
-    before = lax.ppermute(
-        ends, "span", [(i, i + 1) for i in range(span_count - 1)]
-    )
     inputs_ext = jnp.concatenate([before, tokens[0]], 0).astype(F32)
     inv_ext = lax.rsqrt(jnp.mean(inputs_ext * inputs_ext, -1, keepdims=True) + EPSILON)
     normed_ext = (inputs_ext * inv_ext * attn_gain).astype(BF16)
@@ -1561,20 +1602,19 @@
         full_down, 3,
     )
     half_down = half_down.reshape(span_count, -1, half_down.shape[1])
-    half_out = weight_grad(pair_tokens(normal_heads), pair_half(grad_attn_in), span_count)
     (
-        (grad_conv, grad_strength, head_grads, grad_normed_ext), (half_q, half_k, half_v), ffn_parts
+        (grad_conv, grad_strength, head_grads, grad_normed_ext),
+        (half_q, half_k, half_v, halo_back, half_out),
+        ffn_parts,
     ) = backward_call(
         stretch_keep, grad_normal, readout, head_gain, queries, keys, values, wkeys, invs,
         state_in, prefix, new_v, new_p, strength, allow, projected, full_conv,
-        (p_low, p_high, p_chip), pair_tokens(normed_ext), full_qkv, [half_down, half_ffn], heads, 4,
+        (p_low, p_high, p_chip), pair_tokens(normed_ext), full_qkv, pair_tokens(normal_heads),
+        grad_attn_in, [half_down, half_ffn], heads, 4,
     )
     grad_logit = grad_strength * strength * (1.0 - strength)
     grad_logit_low = grad_logit.astype(BF16)
     grad_w_beta = product("td,th->dh", normed, grad_logit_low)
-    halo_back = lax.ppermute(
-        grad_normed_ext[:HALO].astype(BF16), "span", [(i, i - 1) for i in range(1, span_count)]
-    )
     grad_normed = (
         grad_normed_ext[HALO:]
         + product("th,dh->td", grad_logit_low, full_beta)

time: 394 us -> 387 us (0.982)
  starting transfers between devices: 5.73 us -> 0.65 us
  transfers between devices with their start and end apart: 6 -> 3, of which waited for: 1 -> 0; matrix products, arithmetic and copies ran while one was open for 5% -> 2% of each run, Pallas kernels for 19% -> 8%
where the time goes in v6:
time: 387 us; the launch traced here: 386 us
  Pallas kernels  351 us (91%)
  local copies, waits for them, and re-layouts  17.3 us (4%)
  other arithmetic  13.8 us (4%)
    pallas_call x1, Pallas kernels, backward_call(): pl.pallas_call(functools.partial(backward_kernel, streams, spans, heads,...  137 us
    pallas_call x1, Pallas kernels, forward_call(): pl.pallas_call(functools.partial(forward_kernel, streams, spans, heads, l...  84.9 us
    pallas_call x1, Pallas kernels, reduce_call(): pl.pallas_call(functools.partial(reduce_kernel, streams, spans), in_specs...  56.3 us
    pallas_call x1, Pallas kernels, gather_call(): pl.pallas_call(functools.partial(gather_kernel, streams, spans, len(shard...  41.9 us
    pallas_call x1, Pallas kernels, feed_call(): pl.pallas_call(functools.partial(feed_kernel, streams, spans), grid=(coun...  31 us
    unnamed x55, local copies, waits for them, and re-layouts  7.84 us
  transfers between devices with their start and end apart: 3, of which 0 were waited for; matrix products, arithmetic and copies ran while one was open for 2% of the time, Pallas kernels for 8%

profile of v6, /device:TPU:0, one launch (start us, length us, event | category | flops | bytes accessed | tf_op | source)
XLA Modules:
  0.0 386.1 jit_solution(3299085884556167118)
XLA Ops:
  0.6 0.0 copy-start
  0.7 0.8 reshape.259
  1.4 0.8 copy.45
  2.2 0.1 reshape.260
  2.3 0.3 dynamic-update-slice
  2.6 0.2 dynamic-update-slice.1
  2.8 0.8 dynamic-update-slice.2
  3.6 0.8 dynamic-update-slice.3
  4.5 0.8 dynamic-update-slice.4
  5.3 0.6 reshape.261.refs_1_
  5.9 41.9 %gather_weights.1 = (bf16[8,128,3072]{2,1,0:T(8,128)(2,1)}, bf16[8,16,512]{2,1,0:T(8,128)(2,1)}, bf16[16,1024]{1,0:T(8,128)(2,1)}) custom-call(bf16[128,3072]{1,0:T(8,128)(2,1)} %refs_0_.1, bf16[16,512]{1,0:T(8,128)(2,1)} %reshape.261.refs_1_, bf16[256,1024]{1,0:T(8,128)(2,1)} %bitcast.51), custom_call_target="tpu_custom_call" | custom-call | tf_op jit(solution)/shard_map/gather_weights/pallas_call | solution.py:578
  47.9 1.0 copy.56
  48.9 0.6 slice_convert_fusion
  49.5 0.2 reduce-window_clone.1
  49.7 0.2 compare_reduce_fusion
  49.9 0.5 broadcast_subtract_fusion.refs_0_
  50.4 1.0 multiply_reduce_fusion
  51.4 0.6 copy.57
  52.0 0.3 reshape_reshape.3
  52.3 0.1 broadcast_in_dim.8
  52.4 0.1 reshape.266
  52.5 0.8 copy.47.refs_9_.refs_14_
  53.3 0.6 reshape.282.refs_10_.refs_3_
  53.9 0.2 multiply_convert_fusion.refs_1_
  54.1 0.0 copy-start.2
  54.1 1.0 fusion.3.refs_8_.refs_13_
  55.1 84.9 %delta_forward.1 = (bf16[3,272,1024]{2,1,0:T(8,128)(2,1)}, bf16[256,1024]{1,0:T(8,128)(2,1)}, bf16[256,1024]{1,0:T(8,128)(2,1)}, bf16[256,1024]{1,0:T(8,128)(2,1...) custom-call(f32[4]{0:T(128)} %broadcast_subtract_fusion.refs_0_, ...), custom_call_target="tpu_custom_call" | custom-call | tf_op jit(solution)/shard_map/delta_forward/pallas_call | solution.py:1093
  140.0 0.2 collective-permute-start.1
  140.2 0.4 collective-permute-start
  140.6 0.1 slice.57
  140.7 31.0 %feed_forward.1 = (bf16[256,1024]{1,0:T(8,128)(2,1)}, f32[256,1024]{1,0:T(8,128)}, bf16[256,1024]{1,0:T(8,128)(2,1)}, f32[256,1024]{1,0:T(8,128)}, f32[1,1024]{1...) custom-call(bf16[256,1024]{1,0:T(8,128)(2,1)} %get-tuple-element.60.heads_ref, ...), custom_call_target="tpu_custom_call" | custom-call | tf_op jit(solution)/shard_map/feed_forward/pallas_call | solution.py:1494
  171.7 0.1 maximum_convert_fusion
  171.8 0.0 copy-start.3
  171.9 0.9 copy-done.4
  172.7 1.0 pad_maximum_fusion.1.refs_28_
  173.8 1.1 pad_maximum_fusion.refs_24_
  174.8 137.3 %delta_backward.1 = (f32[3,4,1024]{2,1,0:T(4,128)}, f32[256,8]{1,0:T(8,128)}, f32[8,1,128]{2,1,0:T(1,128)}, f32[272,1024]{1,0:T(8,128)}, bf16[8,128,512]{2,1,0:T...) custom-call(f32[4]{0:T(128)} %broadcast_subtract_fusion.refs_0_, ...), custom_call_target="tpu_custom_call" | custom-call | tf_op jit(solution)/shard_map/delta_backward/pallas_call | solution.py:1301
  312.1 1.0 fusion.7
  313.2 0.3 fusion.4
  313.6 0.5 multiply_reduce_fusion.1
  314.1 0.2 copy-done.16
  314.4 0.3 reshape.274
  314.7 0.1 reshape.277
  314.8 0.1 concatenate.19
  315.0 0.4 reshape.278
  315.4 0.5 constant_dynamic-slice_fusion.1
  316.0 0.1 collective-permute-start.2
  316.0 0.5 copy-done.11
  316.5 1.2 convert_element_type.78
  317.7 1.2 convert_element_type.79
  318.9 0.2 copy-done.9
  319.1 1.3 convert_element_type.80
  320.3 1.3 add_bitcast_fusion
  321.6 0.7 bitcast_add_fusion.refs_4_
  322.4 56.3 %reduce_grads.1 = (bf16[128,1024]{1,0:T(8,128)(2,1)}, bf16[128,3072]{1,0:T(8,128)(2,1)}, f32[16,1024]{1,0:T(8,128)}) custom-call(bf16[8,128,512]{2,1,0:T(8,128)(2,1)} %get-tuple-element.88.refs_0_, bf16[8,128,512]{2,1,0:T(8,128)(2,1)} %get-tuple-element.89.refs_1_, bf16[8,128,512]{2,1,0:T(8,128)(2,1)} %get-tuple-element.90.refs_2_, ...), custom_call_target="tpu_custom_call" | custom-call | tf_op jit(solution)/shard_map/reduce_grads/pallas_call | solution.py:887
  378.7 1.5 slice.62
  380.3 0.6 slice.77
  380.9 0.5 fusion.14
  381.4 0.5 slice.79
  381.9 1.3 convert_element_type.76
  383.2 0.6 reshape.280
  383.8 0.7 copy.51
  384.5 0.8 convert_element_type.77
  385.3 0.8 copy.68
  (62 shorter events, 0.3 us)
Async XLA Ops:
  0.6 49.8 %copy-start = (bf16[1,256,1024]{2,1,0:T(8,128)(2,1)S(1)}, bf16[1,256,1024]{2,1,0:T(8,128)(2,1)}, u32[]{:S(2)}) copy-start(bf16[1,256,1024]{2,1,0:T(8,128)(2,1)} %param.14) | copy-start | bytes 1572868
  0.7 48.8 %copy-start.20 = (s32[1,3]{1,0:T(1,128)S(1)}, s32[1,3]{1,0:T(1,128)}, u32[]{:S(2)}) copy-start(s32[1,3]{1,0:T(1,128)} %param.16) | copy-start | bytes 40
  47.9 6.0 %copy-start.13 = (bf16[16,1024]{1,0:T(8,128)(2,1)S(1)}, bf16[16,1024]{1,0:T(8,128)(2,1)}, u32[]{:S(2)}) copy-start(bf16[16,1024]{1,0:T(8,128)(2,1)} %get-tuple-element.57) | copy-start | bytes 98308
  49.5 4.6 %copy-start.21 = (f32[8]{0:T(128)S(1)}, f32[8]{0:T(128)}, u32[]{:S(2)}) copy-start(f32[8]{0:T(128)} %param.20) | copy-start | bytes 100
  54.1 1.0 copy-start.2
  140.0 31.8 %collective-permute-start.1 = (bf16[256,1024]{1,0:T(8,128)(2,1)}, bf16[256,1024]{1,0:T(8,128)(2,1)S(1)}, u32[]{:S(2)}, u32[]{:S(2)}) collective-permute-start(bf16[256,1024]{1,0:T(8,128)(2,1)} %get-tuple-element.60.heads_ref), channel_id=1, source_target_pairs={{0,1},{1,0},{2,3},{3,2},{4,5},{5,4},{6,7},{7,6},{8,9},{9,8},{10,11... | collective-permute-start | bytes 1572872 | tf_op jit(solution)/shard_map/ppermute | solution.py:293
  140.2 33.5 %collective-permute-start = (bf16[272,1024]{1,0:T(8,128)(2,1)}, bf16[272,1024]{1,0:T(8,128)(2,1)S(1)}, u32[]{:S(2)}, u32[]{:S(2)}) collective-permute-start(bf16[272,1024]{1,0:T(8,128)(2,1)} %copy-done.2), channel_id=1, source_target_pairs={{0,1},{1,0},{2,3},{3,2},{4,5},{5,4},{6,7},{7,6},{8,9},{9,8},{10,11... | collective-permute-start | bytes 1671176 | tf_op jit(solution)/shard_map/ppermute | solution.py:293
  140.7 31.0 %copy-start.1 = (bf16[1,256,1024]{2,1,0:T(8,128)(2,1)S(1)}, bf16[1,256,1024]{2,1,0:T(8,128)(2,1)}, u32[]{:S(2)}) copy-start(bf16[1,256,1024]{2,1,0:T(8,128)(2,1)} %param.14) | copy-start | bytes 1572868
  171.7 1.0 copy-start.4
  171.8 1.9 copy-start.3
  174.8 137.3 %copy-start.5 = (f32[256,8]{1,0:T(8,128)S(1)}, f32[256,8]{1,0:T(8,128)}, u32[]{:S(2)}) copy-start(f32[256,8]{1,0:T(8,128)} %fusion.3.refs_8_.refs_13_) | copy-start | bytes 24580
  312.1 1.4 copy-start.7
  312.1 1.4 copy-start.17
  313.6 0.8 copy-start.16
  313.6 1.1 copy-start.19
  313.6 1.2 copy-start.18
  315.4 1.1 copy-start.11
  316.0 1.8 copy-start.10
  316.0 5.6 %collective-permute-start.2 = (f32[8,16,512]{2,1,0:T(8,128)S(1)}, f32[8,16,512]{2,1,0:T(8,128)S(1)}, u32[]{:S(2)}, u32[]{:S(2)}) collective-permute-start(f32[8,16,512]{2,1,0:T(8,128)S(1)} %bitcast.70), channel_id=1, source_target_pairs={{0,1},{1,0},{2,3},{3,2},{4,5},{5,4},{6,7},{7,6},{8,9},{9,8},{10,11... | collective-permute-start | bytes 786440 | tf_op jit(solution)/shard_map/ppermute | solution.py:293
  317.7 1.4 copy-start.9
  318.9 1.4 copy-start.6
  378.7 1.5 copy-start.15
  378.7 3.2 copy-start.8
  381.9 2.6 copy-start.14
  381.9 3.4 copy-start.12

commit v7 on v6

--- a/solution.py
+++ b/solution.py
@@ -20,7 +20,7 @@
 GATHER_LAG = 2
 REDUCE_PIECE = 100 * 1024
 REDUCE_AHEAD = 6
-FORWARD_SLOTS = 11
+FORWARD_SLOTS = 10
 BACKWARD_SLOTS = 11
 
 
@@ -598,13 +598,7 @@
 
     @staticmethod
     def cut(shapes, streams):
-        units = units_of([s[1:] for s in shapes], streams, REDUCE_PIECE // shapes[0][0])
-        sizes = [sum(u[0] == w for u in units) for w in range(len(shapes))]
-        order = []
-        for w, size in enumerate(sizes):
-            own = [u for u in units if u[0] == w]
-            order += [((n + 0.5) / size, w, u) for n, u in enumerate(own)]
-        return [u for _, _, u in sorted(order)]
+        return units_of([s[1:] for s in shapes], streams, REDUCE_PIECE // shapes[0][0])
 
     @staticmethod
     def plan(units, shapes, streams, share):
@@ -1163,7 +1157,7 @@
         split_columns(sums[0], grads[0].shape[2]),
         [(sums[1], 0, 1), (sums[2], 0, 1)],
     ]
-    work = Reduce(place, grads, targets, bufs, reduce_sems, 0.2)
+    work = Reduce(place, grads, targets, bufs, reduce_sems, 0.1)
     steps = work.steps()
     slots = BACKWARD_SLOTS
     size = gain_ref.shape[1]

time: 387 us -> 377 us (0.974)
  Pallas kernels: 351 us -> 342 us
    pallas_call x1, Pallas kernels: 137 us -> 128 us  [backward_call(): pl.pallas_call(functools.partial(backward_kernel, streams, spans, heads,...]
where the time goes in v7:
time: 377 us
  Pallas kernels  342 us (91%)
  local copies, waits for them, and re-layouts  17.3 us (5%)
  other arithmetic  13.8 us (4%)
    pallas_call x1, Pallas kernels, backward_call(): pl.pallas_call(functools.partial(backward_kernel, streams, spans, heads,...  128 us
    pallas_call x1, Pallas kernels, forward_call(): pl.pallas_call(functools.partial(forward_kernel, streams, spans, heads, l...  85.7 us
    pallas_call x1, Pallas kernels, reduce_call(): pl.pallas_call(functools.partial(reduce_kernel, streams, spans), in_specs...  55 us
    pallas_call x1, Pallas kernels, gather_call(): pl.pallas_call(functools.partial(gather_kernel, streams, spans, len(shard...  41.9 us
    pallas_call x1, Pallas kernels, feed_call(): pl.pallas_call(functools.partial(feed_kernel, streams, spans), grid=(coun...  31.1 us
    unnamed x55, local copies, waits for them, and re-layouts  7.84 us
  transfers between devices with their start and end apart: 3, of which 0 were waited for; matrix products, arithmetic and copies ran while one was open for 2% of the time, Pallas kernels for 8%

profile of v7, /device:TPU:0, one launch (start us, length us, event | category | flops | bytes accessed | tf_op | source)
XLA Modules:
  0.0 376.5 jit_solution(2814855396759455471)
XLA Ops:
  0.6 0.0 copy-start
  0.7 0.8 reshape.259
  1.4 0.8 copy.45
  2.2 0.1 reshape.260
  2.3 0.3 dynamic-update-slice
  2.6 0.2 dynamic-update-slice.1
  2.8 0.8 dynamic-update-slice.2
  3.6 0.8 dynamic-update-slice.3
  4.5 0.8 dynamic-update-slice.4
  5.3 0.6 reshape.261.refs_1_
  5.9 41.9 %gather_weights.1 = (bf16[8,128,3072]{2,1,0:T(8,128)(2,1)}, bf16[8,16,512]{2,1,0:T(8,128)(2,1)}, bf16[16,1024]{1,0:T(8,128)(2,1)}) custom-call(bf16[128,3072]{1,0:T(8,128)(2,1)} %refs_0_.1, bf16[16,512]{1,0:T(8,128)(2,1)} %reshape.261.refs_1_, bf16[256,1024]{1,0:T(8,128)(2,1)} %bitcast.51), custom_call_target="tpu_custom_call" | custom-call | tf_op jit(solution)/shard_map/gather_weights/pallas_call | solution.py:578
  47.9 1.0 copy.56
  48.9 0.6 slice_convert_fusion
  49.5 0.2 reduce-window_clone.1
  49.7 0.2 compare_reduce_fusion
  49.9 0.5 broadcast_subtract_fusion.refs_0_
  50.4 1.0 multiply_reduce_fusion
  51.4 0.6 copy.57
  52.0 0.3 reshape_reshape.3
  52.3 0.1 broadcast_in_dim.8
  52.4 0.1 reshape.266
  52.5 0.8 copy.47.refs_9_.refs_14_
  53.3 0.6 reshape.282.refs_10_.refs_3_
  53.9 0.2 multiply_convert_fusion.refs_1_
  54.1 0.0 copy-start.2
  54.1 1.0 fusion.3.refs_8_.refs_13_
  55.1 85.7 %delta_forward.1 = (bf16[3,272,1024]{2,1,0:T(8,128)(2,1)}, bf16[256,1024]{1,0:T(8,128)(2,1)}, bf16[256,1024]{1,0:T(8,128)(2,1)}, bf16[256,1024]{1,0:T(8,128)(2,1...) custom-call(f32[4]{0:T(128)} %broadcast_subtract_fusion.refs_0_, ...), custom_call_target="tpu_custom_call" | custom-call | tf_op jit(solution)/shard_map/delta_forward/pallas_call | solution.py:1087
  140.8 0.4 collective-permute-start.1
  141.3 0.1 collective-permute-start
  141.4 0.1 slice.57
  141.5 31.1 %feed_forward.1 = (bf16[256,1024]{1,0:T(8,128)(2,1)}, f32[256,1024]{1,0:T(8,128)}, bf16[256,1024]{1,0:T(8,128)(2,1)}, f32[256,1024]{1,0:T(8,128)}, f32[1,1024]{1...) custom-call(bf16[256,1024]{1,0:T(8,128)(2,1)} %get-tuple-element.60.heads_ref, ...), custom_call_target="tpu_custom_call" | custom-call | tf_op jit(solution)/shard_map/feed_forward/pallas_call | solution.py:1488
  172.6 0.1 maximum_convert_fusion
  172.8 0.0 copy-start.3
  172.8 0.9 copy-done.4
  173.7 1.0 pad_maximum_fusion.1.refs_28_
  174.7 1.1 pad_maximum_fusion.refs_24_
  175.8 128.2 %delta_backward.1 = (f32[3,4,1024]{2,1,0:T(4,128)}, f32[256,8]{1,0:T(8,128)}, f32[8,1,128]{2,1,0:T(1,128)}, f32[272,1024]{1,0:T(8,128)}, bf16[8,128,512]{2,1,0:T...) custom-call(f32[4]{0:T(128)} %broadcast_subtract_fusion.refs_0_, ...), custom_call_target="tpu_custom_call" | custom-call | tf_op jit(solution)/shard_map/delta_backward/pallas_call | solution.py:1295
  304.0 1.0 fusion.7
  305.0 0.3 fusion.4
  305.4 0.5 multiply_reduce_fusion.1
  305.9 0.2 copy-done.16
  306.2 0.3 reshape.274
  306.6 0.1 reshape.277
  306.6 0.1 concatenate.19
  306.8 0.4 reshape.278
  307.2 0.5 constant_dynamic-slice_fusion.1
  307.8 0.1 collective-permute-start.2
  307.9 0.5 copy-done.11
  308.3 1.2 convert_element_type.78
  309.5 1.2 convert_element_type.79
  310.7 0.2 copy-done.9
  310.9 1.3 convert_element_type.80
  312.2 1.3 add_bitcast_fusion
  313.4 0.7 bitcast_add_fusion.refs_4_
  314.2 55.0 %reduce_grads.1 = (bf16[128,1024]{1,0:T(8,128)(2,1)}, bf16[128,3072]{1,0:T(8,128)(2,1)}, f32[16,1024]{1,0:T(8,128)}) custom-call(bf16[8,128,512]{2,1,0:T(8,128)(2,1)} %get-tuple-element.88.refs_0_, bf16[8,128,512]{2,1,0:T(8,128)(2,1)} %get-tuple-element.89.refs_1_, bf16[8,128,512]{2,1,0:T(8,128)(2,1)} %get-tuple-element.90.refs_2_, ...), custom_call_target="tpu_custom_call" | custom-call | tf_op jit(solution)/shard_map/reduce_grads/pallas_call | solution.py:881
  369.2 1.5 slice.62
  370.7 0.6 slice.77
  371.3 0.5 fusion.14
  371.8 0.5 slice.79
  372.3 1.3 convert_element_type.76
  373.6 0.6 reshape.280
  374.2 0.7 copy.51
  374.9 0.8 convert_element_type.77
  375.8 0.8 copy.68
  (62 shorter events, 0.3 us)
Async XLA Ops:
  0.6 49.8 %copy-start = (bf16[1,256,1024]{2,1,0:T(8,128)(2,1)S(1)}, bf16[1,256,1024]{2,1,0:T(8,128)(2,1)}, u32[]{:S(2)}) copy-start(bf16[1,256,1024]{2,1,0:T(8,128)(2,1)} %param.14) | copy-start | bytes 1572868
  0.7 48.8 %copy-start.20 = (s32[1,3]{1,0:T(1,128)S(1)}, s32[1,3]{1,0:T(1,128)}, u32[]{:S(2)}) copy-start(s32[1,3]{1,0:T(1,128)} %param.16) | copy-start | bytes 40
  47.9 6.0 %copy-start.13 = (bf16[16,1024]{1,0:T(8,128)(2,1)S(1)}, bf16[16,1024]{1,0:T(8,128)(2,1)}, u32[]{:S(2)}) copy-start(bf16[16,1024]{1,0:T(8,128)(2,1)} %get-tuple-element.57) | copy-start | bytes 98308
  49.5 4.6 %copy-start.21 = (f32[8]{0:T(128)S(1)}, f32[8]{0:T(128)}, u32[]{:S(2)}) copy-start(f32[8]{0:T(128)} %param.20) | copy-start | bytes 100
  54.1 1.0 copy-start.2
  140.8 32.0 %collective-permute-start.1 = (bf16[256,1024]{1,0:T(8,128)(2,1)}, bf16[256,1024]{1,0:T(8,128)(2,1)S(1)}, u32[]{:S(2)}, u32[]{:S(2)}) collective-permute-start(bf16[256,1024]{1,0:T(8,128)(2,1)} %get-tuple-element.60.heads_ref), channel_id=1, source_target_pairs={{0,1},{1,0},{2,3},{3,2},{4,5},{5,4},{6,7},{7,6},{8,9},{9,8},{10,11... | collective-permute-start | bytes 1572872 | tf_op jit(solution)/shard_map/ppermute | solution.py:293
  141.3 33.4 %collective-permute-start = (bf16[272,1024]{1,0:T(8,128)(2,1)}, bf16[272,1024]{1,0:T(8,128)(2,1)S(1)}, u32[]{:S(2)}, u32[]{:S(2)}) collective-permute-start(bf16[272,1024]{1,0:T(8,128)(2,1)} %copy-done.2), channel_id=1, source_target_pairs={{0,1},{1,0},{2,3},{3,2},{4,5},{5,4},{6,7},{7,6},{8,9},{9,8},{10,11... | collective-permute-start | bytes 1671176 | tf_op jit(solution)/shard_map/ppermute | solution.py:293
  141.5 31.2 %copy-start.1 = (bf16[1,256,1024]{2,1,0:T(8,128)(2,1)S(1)}, bf16[1,256,1024]{2,1,0:T(8,128)(2,1)}, u32[]{:S(2)}) copy-start(bf16[1,256,1024]{2,1,0:T(8,128)(2,1)} %param.14) | copy-start | bytes 1572868
  172.6 1.0 copy-start.4
  172.8 1.9 copy-start.3
  175.8 128.2 %copy-start.5 = (f32[256,8]{1,0:T(8,128)S(1)}, f32[256,8]{1,0:T(8,128)}, u32[]{:S(2)}) copy-start(f32[256,8]{1,0:T(8,128)} %fusion.3.refs_8_.refs_13_) | copy-start | bytes 24580
  303.9 1.4 copy-start.7
  303.9 1.4 copy-start.17
  305.4 0.8 copy-start.16
  305.4 1.1 copy-start.19
  305.4 1.2 copy-start.18
  307.2 1.1 copy-start.11
  307.8 1.8 copy-start.10
  307.8 5.6 %collective-permute-start.2 = (f32[8,16,512]{2,1,0:T(8,128)S(1)}, f32[8,16,512]{2,1,0:T(8,128)S(1)}, u32[]{:S(2)}, u32[]{:S(2)}) collective-permute-start(f32[8,16,512]{2,1,0:T(8,128)S(1)} %bitcast.70), channel_id=1, source_target_pairs={{0,1},{1,0},{2,3},{3,2},{4,5},{5,4},{6,7},{7,6},{8,9},{9,8},{10,11... | collective-permute-start | bytes 786440 | tf_op jit(solution)/shard_map/ppermute | solution.py:293
  309.5 1.4 copy-start.9
  310.7 1.4 copy-start.6
  369.2 1.5 copy-start.15
  369.2 3.2 copy-start.8
  372.3 2.6 copy-start.14
  372.3 3.4 copy-start.12

commit v8 on v7

--- a/solution.py
+++ b/solution.py
@@ -19,9 +19,9 @@
 GATHER_AHEAD = 3
 GATHER_LAG = 2
 REDUCE_PIECE = 100 * 1024
-REDUCE_AHEAD = 6
+REDUCE_AHEAD = 5
 FORWARD_SLOTS = 10
-BACKWARD_SLOTS = 11
+BACKWARD_SLOTS = 13
 
 
 def nn(a, b):
@@ -398,7 +398,8 @@
 
 
 class Gather:
-    def __init__(self, place, shards, fulls, sems):
+    def __init__(self, place, shards, fulls, sems, depth):
+        self.depth = depth
         self.place, self.shards, self.fulls = place, shards, fulls
         self.sems = sems
         self.units = units_of([x.shape for x in shards], place.streams, GATHER_PIECE)
@@ -537,7 +538,7 @@
                         self.sideways(unit, k, 2).wait_send()
                         self.corner(unit, k).wait_send()
 
-        ahead, lag = GATHER_AHEAD, GATHER_LAG
+        ahead, lag = self.depth
         for unit in range(min(ahead, count)):
             steps.append(functools.partial(begin, unit))
         for t in range(count + 2 * lag):
@@ -559,7 +560,7 @@
     shards, tok_ref, fulls = refs[:count], refs[count], refs[count + 1 : 2 * count + 1]
     halo_ref, sems, halo_sem = refs[2 * count + 1], refs[2 * count + 2 : -1], refs[-1]
     place = Place(streams, spans)
-    work = Gather(place, shards, fulls, sems)
+    work = Gather(place, shards, fulls, sems, (2, 1))
     greet(work.neighbours() + place.either_side())
     halo = copy_to(
         tok_ref.at[pl.ds(tok_ref.shape[0] - HALO, HALO)], halo_ref, halo_sem.at[0], halo_sem.at[1],
@@ -1019,7 +1020,7 @@
      state_ref, p_low, p_high, p_chip, out_ref, normal_ref) = outs
     step_id = pl.program_id(0)
     place = Place(streams, spans)
-    work = Gather(place, shards, fulls, gather_sems)
+    work = Gather(place, shards, fulls, gather_sems, (GATHER_AHEAD, GATHER_LAG))
     steps = work.steps()
 
     @pl.when(step_id == 0)

time: 377 us -> 376 us (level)
  no operation moved by 1% of the time
where the time goes in v8:
time: 376 us
  Pallas kernels  341 us (91%)
  local copies, waits for them, and re-layouts  17.3 us (5%)
  other arithmetic  13.8 us (4%)
    pallas_call x1, Pallas kernels, backward_call(): pl.pallas_call(functools.partial(backward_kernel, streams, spans, heads,...  126 us
    pallas_call x1, Pallas kernels, forward_call(): pl.pallas_call(functools.partial(forward_kernel, streams, spans, heads, l...  88 us
    pallas_call x1, Pallas kernels, reduce_call(): pl.pallas_call(functools.partial(reduce_kernel, streams, spans), in_specs...  55.5 us
    pallas_call x1, Pallas kernels, gather_call(): pl.pallas_call(functools.partial(gather_kernel, streams, spans, len(shard...  40.2 us
    pallas_call x1, Pallas kernels, feed_call(): pl.pallas_call(functools.partial(feed_kernel, streams, spans), grid=(coun...  31.1 us
    unnamed x55, local copies, waits for them, and re-layouts  7.84 us
  transfers between devices with their start and end apart: 3, of which 0 were waited for; matrix products, arithmetic and copies ran while one was open for 2% of the time, Pallas kernels for 8%

profile of v8, /device:TPU:0, one launch (start us, length us, event | category | flops | bytes accessed | tf_op | source)
XLA Modules:
  0.0 375.9 jit_solution(6033459099587880277)
XLA Ops:
  0.6 0.0 copy-start
  0.7 0.8 reshape.259
  1.4 0.8 copy.45
  2.2 0.1 reshape.260
  2.3 0.3 dynamic-update-slice
  2.6 0.2 dynamic-update-slice.1
  2.8 0.8 dynamic-update-slice.2
  3.6 0.8 dynamic-update-slice.3
  4.5 0.8 dynamic-update-slice.4
  5.3 0.6 reshape.261.refs_1_
  5.9 40.2 %gather_weights.1 = (bf16[8,128,3072]{2,1,0:T(8,128)(2,1)}, bf16[8,16,512]{2,1,0:T(8,128)(2,1)}, bf16[16,1024]{1,0:T(8,128)(2,1)}) custom-call(bf16[128,3072]{1,0:T(8,128)(2,1)} %refs_0_.1, bf16[16,512]{1,0:T(8,128)(2,1)} %reshape.261.refs_1_, bf16[256,1024]{1,0:T(8,128)(2,1)} %bitcast.51), custom_call_target="tpu_custom_call" | custom-call | tf_op jit(solution)/shard_map/gather_weights/pallas_call | solution.py:579
  46.1 1.0 copy.56
  47.1 0.6 slice_convert_fusion
  47.7 0.2 reduce-window_clone.1
  47.9 0.2 compare_reduce_fusion
  48.1 0.5 broadcast_subtract_fusion.refs_0_
  48.7 1.0 multiply_reduce_fusion
  49.6 0.6 copy.57
  50.2 0.3 reshape_reshape.3
  50.6 0.1 broadcast_in_dim.8
  50.7 0.1 reshape.266
  50.8 0.8 copy.47.refs_9_.refs_14_
  51.6 0.6 reshape.282.refs_10_.refs_3_
  52.2 0.2 multiply_convert_fusion.refs_1_
  52.4 0.0 copy-start.2
  52.4 1.0 fusion.3.refs_8_.refs_13_
  53.4 88.0 %delta_forward.1 = (bf16[3,272,1024]{2,1,0:T(8,128)(2,1)}, bf16[256,1024]{1,0:T(8,128)(2,1)}, bf16[256,1024]{1,0:T(8,128)(2,1)}, bf16[256,1024]{1,0:T(8,128)(2,1...) custom-call(f32[4]{0:T(128)} %broadcast_subtract_fusion.refs_0_, ...), custom_call_target="tpu_custom_call" | custom-call | tf_op jit(solution)/shard_map/delta_forward/pallas_call | solution.py:1088
  141.3 0.4 collective-permute-start.1
  141.8 0.1 collective-permute-start
  141.9 0.1 slice.57
  142.0 31.1 %feed_forward.1 = (bf16[256,1024]{1,0:T(8,128)(2,1)}, f32[256,1024]{1,0:T(8,128)}, bf16[256,1024]{1,0:T(8,128)(2,1)}, f32[256,1024]{1,0:T(8,128)}, f32[1,1024]{1...) custom-call(bf16[256,1024]{1,0:T(8,128)(2,1)} %get-tuple-element.60.heads_ref, ...), custom_call_target="tpu_custom_call" | custom-call | tf_op jit(solution)/shard_map/feed_forward/pallas_call | solution.py:1489
  173.1 0.1 maximum_convert_fusion
  173.2 0.0 copy-start.3
  173.3 0.9 copy-done.4
  174.1 1.0 pad_maximum_fusion.1.refs_28_
  175.2 1.1 pad_maximum_fusion.refs_24_
  176.2 126.5 %delta_backward.1 = (f32[3,4,1024]{2,1,0:T(4,128)}, f32[256,8]{1,0:T(8,128)}, f32[8,1,128]{2,1,0:T(1,128)}, f32[272,1024]{1,0:T(8,128)}, bf16[8,128,512]{2,1,0:T...) custom-call(f32[4]{0:T(128)} %broadcast_subtract_fusion.refs_0_, ...), custom_call_target="tpu_custom_call" | custom-call | tf_op jit(solution)/shard_map/delta_backward/pallas_call | solution.py:1296
  302.8 1.0 fusion.7
  303.8 0.3 fusion.4
  304.2 0.5 multiply_reduce_fusion.1
  304.7 0.2 copy-done.16
  305.0 0.3 reshape.274
  305.4 0.1 reshape.277
  305.4 0.1 concatenate.19
  305.6 0.4 reshape.278
  306.0 0.5 constant_dynamic-slice_fusion.1
  306.6 0.1 collective-permute-start.2
  306.7 0.5 copy-done.11
  307.1 1.2 convert_element_type.78
  308.3 1.2 convert_element_type.79
  309.5 0.2 copy-done.9
  309.7 1.3 convert_element_type.80
  310.9 1.3 add_bitcast_fusion
  312.2 0.7 bitcast_add_fusion.refs_4_
  313.0 55.5 %reduce_grads.1 = (bf16[128,1024]{1,0:T(8,128)(2,1)}, bf16[128,3072]{1,0:T(8,128)(2,1)}, f32[16,1024]{1,0:T(8,128)}) custom-call(bf16[8,128,512]{2,1,0:T(8,128)(2,1)} %get-tuple-element.88.refs_0_, bf16[8,128,512]{2,1,0:T(8,128)(2,1)} %get-tuple-element.89.refs_1_, bf16[8,128,512]{2,1,0:T(8,128)(2,1)} %get-tuple-element.90.refs_2_, ...), custom_call_target="tpu_custom_call" | custom-call | tf_op jit(solution)/shard_map/reduce_grads/pallas_call | solution.py:882
  368.5 1.5 slice.62
  370.1 0.6 slice.77
  370.6 0.5 fusion.14
  371.2 0.5 slice.79
  371.7 1.3 convert_element_type.76
  373.0 0.6 reshape.280
  373.6 0.7 copy.51
  374.2 0.8 convert_element_type.77
  375.1 0.8 copy.68
  (62 shorter events, 0.3 us)
Async XLA Ops:
  0.6 48.0 %copy-start = (bf16[1,256,1024]{2,1,0:T(8,128)(2,1)S(1)}, bf16[1,256,1024]{2,1,0:T(8,128)(2,1)}, u32[]{:S(2)}) copy-start(bf16[1,256,1024]{2,1,0:T(8,128)(2,1)} %param.14) | copy-start | bytes 1572868
  0.7 47.1 %copy-start.20 = (s32[1,3]{1,0:T(1,128)S(1)}, s32[1,3]{1,0:T(1,128)}, u32[]{:S(2)}) copy-start(s32[1,3]{1,0:T(1,128)} %param.16) | copy-start | bytes 40
  46.1 6.0 %copy-start.13 = (bf16[16,1024]{1,0:T(8,128)(2,1)S(1)}, bf16[16,1024]{1,0:T(8,128)(2,1)}, u32[]{:S(2)}) copy-start(bf16[16,1024]{1,0:T(8,128)(2,1)} %get-tuple-element.57) | copy-start | bytes 98308
  47.7 4.6 %copy-start.21 = (f32[8]{0:T(128)S(1)}, f32[8]{0:T(128)}, u32[]{:S(2)}) copy-start(f32[8]{0:T(128)} %param.20) | copy-start | bytes 100
  52.4 1.0 copy-start.2
  141.3 31.9 %collective-permute-start.1 = (bf16[256,1024]{1,0:T(8,128)(2,1)}, bf16[256,1024]{1,0:T(8,128)(2,1)S(1)}, u32[]{:S(2)}, u32[]{:S(2)}) collective-permute-start(bf16[256,1024]{1,0:T(8,128)(2,1)} %get-tuple-element.60.heads_ref), channel_id=1, source_target_pairs={{0,1},{1,0},{2,3},{3,2},{4,5},{5,4},{6,7},{7,6},{8,9},{9,8},{10,11... | collective-permute-start | bytes 1572872 | tf_op jit(solution)/shard_map/ppermute | solution.py:293
  141.8 33.4 %collective-permute-start = (bf16[272,1024]{1,0:T(8,128)(2,1)}, bf16[272,1024]{1,0:T(8,128)(2,1)S(1)}, u32[]{:S(2)}, u32[]{:S(2)}) collective-permute-start(bf16[272,1024]{1,0:T(8,128)(2,1)} %copy-done.2), channel_id=1, source_target_pairs={{0,1},{1,0},{2,3},{3,2},{4,5},{5,4},{6,7},{7,6},{8,9},{9,8},{10,11... | collective-permute-start | bytes 1671176 | tf_op jit(solution)/shard_map/ppermute | solution.py:293
  142.0 31.1 %copy-start.1 = (bf16[1,256,1024]{2,1,0:T(8,128)(2,1)S(1)}, bf16[1,256,1024]{2,1,0:T(8,128)(2,1)}, u32[]{:S(2)}) copy-start(bf16[1,256,1024]{2,1,0:T(8,128)(2,1)} %param.14) | copy-start | bytes 1572868
  173.1 1.0 copy-start.4
  173.2 1.9 copy-start.3
  176.2 126.5 %copy-start.5 = (f32[256,8]{1,0:T(8,128)S(1)}, f32[256,8]{1,0:T(8,128)}, u32[]{:S(2)}) copy-start(f32[256,8]{1,0:T(8,128)} %fusion.3.refs_8_.refs_13_) | copy-start | bytes 24580
  302.7 1.4 copy-start.7
  302.7 1.4 copy-start.17
  304.2 0.8 copy-start.16
  304.2 1.1 copy-start.19
  304.2 1.2 copy-start.18
  306.0 1.1 copy-start.11
  306.6 1.8 copy-start.10
  306.6 5.6 %collective-permute-start.2 = (f32[8,16,512]{2,1,0:T(8,128)S(1)}, f32[8,16,512]{2,1,0:T(8,128)S(1)}, u32[]{:S(2)}, u32[]{:S(2)}) collective-permute-start(f32[8,16,512]{2,1,0:T(8,128)S(1)} %bitcast.70), channel_id=1, source_target_pairs={{0,1},{1,0},{2,3},{3,2},{4,5},{5,4},{6,7},{7,6},{8,9},{9,8},{10,11... | collective-permute-start | bytes 786440 | tf_op jit(solution)/shard_map/ppermute | solution.py:293
  308.3 1.4 copy-start.9
  309.5 1.4 copy-start.6
  368.5 1.5 copy-start.15
  368.5 3.2 copy-start.8
  371.7 2.6 copy-start.14
  371.7 3.4 copy-start.12
